TPU v7x, 512 devices: a whole 4x8x8 slice. The times are simulated.
512 devices in a mesh: grp: 16 (over x, y_hi), dev: 32 (over z, y_lo, core).
Axes of the slice: x: 4, y: 8 (y_hi: 4, y_lo: 2; y = y_hi * 2 + y_lo), z: 8, core: 2. Of those that a mesh axis runs over, the one named last changes fastest.
Arguments:
- generated: float32 [8192, 1024], P(('grp', 'dev')), may hold values from -16 to 16
- data: float32 [8192, 1024], P(('grp', 'dev')), may hold values from -24 to 24
Outputs:
- force_rows: float32 [8192, 1024], P(('grp', 'dev'))
- energy: float32 [], replicated
All inputs are finite; a program needn't handle non-finite values.
Results may differ from a plain program's by a relative error of at most 0.0002.
Values sent between devices are 32-bit elements; how exact they have to be, the bound alone decides.
No kernel may reach another device: no remote copies, remote signals or barrier semaphores. Data moves between devices by JAX's collectives and lax.ppermute only.
A program may use at most 64 MiB of HBM per device.

v0:
```python
import jax
import jax.numpy as jnp
from jax import lax
from jax.sharding import PartitionSpec as P

HIGH = lax.Precision.HIGHEST


def shifted(value, axis, steps):
    count = lax.axis_size(axis)
    pairs = [(source, (source + steps) % count) for source in range(count)]
    return lax.ppermute(value, axis, pairs)


def distances(left, right):
    left_sq = jnp.sum(left * left, axis=1)
    right_sq = jnp.sum(right * right, axis=1)
    inner = lax.dot_general(
        left, right, (((1,), (1,)), ((), ())), precision=HIGH, preferred_element_type=jnp.float32
    )
    return jnp.sqrt(jnp.maximum(left_sq[:, None] + right_sq[None, :] - 2.0 * inner, 0.0) + 1.0)


def pair_terms(part_gen, part_data, gen_group, data_group, n_gen, n_data, root_width, with_columns):
    count = part_gen.shape[0]
    own_rows = jnp.concatenate([part_gen, part_data], axis=0)
    to_gen = distances(own_rows, gen_group)
    to_data = distances(own_rows, data_group)
    energy_part = -jnp.sum(to_gen[:count]) / (n_gen * n_gen) + jnp.sum(to_data[:count]) / (
        n_gen * n_data
    )
    energy_part = (
        energy_part
        + jnp.sum(to_gen[count:]) / (n_gen * n_data)
        - jnp.sum(to_data[count:]) / (n_data * n_data)
    )
    weight_gen = -root_width / n_gen / to_gen[:count]
    weight_data = root_width / n_data / to_data[:count]
    totals = jnp.sum(weight_gen, axis=1) + jnp.sum(weight_data, axis=1)
    row_force = totals[:, None] * part_gen
    row_force = row_force - jnp.dot(
        weight_gen, gen_group, precision=HIGH, preferred_element_type=jnp.float32
    )
    row_force = row_force - jnp.dot(
        weight_data, data_group, precision=HIGH, preferred_element_type=jnp.float32
    )
    if not with_columns:
        return (energy_part, row_force)
    row_coef = jnp.where(
        jnp.arange(own_rows.shape[0]) < count, -root_width / n_gen, root_width / n_data
    ).astype(jnp.float32)
    weight_cols = row_coef[:, None] / to_gen
    col_force = jnp.sum(weight_cols, axis=0)[:, None] * gen_group
    col_force = col_force - lax.dot_general(
        weight_cols,
        own_rows,
        (((0,), (0,)), ((), ())),
        precision=HIGH,
        preferred_element_type=jnp.float32,
    )
    return (energy_part, row_force, col_force)


def body(generated, data):
    groups = lax.axis_size("grp")
    members = lax.axis_size("dev")
    n_gen = generated.shape[0] * groups * members
    n_data = data.shape[0] * groups * members
    root_width = float(generated.shape[1]) ** 0.5
    gen_group, data_group = (
        lax.all_gather(generated, "dev", axis=0, tiled=True),
        lax.all_gather(data, "dev", axis=0, tiled=True),
    )
    energy_sum, force_rows = pair_terms(
        generated, data, gen_group, data_group, n_gen, n_data, root_width, False
    )
    half_loop = groups // 2
    column_total = jnp.zeros(gen_group.shape, jnp.float32)
    for distance in range(1, half_loop + 1):
        portion = 1.0 if 2 * distance < groups else 0.5
        partner_gen, partner_data = shifted((generated, data), "grp", distance)
        energy_part, row_force, col_force = pair_terms(
            partner_gen, partner_data, gen_group, data_group, n_gen, n_data, root_width, True
        )
        energy_sum = energy_sum + 2.0 * portion * energy_part
        column_total = column_total + portion * col_force
        force_rows = force_rows + shifted(portion * row_force, "grp", -distance)
    force_rows = force_rows + lax.psum_scatter(column_total, "dev", scatter_dimension=0, tiled=True)
    energy = lax.psum(energy_sum, ("grp", "dev")) / root_width
    return (force_rows, energy)


def solution(mesh):
    placed = (P(("grp", "dev"), None), P(("grp", "dev"), None))
    return jax.shard_map(
        body, mesh=mesh, in_specs=placed, out_specs=(P(("grp", "dev"), None), P()), check_vma=False
    )
```

profile of v0, /device:TPU:1, one launch (start us, length us, event | category | flops | bytes accessed | tf_op | source)
XLA Modules:
  0.0 423.8 jit_solution(15588864787015770488)
XLA Ops:
  8.7 9.2 %collective-permute-start.16 = (f32[16,1024]{1,0:T(8,128)}, f32[16,1024]{1,0:T(8,128)S(1)}, u32[]{:S(2)}, u32[]{:S(2)}) collective-permute-start(f32[16,1024]{1,0:T(8,128)} %param.3), channel_id=1, source_target_pairs={{0,192},{32,224},{64,256},{96,288},{128,320},{160,352},{192,384},{... | collective-permute-start | bytes 196616 | tf_op jit(solution)/shard_map/ppermute | solution.py:12
  17.9 3.3 collective-permute-start.13
  21.3 2.8 collective-permute-start.10
  24.1 5.3 %collective-permute-start.7 = (f32[16,1024]{1,0:T(8,128)}, f32[16,1024]{1,0:T(8,128)S(1)}, u32[]{:S(2)}, u32[]{:S(2)}) collective-permute-start(f32[16,1024]{1,0:T(8,128)} %param.3), channel_id=1, source_target_pairs={{0,96},{32,128},{64,160},{96,192},{128,224},{160,256},{192,288},{2... | collective-permute-start | bytes 196616 | tf_op jit(solution)/shard_map/ppermute | solution.py:12
  29.4 2.8 collective-permute-start.18
  34.1 4.2 collective-permute-done.18
  38.3 4.0 collective-permute-start.21
  42.3 2.7 collective-permute-done.21
  45.0 2.3 collective-permute-start
  47.3 7.2 %collective-permute-done = f32[16,1024]{1,0:T(8,128)S(1)} collective-permute-done((f32[16,1024]{1,0:T(8,128)}, f32[16,1024]{1,0:T(8,128)S(1)}, u32[]{:S(2)}, u32[]{:S(2)}) %collective-permute-start) | collective-permute-done | bytes 65568 | tf_op jit(solution)/shard_map/ppermute | solution.py:12
  56.5 9.5 %collective-permute-done.3 = f32[16,1024]{1,0:T(8,128)S(1)} collective-permute-done((f32[16,1024]{1,0:T(8,128)}, f32[16,1024]{1,0:T(8,128)S(1)}, u32[]{:S(2)}, u32[]{:S(2)}) %collective-permute-start.3) | collective-permute-done | bytes 65568 | tf_op jit(solution)/shard_map/ppermute | solution.py:12
  67.9 6.4 %collective-permute-done.6 = f32[16,1024]{1,0:T(8,128)S(1)} collective-permute-done((f32[16,1024]{1,0:T(8,128)}, f32[16,1024]{1,0:T(8,128)S(1)}, u32[]{:S(2)}, u32[]{:S(2)}) %collective-permute-start.6) | collective-permute-done | bytes 65568 | tf_op jit(solution)/shard_map/ppermute | solution.py:12
  76.2 4.8 %collective-permute-done.9 = f32[16,1024]{1,0:T(8,128)S(1)} collective-permute-done((f32[16,1024]{1,0:T(8,128)}, f32[16,1024]{1,0:T(8,128)S(1)}, u32[]{:S(2)}, u32[]{:S(2)}) %collective-permute-start.9) | collective-permute-done | bytes 65568 | tf_op jit(solution)/shard_map/ppermute | solution.py:12
  82.9 7.8 %collective-permute-done.12 = f32[16,1024]{1,0:T(8,128)S(1)} collective-permute-done((f32[16,1024]{1,0:T(8,128)}, f32[16,1024]{1,0:T(8,128)S(1)}, u32[]{:S(2)}, u32[]{:S(2)}) %collective-permute-start.12) | collective-permute-done | bytes 65568 | tf_op jit(solution)/shard_map/ppermute | solution.py:12
  92.7 9.6 %collective-permute-done.15 = f32[16,1024]{1,0:T(8,128)S(1)} collective-permute-done((f32[16,1024]{1,0:T(8,128)}, f32[16,1024]{1,0:T(8,128)S(1)}, u32[]{:S(2)}, u32[]{:S(2)}) %collective-permute-start.15) | collective-permute-done | bytes 65568 | tf_op jit(solution)/shard_map/ppermute | solution.py:12
  104.2 6.6 %collective-permute-done.19 = f32[16,1024]{1,0:T(8,128)S(1)} collective-permute-done((f32[16,1024]{1,0:T(8,128)}, f32[16,1024]{1,0:T(8,128)S(1)}, u32[]{:S(2)}, u32[]{:S(2)}) %collective-permute-start.19) | collective-permute-done | bytes 65568 | tf_op jit(solution)/shard_map/ppermute | solution.py:12
  112.7 4.8 %collective-permute-done.22 = f32[16,1024]{1,0:T(8,128)S(1)} collective-permute-done((f32[16,1024]{1,0:T(8,128)}, f32[16,1024]{1,0:T(8,128)S(1)}, u32[]{:S(2)}, u32[]{:S(2)}) %collective-permute-start.22) | collective-permute-done | bytes 65568 | tf_op jit(solution)/shard_map/ppermute | solution.py:12
  119.4 7.8 %collective-permute-done.1 = f32[16,1024]{1,0:T(8,128)S(1)} collective-permute-done((f32[16,1024]{1,0:T(8,128)}, f32[16,1024]{1,0:T(8,128)S(1)}, u32[]{:S(2)}, u32[]{:S(2)}) %collective-permute-start.1) | collective-permute-done | bytes 65568 | tf_op jit(solution)/shard_map/ppermute | solution.py:12
  129.2 9.9 %collective-permute-done.4 = f32[16,1024]{1,0:T(8,128)S(1)} collective-permute-done((f32[16,1024]{1,0:T(8,128)}, f32[16,1024]{1,0:T(8,128)S(1)}, u32[]{:S(2)}, u32[]{:S(2)}) %collective-permute-start.4) | collective-permute-done | bytes 65568 | tf_op jit(solution)/shard_map/ppermute | solution.py:12
  146.4 6.8 %all-gather.5.cloned.1.call-done = f32[512,1024]{1,0:T(8,128)} async-done(((f32[16,1024]{1,0:T(8,128)}), f32[512,1024]{1,0:T(8,128)}) %all-gather.5.cloned.1.call-update) | async-done | bytes 2097168 | tf_op jit(solution)/shard_map/all_gather | solution.py:72
  155.2 2.7 add_sqrt_fusion.3
  163.5 6.8 %collective-permute-start.20 = (f32[16,1024]{1,0:T(8,128)}, f32[16,1024]{1,0:T(8,128)}, u32[]{:S(2)}, u32[]{:S(2)}) collective-permute-start(f32[16,1024]{1,0:T(8,128)} %subtract_subtract_fusion), channel_id=1, source_target_pairs={{0,288},{32,320},{64,352},{96,384},{128,416},{160,448},{192,480},{... | collective-permute-start | bytes 196616 | tf_op jit(solution)/shard_map/ppermute | solution.py:12
  178.0 2.2 collective-permute-start.23
  191.7 7.3 %collective-permute-start.5 = (f32[16,1024]{1,0:T(8,128)}, f32[16,1024]{1,0:T(8,128)}, u32[]{:S(2)}, u32[]{:S(2)}) collective-permute-start(f32[16,1024]{1,0:T(8,128)} %subtract_subtract_fusion.5), channel_id=1, source_target_pairs={{0,448},{32,480},{64,0},{96,32},{128,64},{160,96},{192,128},{224,1... | collective-permute-start | bytes 196616 | tf_op jit(solution)/shard_map/ppermute | solution.py:12
  208.6 3.0 collective-permute-start.8
  220.6 2.2 collective-permute-start.11
  234.8 5.2 %multiply_add_fusion = f32[512,1024]{1,0:T(8,128)} fusion(f32[512,1024]{1,0:T(8,128)S(1)} %copy-done, f32[512,1024]{1,0:T(8,128)S(1)} %fusion.54, f32[512,1024]{1,0:T(8,128)S(1)} %fusion.52, f32[512,1024]{1,0:T(8,128)S(1)} %fusion.50, f32[512,1024]{1,0:T(8,128)S(1)} %fusion.48, f32[512,1024]{1,0:T(8,128)S(1)} %fusion.46, f32[512,1024]{1,0:T(8,128)S(1)} %fusion.44, ...), kind=kOutput, calls=%fused_computation | convolution fusion | flops 213925888 | bytes 19087488 | tf_op jit(solution)/shard_map/dot_general | solution.py:54
  240.0 3.7 add_sqrt_fusion.6
  286.7 5.3 %collective-permute-start.14 = (f32[16,1024]{1,0:T(8,128)S(1)}, f32[16,1024]{1,0:T(8,128)S(1)}, u32[]{:S(2)}, u32[]{:S(2)}) collective-permute-start(f32[16,1024]{1,0:T(8,128)S(1)} %subtract_subtract_fusion.2), channel_id=1, source_target_pairs={{0,352},{32,384},{64,416},{96,448},{128,480},{160,0},{192,32},{224... | collective-permute-start | bytes 196616 | tf_op jit(solution)/shard_map/ppermute | solution.py:12
  292.0 6.6 %collective-permute-start.17 = (f32[16,1024]{1,0:T(8,128)S(1)}, f32[16,1024]{1,0:T(8,128)S(1)}, u32[]{:S(2)}, u32[]{:S(2)}) collective-permute-start(f32[16,1024]{1,0:T(8,128)S(1)} %subtract_subtract_fusion.1), channel_id=1, source_target_pairs={{0,320},{32,352},{64,384},{96,416},{128,448},{160,480},{192,0},{22... | collective-permute-start | bytes 196616 | tf_op jit(solution)/shard_map/ppermute | solution.py:12
  300.7 2.7 convolution_subtract_fusion
  303.4 109.9 %psum.7 = f32[]{:T(128)} all-reduce(f32[]{:T(128)S(6)} %add.546), channel_id=1, replica_groups=mesh['grp'=16,'dev'=32] {'grp','dev'}, use_global_device_ids=true, to_apply=%region_74.75 | all-reduce | flops 1 | bytes 8 | tf_op jit(solution)/shard_map/psum | solution.py:89
  (163 shorter events, 109.1 us)
Async XLA Ops:
  7.2 137.3 %all-gather.3.cloned.1.call-start = ((), (), s32[]{:S(2)}) async-start(), calls=%async_computation.1 | async-start | bytes 2162688 | tf_op jit(solution)/shard_map/all_gather | solution.py:71
  7.9 145.3 %all-gather.5.cloned.1.call-start = ((), (), s32[]{:S(2)}) async-start(), calls=%async_computation.2 | async-start | bytes 2162688 | tf_op jit(solution)/shard_map/all_gather | solution.py:72
  8.6 405.4 %reduce-scatter.2.cloned.1.call-start = ((), (), s32[]{:S(2)}) async-start(), calls=%async_computation.3 | async-start | bytes 2162688 | tf_op jit(solution)/shard_map/reduce_scatter | solution.py:88
  8.7 130.4 %collective-permute-start.16 = (f32[16,1024]{1,0:T(8,128)}, f32[16,1024]{1,0:T(8,128)S(1)}, u32[]{:S(2)}, u32[]{:S(2)}) collective-permute-start(f32[16,1024]{1,0:T(8,128)} %param.3), channel_id=1, source_target_pairs={{0,192},{32,224},{64,256},{96,288},{128,320},{160,352},{192,384},{... | collective-permute-start | bytes 196616 | tf_op jit(solution)/shard_map/ppermute | solution.py:12
  17.9 121.2 %collective-permute-start.13 = (f32[16,1024]{1,0:T(8,128)}, f32[16,1024]{1,0:T(8,128)S(1)}, u32[]{:S(2)}, u32[]{:S(2)}) collective-permute-start(f32[16,1024]{1,0:T(8,128)} %param.3), channel_id=1, source_target_pairs={{0,160},{32,192},{64,224},{96,256},{128,288},{160,320},{192,352},{... | collective-permute-start | bytes 196616 | tf_op jit(solution)/shard_map/ppermute | solution.py:12
  21.3 117.8 %collective-permute-start.10 = (f32[16,1024]{1,0:T(8,128)}, f32[16,1024]{1,0:T(8,128)S(1)}, u32[]{:S(2)}, u32[]{:S(2)}) collective-permute-start(f32[16,1024]{1,0:T(8,128)} %param.3), channel_id=1, source_target_pairs={{0,128},{32,160},{64,192},{96,224},{128,256},{160,288},{192,320},{... | collective-permute-start | bytes 196616 | tf_op jit(solution)/shard_map/ppermute | solution.py:12
  24.1 115.0 %collective-permute-start.7 = (f32[16,1024]{1,0:T(8,128)}, f32[16,1024]{1,0:T(8,128)S(1)}, u32[]{:S(2)}, u32[]{:S(2)}) collective-permute-start(f32[16,1024]{1,0:T(8,128)} %param.3), channel_id=1, source_target_pairs={{0,96},{32,128},{64,160},{96,192},{128,224},{160,256},{192,288},{2... | collective-permute-start | bytes 196616 | tf_op jit(solution)/shard_map/ppermute | solution.py:12
  29.4 8.8 %collective-permute-start.18 = (f32[16,1024]{1,0:T(8,128)}, f32[16,1024]{1,0:T(8,128)S(1)}, u32[]{:S(2)}, u32[]{:S(2)}) collective-permute-start(f32[16,1024]{1,0:T(8,128)} %param.2), channel_id=1, source_target_pairs={{0,224},{32,256},{64,288},{96,320},{128,352},{160,384},{192,416},{... | collective-permute-start | bytes 196616 | tf_op jit(solution)/shard_map/ppermute | solution.py:12
  38.3 16.3 %copy-start.10 = (f32[16,1024]{1,0:T(8,128)}, f32[16,1024]{1,0:T(8,128)S(1)}, u32[]{:S(2)}) copy-start(f32[16,1024]{1,0:T(8,128)S(1)} %collective-permute-done.18) | copy-start | bytes 196612
  38.3 6.7 %collective-permute-start.21 = (f32[16,1024]{1,0:T(8,128)}, f32[16,1024]{1,0:T(8,128)S(1)}, u32[]{:S(2)}, u32[]{:S(2)}) collective-permute-start(f32[16,1024]{1,0:T(8,128)} %param.2), channel_id=1, source_target_pairs={{0,256},{32,288},{64,320},{96,352},{128,384},{160,416},{192,448},{... | collective-permute-start | bytes 196616 | tf_op jit(solution)/shard_map/ppermute | solution.py:12
  45.0 9.5 %copy-start.8 = (f32[16,1024]{1,0:T(8,128)}, f32[16,1024]{1,0:T(8,128)S(1)}, u32[]{:S(2)}) copy-start(f32[16,1024]{1,0:T(8,128)S(1)} %collective-permute-done.21) | copy-start | bytes 196612
  45.0 9.5 %collective-permute-start = (f32[16,1024]{1,0:T(8,128)}, f32[16,1024]{1,0:T(8,128)S(1)}, u32[]{:S(2)}, u32[]{:S(2)}) collective-permute-start(f32[16,1024]{1,0:T(8,128)} %param.2), channel_id=1, source_target_pairs={{0,32},{32,64},{64,96},{96,128},{128,160},{160,192},{192,224},{224... | collective-permute-start | bytes 196616 | tf_op jit(solution)/shard_map/ppermute | solution.py:12
  54.5 11.4 %collective-permute-start.3 = (f32[16,1024]{1,0:T(8,128)}, f32[16,1024]{1,0:T(8,128)S(1)}, u32[]{:S(2)}, u32[]{:S(2)}) collective-permute-start(f32[16,1024]{1,0:T(8,128)} %param.2), channel_id=1, source_target_pairs={{0,64},{32,96},{64,128},{96,160},{128,192},{160,224},{192,256},{22... | collective-permute-start | bytes 196616 | tf_op jit(solution)/shard_map/ppermute | solution.py:12
  65.9 8.3 %collective-permute-start.6 = (f32[16,1024]{1,0:T(8,128)}, f32[16,1024]{1,0:T(8,128)S(1)}, u32[]{:S(2)}, u32[]{:S(2)}) collective-permute-start(f32[16,1024]{1,0:T(8,128)} %param.2), channel_id=1, source_target_pairs={{0,96},{32,128},{64,160},{96,192},{128,224},{160,256},{192,288},{2... | collective-permute-start | bytes 196616 | tf_op jit(solution)/shard_map/ppermute | solution.py:12
  74.2 6.8 %collective-permute-start.9 = (f32[16,1024]{1,0:T(8,128)}, f32[16,1024]{1,0:T(8,128)S(1)}, u32[]{:S(2)}, u32[]{:S(2)}) collective-permute-start(f32[16,1024]{1,0:T(8,128)} %param.2), channel_id=1, source_target_pairs={{0,128},{32,160},{64,192},{96,224},{128,256},{160,288},{192,320},{... | collective-permute-start | bytes 196616 | tf_op jit(solution)/shard_map/ppermute | solution.py:12
  81.0 9.8 %collective-permute-start.12 = (f32[16,1024]{1,0:T(8,128)}, f32[16,1024]{1,0:T(8,128)S(1)}, u32[]{:S(2)}, u32[]{:S(2)}) collective-permute-start(f32[16,1024]{1,0:T(8,128)} %param.2), channel_id=1, source_target_pairs={{0,160},{32,192},{64,224},{96,256},{128,288},{160,320},{192,352},{... | collective-permute-start | bytes 196616 | tf_op jit(solution)/shard_map/ppermute | solution.py:12
  90.8 11.5 %collective-permute-start.15 = (f32[16,1024]{1,0:T(8,128)}, f32[16,1024]{1,0:T(8,128)S(1)}, u32[]{:S(2)}, u32[]{:S(2)}) collective-permute-start(f32[16,1024]{1,0:T(8,128)} %param.2), channel_id=1, source_target_pairs={{0,192},{32,224},{64,256},{96,288},{128,320},{160,352},{192,384},{... | collective-permute-start | bytes 196616 | tf_op jit(solution)/shard_map/ppermute | solution.py:12
  102.3 8.5 %collective-permute-start.19 = (f32[16,1024]{1,0:T(8,128)}, f32[16,1024]{1,0:T(8,128)S(1)}, u32[]{:S(2)}, u32[]{:S(2)}) collective-permute-start(f32[16,1024]{1,0:T(8,128)} %param.3), channel_id=1, source_target_pairs={{0,224},{32,256},{64,288},{96,320},{128,352},{160,384},{192,416},{... | collective-permute-start | bytes 196616 | tf_op jit(solution)/shard_map/ppermute | solution.py:12
  110.8 6.7 %collective-permute-start.22 = (f32[16,1024]{1,0:T(8,128)}, f32[16,1024]{1,0:T(8,128)S(1)}, u32[]{:S(2)}, u32[]{:S(2)}) collective-permute-start(f32[16,1024]{1,0:T(8,128)} %param.3), channel_id=1, source_target_pairs={{0,256},{32,288},{64,320},{96,352},{128,384},{160,416},{192,448},{... | collective-permute-start | bytes 196616 | tf_op jit(solution)/shard_map/ppermute | solution.py:12
  117.5 9.7 %collective-permute-start.1 = (f32[16,1024]{1,0:T(8,128)}, f32[16,1024]{1,0:T(8,128)S(1)}, u32[]{:S(2)}, u32[]{:S(2)}) collective-permute-start(f32[16,1024]{1,0:T(8,128)} %param.3), channel_id=1, source_target_pairs={{0,32},{32,64},{64,96},{96,128},{128,160},{160,192},{192,224},{224... | collective-permute-start | bytes 196616 | tf_op jit(solution)/shard_map/ppermute | solution.py:12
  127.3 11.8 %collective-permute-start.4 = (f32[16,1024]{1,0:T(8,128)}, f32[16,1024]{1,0:T(8,128)S(1)}, u32[]{:S(2)}, u32[]{:S(2)}) collective-permute-start(f32[16,1024]{1,0:T(8,128)} %param.3), channel_id=1, source_target_pairs={{0,64},{32,96},{64,128},{96,160},{128,192},{160,224},{192,256},{22... | collective-permute-start | bytes 196616 | tf_op jit(solution)/shard_map/ppermute | solution.py:12
  144.5 10.7 %copy-start = (f32[512,1024]{1,0:T(8,128)S(1)}, f32[512,1024]{1,0:T(8,128)}, u32[]{:S(2)}) copy-start(f32[512,1024]{1,0:T(8,128)} %all-gather.3.cloned.1.call-done) | copy-start | bytes 6291460
  160.7 9.6 %copy-start.19 = (f32[32]{0:T(128)S(1)}, f32[32]{0:T(128)}, u32[]{:S(2)}) copy-start(f32[32]{0:T(128)} %multiply_reduce_fusion.2) | copy-start | bytes 388
  163.5 123.2 %collective-permute-start.20 = (f32[16,1024]{1,0:T(8,128)}, f32[16,1024]{1,0:T(8,128)}, u32[]{:S(2)}, u32[]{:S(2)}) collective-permute-start(f32[16,1024]{1,0:T(8,128)} %subtract_subtract_fusion), channel_id=1, source_target_pairs={{0,288},{32,320},{64,352},{96,384},{128,416},{160,448},{192,480},{... | collective-permute-start | bytes 196616 | tf_op jit(solution)/shard_map/ppermute | solution.py:12
  178.0 114.0 %collective-permute-start.23 = (f32[16,1024]{1,0:T(8,128)}, f32[16,1024]{1,0:T(8,128)}, u32[]{:S(2)}, u32[]{:S(2)}) collective-permute-start(f32[16,1024]{1,0:T(8,128)} %subtract_multiply_fusion), channel_id=1, source_target_pairs={{0,256},{32,288},{64,320},{96,352},{128,384},{160,416},{192,448},{... | collective-permute-start | bytes 196616 | tf_op jit(solution)/shard_map/ppermute | solution.py:12
  188.9 10.1 %copy-start.17 = (f32[32]{0:T(128)S(1)}, f32[32]{0:T(128)}, u32[]{:S(2)}) copy-start(f32[32]{0:T(128)} %multiply_reduce_fusion.7) | copy-start | bytes 388
  191.7 106.9 %collective-permute-start.5 = (f32[16,1024]{1,0:T(8,128)}, f32[16,1024]{1,0:T(8,128)}, u32[]{:S(2)}, u32[]{:S(2)}) collective-permute-start(f32[16,1024]{1,0:T(8,128)} %subtract_subtract_fusion.5), channel_id=1, source_target_pairs={{0,448},{32,480},{64,0},{96,32},{128,64},{160,96},{192,128},{224,1... | collective-permute-start | bytes 196616 | tf_op jit(solution)/shard_map/ppermute | solution.py:12
  208.6 205.3 %collective-permute-start.8 = (f32[16,1024]{1,0:T(8,128)}, f32[16,1024]{1,0:T(8,128)}, u32[]{:S(2)}, u32[]{:S(2)}) collective-permute-start(f32[16,1024]{1,0:T(8,128)} %subtract_subtract_fusion.4), channel_id=1, source_target_pairs={{0,416},{32,448},{64,480},{96,0},{128,32},{160,64},{192,96},{224,1... | collective-permute-start | bytes 196616 | tf_op jit(solution)/shard_map/ppermute | solution.py:12
  220.6 193.4 %collective-permute-start.11 = (f32[16,1024]{1,0:T(8,128)S(1)}, f32[16,1024]{1,0:T(8,128)S(1)}, u32[]{:S(2)}, u32[]{:S(2)}) collective-permute-start(f32[16,1024]{1,0:T(8,128)S(1)} %subtract_subtract_fusion.3), channel_id=1, source_target_pairs={{0,384},{32,416},{64,448},{96,480},{128,0},{160,32},{192,64},{224,... | collective-permute-start | bytes 196616 | tf_op jit(solution)/shard_map/ppermute | solution.py:12
  286.7 127.3 %collective-permute-start.14 = (f32[16,1024]{1,0:T(8,128)S(1)}, f32[16,1024]{1,0:T(8,128)S(1)}, u32[]{:S(2)}, u32[]{:S(2)}) collective-permute-start(f32[16,1024]{1,0:T(8,128)S(1)} %subtract_subtract_fusion.2), channel_id=1, source_target_pairs={{0,352},{32,384},{64,416},{96,448},{128,480},{160,0},{192,32},{224... | collective-permute-start | bytes 196616 | tf_op jit(solution)/shard_map/ppermute | solution.py:12
  292.0 122.0 %collective-permute-start.17 = (f32[16,1024]{1,0:T(8,128)S(1)}, f32[16,1024]{1,0:T(8,128)S(1)}, u32[]{:S(2)}, u32[]{:S(2)}) collective-permute-start(f32[16,1024]{1,0:T(8,128)S(1)} %subtract_subtract_fusion.1), channel_id=1, source_target_pairs={{0,320},{32,352},{64,384},{96,416},{128,448},{160,480},{192,0},{22... | collective-permute-start | bytes 196616 | tf_op jit(solution)/shard_map/ppermute | solution.py:12
  298.6 115.4 %collective-permute-start.2 = (f32[16,1024]{1,0:T(8,128)S(1)}, f32[16,1024]{1,0:T(8,128)S(1)}, u32[]{:S(2)}, u32[]{:S(2)}) collective-permute-start(f32[16,1024]{1,0:T(8,128)S(1)} %subtract_subtract_fusion.6), channel_id=1, source_target_pairs={{0,480},{32,0},{64,32},{96,64},{128,96},{160,128},{192,160},{224,1... | collective-permute-start | bytes 196616 | tf_op jit(solution)/shard_map/ppermute | solution.py:12
  (16 other events, 72.7 us)
Sparse Core Ops, SparseCore 0:
  10.1 73.7 all-gather.2
  86.0 67.1 all-gather.4
  240.2 128.9 reduce-scatter.1
where the time goes:
time: 431 us; the launch traced here: 424 us
  blocking collectives  110 us (26%)
  waiting for transfers between devices  89.4 us (21%)
  starting transfers between devices  82.5 us (19%)
  matrix products  81.9 us (19%)
  between operations  39.3 us (9%)
  other arithmetic  18.8 us (4%)
    psum x1, blocking collectives, body(): energy = lax.psum(energy_sum, ('grp', 'dev')) / root_width  110 us
    ppermute x24, starting transfers between devices, shifted(): return lax.ppermute(value, axis, pairs)  82.4 us
    ppermute x24, waiting for transfers between devices, shifted(): return lax.ppermute(value, axis, pairs)  81.3 us
    dot_general x18, matrix products, distances(): lax.dot_general(left, right, (((1,), (1,)), ((), ())), precision=HIGH, pr...  39.1 us
    dot_general x8, matrix products, pair_terms(): lax.dot_general(weight_cols, own_rows, (((0,), (0,)), ((), ())), precisio...  18.6 us
    dot_general x9, matrix products, pair_terms(): jnp.dot(weight_gen, gen_group, precision=HIGH, preferred_element_type=jnp...  12.7 us
    dot_general x9, matrix products, pair_terms(): jnp.dot(weight_data, data_group, precision=HIGH, preferred_element_type=j...  11.5 us
  transfers between devices with their start and end apart: 27, of which 13 were waited for; matrix products, arithmetic and copies ran while one was open for 21% of the time, Pallas kernels for 0%

commit v1 on v0

v1 whole, which is shorter than its diff:
```python
import jax
import jax.numpy as jnp
from jax import lax
from jax.experimental import pallas as pl
from jax.experimental.pallas import tpu as pltpu
from jax.sharding import Mesh, PartitionSpec as P

AXES = ("x", "yh", "z", "yl", "c")
SIZES = (4, 4, 8, 2, 2)
ROOT_WIDTH = 32.0
COUNT = 8192.0
NT = (((1,), (1,)), ((), ()))
NN = (((1,), (0,)), ((), ()))


def halves(value):
    high = value.astype(jnp.bfloat16)
    low = (value - high.astype(jnp.float32)).astype(jnp.bfloat16)
    return high, low


def product(left, right, dims):
    def dot(a, b):
        return lax.dot_general(a, b, dims, preferred_element_type=jnp.float32)

    return dot(left[0], right[0]) + (dot(left[0], right[1]) + dot(left[1], right[0]))


def flat(block):
    return block.reshape(block.shape[0] * block.shape[1], block.shape[2])


def pair_kernel(rows_ref, cols_ref, force_ref, energy_ref):
    own = rows_ref.shape[1] // 2
    row_gen = flat(rows_ref[:, :own, :])
    row_data = flat(rows_ref[:, own:, :])
    count = row_gen.shape[0]
    rows = jnp.concatenate([row_gen, row_data], axis=0)
    rows_sq = jnp.sum(rows * rows, axis=1, keepdims=True)
    rows_hl = halves(rows)
    chunk = 16
    total = jnp.zeros((count, 1), jnp.float32)
    force = jnp.zeros(row_gen.shape, jnp.float32)
    energy = jnp.zeros((1, chunk * own), jnp.float32)
    for kind in range(2):
        for start in range(0, cols_ref.shape[0], chunk):
            cols = flat(cols_ref[start : start + chunk, kind * own : (kind + 1) * own, :])
            cols_sq = jnp.sum(cols * cols, axis=1, keepdims=True)
            cols_sq = jnp.transpose(jnp.broadcast_to(cols_sq, (cols.shape[0], 128)))[0:1, :]
            cols_hl = halves(cols)
            used = count if kind == 0 else 2 * count
            inner = product((rows_hl[0][:used], rows_hl[1][:used]), cols_hl, NT)
            square = jnp.maximum(rows_sq[:used] + cols_sq - 2.0 * inner, 0.0) + 1.0
            inverse = lax.rsqrt(square)
            distance = square * inverse
            near = jnp.sum(distance[:count], axis=0, keepdims=True)
            if kind == 0:
                energy = energy - near
            else:
                energy = energy + 2.0 * near
                energy = energy - jnp.sum(distance[count:], axis=0, keepdims=True)
            coef = (-1.0 if kind == 0 else 1.0) * ROOT_WIDTH / COUNT
            weight = coef * inverse[:count]
            total = total + jnp.sum(weight, axis=1, keepdims=True)
            force = force + product(halves(weight), cols_hl, NN)
    force_ref[...] = total * row_gen - force
    energy_ref[...] = jnp.broadcast_to(
        jnp.sum(energy, axis=1, keepdims=True) / (COUNT * COUNT * ROOT_WIDTH), energy_ref.shape
    )


def pairs(rows, cols):
    count = rows.shape[0] * rows.shape[1] // 2
    width = rows.shape[2]
    return pl.pallas_call(
        pair_kernel,
        out_shape=(
            jax.ShapeDtypeStruct((count, width), jnp.float32),
            jax.ShapeDtypeStruct((8, 128), jnp.float32),
        ),
        in_specs=[pl.BlockSpec(memory_space=pltpu.VMEM)] * 2,
        out_specs=[pl.BlockSpec(memory_space=pltpu.VMEM)] * 2,
        compiler_params=pltpu.CompilerParams(vmem_limit_bytes=48 * 1024 * 1024),
        cost_estimate=pl.CostEstimate(flops=4_000_000_000, bytes_accessed=8_000_000, transcendentals=400_000),
    )(rows, cols)


def exchanged(value, axes):
    return lax.all_to_all(value, axes, split_axis=0, concat_axis=0, tiled=True)


def body(generated, data):
    own = jnp.concatenate([generated, data], axis=0)
    cols = lax.all_gather(own, ("x", "z"), axis=0, tiled=False)
    line = exchanged(jnp.broadcast_to(own[None], (8,) + own.shape), ("yh", "yl"))
    other = lax.ppermute(line, "c", [(0, 1), (1, 0)])
    core = lax.axis_index("c")
    first = jnp.where(core == 0, line, other)
    second = jnp.where(core == 0, other, line)
    rows = jnp.stack([first, second], axis=1).reshape(16, 32, 1024)
    force, energy = pairs(rows, cols)
    force = exchanged(force.reshape(16, 16, 1024), ("yh", "yl", "c"))
    force_rows = jnp.sum(force, axis=0)
    energy = jnp.sum(exchanged(jnp.broadcast_to(energy[None, :1], (16, 1, 128)), ("yh", "yl", "c")), axis=0)
    energy = jnp.sum(exchanged(jnp.broadcast_to(energy[None], (32, 1, 128)), ("x", "z")), axis=0)
    return (force_rows, energy[0, 0])


def solution(mesh):
    fine = Mesh(mesh.devices.reshape(SIZES), AXES)
    placed = P(AXES, None)
    return jax.shard_map(body, mesh=fine, in_specs=(placed, placed), out_specs=(placed, P()), check_vma=False)
```

time: 431 us -> 183 us (0.42); the launches traced: 424 us -> 182 us
  matrix products: 81.9 us -> 0 us
  starting transfers between devices: 82.5 us -> 11.2 us
  blocking collectives: 110 us -> 64.3 us
  between operations: 39.3 us -> 14.1 us
  other arithmetic: 18.8 us -> 1.7 us
  waiting for transfers between devices: 89.4 us -> 79.1 us
  Pallas kernels: 0 us -> 8.47 us
    psum x1 -> x0, blocking collectives: 110 us -> none  [body(): energy = lax.psum(energy_sum, ('grp', 'dev')) / root_width]
    dot_general x44 -> x0, matrix products: 81.9 us -> none  [the longest x18 39.1 us: distances(): lax.dot_general(left, right, (((1,), (1,)), ((), ())), precision=HIGH, pr...]
    ppermute x24 -> x1, waiting for transfers between devices: 81.3 us -> 2.26 us  [body(): other = lax.ppermute(line, 'c', [(0, 1), (1, 0)])]
    ppermute x24 -> x1, starting transfers between devices: 82.4 us -> 5.62 us  [body(): other = lax.ppermute(line, 'c', [(0, 1), (1, 0)])]
    all_to_all x0 -> x3, blocking collectives: none -> 64.3 us  [exchanged(): return lax.all_to_all(value, axes, split_axis=0, concat_axis=0, tiled=True)]
    all_gather x2 -> x1, waiting for transfers between devices: 6.76 us -> 49.4 us  [body(): cols = lax.all_gather(own, ('x', 'z'), axis=0, tiled=False)]
    all_to_all x0 -> x1, waiting for transfers between devices: none -> 27.4 us  [exchanged(): return lax.all_to_all(value, axes, split_axis=0, concat_axis=0, tiled=True)]
    reduce_sum x22 -> x3, other arithmetic: 17.1 us -> 1.23 us  [the longest x1 0.69 us: body(): force_rows = jnp.sum(force, axis=0)]
  transfers between devices with their start and end apart: 27 -> 3, of which waited for: 13 -> 3; matrix products, arithmetic and copies ran while one was open for 21% -> 1% of each run, Pallas kernels for 0% -> 0%
where the time goes in v1:
time: 183 us; the launch traced here: 182 us
  waiting for transfers between devices  79.1 us (43%)
  blocking collectives  64.3 us (35%)
  between operations  14.1 us (8%)
  starting transfers between devices  11.2 us (6%)
  Pallas kernels  8.47 us (5%)
  local copies, waits for them, and re-layouts  3.38 us (2%)
    all_to_all x3, blocking collectives, exchanged(): return lax.all_to_all(value, axes, split_axis=0, concat_axis=0, tiled=True)  64.3 us
    all_gather x1, waiting for transfers between devices, body(): cols = lax.all_gather(own, ('x', 'z'), axis=0, tiled=False)  49.4 us
    all_to_all x1, waiting for transfers between devices, exchanged(): return lax.all_to_all(value, axes, split_axis=0, concat_axis=0, tiled=True)  27.4 us
    pallas_call x1, Pallas kernels, pairs(): pl.pallas_call(pair_kernel, out_shape=(jax.ShapeDtypeStruct((count, width...  8.47 us
    ppermute x1, starting transfers between devices, body(): other = lax.ppermute(line, 'c', [(0, 1), (1, 0)])  5.62 us
    all_to_all x1, starting transfers between devices, exchanged(): return lax.all_to_all(value, axes, split_axis=0, concat_axis=0, tiled=True)  5.53 us
  transfers between devices with their start and end apart: 3, of which 3 were waited for; matrix products, arithmetic and copies ran while one was open for 1% of the time, Pallas kernels for 0%

profile of v1, /device:TPU:1, one launch (start us, length us, event | category | flops | bytes accessed | tf_op | source)
XLA Modules:
  0.0 182.2 jit_solution(2476792920071418055)
XLA Ops:
  7.2 0.0 all-gather.3.cloned.1.call-start
  7.2 0.8 constant_dynamic-update-slice_fusion.1
  8.1 0.8 constant_dynamic-update-slice_fusion
  8.9 0.0 copy-start
  8.9 0.7 copy-done
  9.6 0.0 all-gather.3.cloned.1.call-update
  9.6 1.0 broadcast_in_dim.10
  10.6 33.4 %all_to_all.20 = f32[8,32,1024]{2,1,0:T(8,128)S(1)} all-to-all(f32[8,32,1024]{2,1,0:T(8,128)S(1)} %broadcast_in_dim.10), channel_id=1, replica_groups=mesh['x'=4,'yh'=4,'z'=8,'yl'=2,'c'=2] {'yh','yl'}, dimensions={0} | all-to-all | bytes 2097152 | tf_op jit(solution)/shard_map/all_to_all | solution.py:89
  44.0 5.6 %collective-permute-start = (f32[8,32,1024]{2,1,0:T(8,128)S(1)}, f32[8,32,1024]{2,1,0:T(8,128)S(1)}, u32[]{:S(2)}, u32[]{:S(2)}) collective-permute-start(f32[8,32,1024]{2,1,0:T(8,128)S(1)} %all_to_all.20), channel_id=1, source_target_pairs={{0,1},{1,0},{2,3},{3,2},{4,5},{5,4},{6,7},{7,6},{8,9},{9,8},{10,11... | collective-permute-start | bytes 3145736 | tf_op jit(solution)/shard_map/ppermute | solution.py:96
  49.6 2.3 %collective-permute-done = f32[8,32,1024]{2,1,0:T(8,128)S(1)} collective-permute-done((f32[8,32,1024]{2,1,0:T(8,128)S(1)}, f32[8,32,1024]{2,1,0:T(8,128)S(1)}, u32[]{:S(2)}, u32[]{:S(2)}) %collective-permute-start) | collective-permute-done | bytes 1048608 | tf_op jit(solution)/shard_map/ppermute | solution.py:96
  51.9 0.2 select_bitcast_fusion.1
  52.1 0.2 pad_maximum_fusion
  52.4 49.4 %all-gather.3.cloned.1.call-done = f32[1024,1024]{1,0:T(8,128)} async-done(((f32[32,1024]{1,0:T(8,128)}), f32[1024,1024]{1,0:T(8,128)}) %all-gather.3.cloned.1.call-update) | async-done | bytes 4194320 | tf_op jit(solution)/shard_map/all_gather | solution.py:94
  101.8 8.5 %shard_map.41 = (f32[256,1024]{1,0:T(8,128)}, f32[8,128]{1,0:T(8,128)S(1)}) custom-call(f32[16,32,1024]{2,1,0:T(8,128)S(1)} %bitcast.16, f32[32,32,1024]{2,1,0:T(8,128)} %bitcast.20), custom_call_target="tpu_custom_call" | custom-call | flops 4000000000 | bytes 8000000 | tf_op jit(solution)/shard_map/pallas_call | solution.py:75
  110.3 17.6 %all_to_all.21 = f32[16,1,128]{2,1,0:T(1,128)S(1)} all-to-all(f32[16,1,128]{2,1,0:T(1,128)S(1)} %broadcast_in_dim.25), channel_id=1, replica_groups=mesh['x'=4,'yh'=4,'z'=8,'yl'=2,'c'=2] {'yh','yl','c'}, dimensions={0} | all-to-all | bytes 16384 | tf_op jit(solution)/shard_map/all_to_all | solution.py:89
  127.9 13.3 %all_to_all.22 = f32[32,1,128]{2,1,0:T(1,128)S(1)} all-to-all(f32[32,1,128]{2,1,0:T(1,128)S(1)} %broadcast_in_dim.26), channel_id=1, replica_groups=mesh['x'=4,'yh'=4,'z'=8,'yl'=2,'c'=2] {'x','z'}, dimensions={0} | all-to-all | bytes 32768 | tf_op jit(solution)/shard_map/all_to_all | solution.py:89
  141.2 5.5 %all-to-all-start.1 = ((f32[16,16,1024]{2,1,0:T(8,128)}), f32[16,16,1024]{2,1,0:T(8,128)S(1)}, u32[]{:S(2)}, u32[]{:S(2)}) async-start(f32[16,16,1024]{2,1,0:T(8,128)} %bitcast.5), calls=%async_computation.1 | async-start | bytes 2097152 | tf_op jit(solution)/shard_map/all_to_all | solution.py:89
  146.7 0.5 reduce_sum.31
  147.2 27.4 %all-to-all-done.1 = f32[16,16,1024]{2,1,0:T(8,128)S(1)} async-done(((f32[16,16,1024]{2,1,0:T(8,128)}), f32[16,16,1024]{2,1,0:T(8,128)S(1)}, u32[]{:S(2)}, u32[]{:S(2)}) %all-to-all-start.1) | async-done | bytes 1048608 | tf_op jit(solution)/shard_map/all_to_all | solution.py:89
  174.7 0.7 reduce_sum.29
  (4 shorter events, 0.0 us)
Async XLA Ops:
  7.2 94.6 %all-gather.3.cloned.1.call-start = ((), (), s32[]{:S(2)}) async-start(), calls=%async_computation.4 | async-start | bytes 4325376 | tf_op jit(solution)/shard_map/all_gather | solution.py:94
  8.9 0.7 copy-start
  44.0 7.9 %collective-permute-start = (f32[8,32,1024]{2,1,0:T(8,128)S(1)}, f32[8,32,1024]{2,1,0:T(8,128)S(1)}, u32[]{:S(2)}, u32[]{:S(2)}) collective-permute-start(f32[8,32,1024]{2,1,0:T(8,128)S(1)} %all_to_all.20), channel_id=1, source_target_pairs={{0,1},{1,0},{2,3},{3,2},{4,5},{5,4},{6,7},{7,6},{8,9},{9,8},{10,11... | collective-permute-start | bytes 3145736 | tf_op jit(solution)/shard_map/ppermute | solution.py:96
  141.2 33.5 %all-to-all-start.1 = ((f32[16,16,1024]{2,1,0:T(8,128)}), f32[16,16,1024]{2,1,0:T(8,128)S(1)}, u32[]{:S(2)}, u32[]{:S(2)}) async-start(f32[16,16,1024]{2,1,0:T(8,128)} %bitcast.5), calls=%async_computation.1 | async-start | bytes 2097152 | tf_op jit(solution)/shard_map/all_to_all | solution.py:89
Sparse Core Ops, SparseCore 0:
  11.2 90.5 all-gather.2

commit v2 on v1

v2 whole, which is shorter than its diff:
```python
import jax
import jax.numpy as jnp
from jax import lax
from jax.experimental import pallas as pl
from jax.experimental.pallas import tpu as pltpu
from jax.sharding import Mesh, PartitionSpec as P

AXES = ("x", "yh", "z", "yl", "c")
SIZES = dict(zip(AXES, (4, 4, 8, 2, 2)))
Y = ("yh", "yl")
OWN = 16
WIDTH = 1024
ROOT_WIDTH = 32.0
COUNT = 8192.0
NT = (((1,), (1,)), ((), ()))
NN = (((1,), (0,)), ((), ()))


def halves(value):
    high = value.astype(jnp.bfloat16)
    low = (value - high.astype(jnp.float32)).astype(jnp.bfloat16)
    return high, low


def product(left, right, dims):
    def dot(a, b):
        return lax.dot_general(a, b, dims, preferred_element_type=jnp.float32)

    return dot(left[0], right[0]) + (dot(left[0], right[1]) + dot(left[1], right[0]))


def flat(block):
    return block.reshape(block.shape[0] * block.shape[1], block.shape[2])


def pair_kernel(n_cols, line_ref, other_ref, *refs):
    col_refs = refs[:n_cols]
    mine_ref, away_ref, energy_ref, high_ref, low_ref = refs[n_cols:]
    units = [ref[member] for ref in (line_ref, other_ref) for member in range(ref.shape[0])]
    half = len(units) // 2 * OWN
    row_gen = jnp.concatenate([unit[:OWN] for unit in units], axis=0)
    row_data = jnp.concatenate([unit[OWN:] for unit in units], axis=0)
    count = 2 * half
    rows = jnp.concatenate([row_gen, row_data], axis=0)
    rows_sq = jnp.sum(rows * rows, axis=1, keepdims=True)
    rows_hl = halves(rows)
    squares = []
    for kind in range(2):
        at = 0
        for ref in col_refs:
            cols = flat(ref[:, kind * OWN : (kind + 1) * OWN, :])
            squares.append(jnp.sum(cols * cols, axis=1, keepdims=True))
            high, low = halves(cols)
            high_ref[kind, at : at + cols.shape[0], :] = high
            low_ref[kind, at : at + cols.shape[0], :] = low
            at += cols.shape[0]
    depth = high_ref.shape[1]
    squares = jnp.concatenate(squares, axis=0)
    squares = jnp.transpose(jnp.broadcast_to(squares, (2 * depth, 128)))[0:1, :]
    chunk = 256
    total = jnp.zeros((count, 1), jnp.float32)
    force = jnp.zeros(row_gen.shape, jnp.float32)
    energy = jnp.zeros((1, chunk), jnp.float32)
    for kind in range(2):
        for start in range(0, depth, chunk):
            cols_hl = (high_ref[kind, start : start + chunk, :], low_ref[kind, start : start + chunk, :])
            cols_sq = squares[:, kind * depth + start : kind * depth + start + chunk]
            used = count if kind == 0 else 2 * count
            inner = product((rows_hl[0][:used], rows_hl[1][:used]), cols_hl, NT)
            square = jnp.maximum(rows_sq[:used] + cols_sq - 2.0 * inner, 0.0) + 1.0
            inverse = lax.rsqrt(square)
            distance = square * inverse
            near = jnp.sum(distance[:count], axis=0, keepdims=True)
            if kind == 0:
                energy = energy - near
            else:
                energy = energy + 2.0 * near
                energy = energy - jnp.sum(distance[count:], axis=0, keepdims=True)
            coef = (-1.0 if kind == 0 else 1.0) * ROOT_WIDTH / COUNT
            weight = coef * inverse[:count]
            total = total + jnp.sum(weight, axis=1, keepdims=True)
            force = force + product(halves(weight), cols_hl, NN)
    force = total * row_gen - force
    for member in range(len(units) // 2):
        mine_ref[member] = force[member * OWN : (member + 1) * OWN]
        away_ref[member] = force[half + member * OWN : half + (member + 1) * OWN]
    energy_ref[...] = jnp.broadcast_to(
        jnp.sum(energy, axis=1, keepdims=True) / (COUNT * COUNT * ROOT_WIDTH), energy_ref.shape
    )


def pairs(line, other, cols):
    members = line.shape[0]
    depth = sum(c.shape[0] for c in cols) * OWN
    vmem = pl.BlockSpec(memory_space=pltpu.VMEM)

    def kernel(*refs):
        pair_kernel(len(cols), *refs)

    return pl.pallas_call(
        kernel,
        out_shape=(
            jax.ShapeDtypeStruct((members, OWN, WIDTH), jnp.float32),
            jax.ShapeDtypeStruct((members, OWN, WIDTH), jnp.float32),
            jax.ShapeDtypeStruct((8, 128), jnp.float32),
        ),
        in_specs=[vmem] * (2 + len(cols)),
        out_specs=[vmem] * 3,
        scratch_shapes=[pltpu.VMEM((2, depth, WIDTH), jnp.bfloat16)] * 2,
        compiler_params=pltpu.CompilerParams(vmem_limit_bytes=40 * 1024 * 1024),
        cost_estimate=pl.CostEstimate(flops=4_000_000_000, bytes_accessed=8_000_000, transcendentals=400_000),
    )(line, other, *cols)


def sent(value, axes, move):
    sizes = [SIZES[a] for a in axes]
    perm = []
    total = 1
    for s in sizes:
        total *= s
    for source in range(total):
        rest, place = source, []
        for s in reversed(sizes):
            place.insert(0, rest % s)
            rest //= s
        target = 0
        for s, p in zip(sizes, move(*place)):
            target = target * s + p % s
        perm.append((source, target))
    return lax.ppermute(value, axes, perm)


def exchanged(value, axes):
    return lax.all_to_all(value, axes, split_axis=0, concat_axis=0, tiled=True)


def swapped(value):
    return sent(value, ("c",), lambda c: (1 - c,))


def shifted(value, axis, steps):
    return sent(value, (axis, "c"), lambda place, c: (place + steps * (1 - 2 * c), c))


def exchanged(value, axes):
    return lax.all_to_all(value, axes, split_axis=0, concat_axis=0, tiled=True)


def swapped(value):
    return sent(value, ("c",), lambda c: (1 - c,))


def joined(*parts):
    return jnp.concatenate(parts, axis=0)


def columns(own):
    parity = [own]
    for _ in range(3):
        parity.append(shifted(parity[-1], "z", 2))
    first = jnp.stack(parity)
    second = shifted(first, "x", 1)
    third = shifted(second, "x", 1)
    fourth = shifted(third, "x", 1)
    early, late = joined(first, second), joined(third, fourth)
    return [early, swapped(early), late, swapped(late)]


def body(generated, data):
    own = jnp.concatenate([generated, data], axis=0)
    line = exchanged(jnp.broadcast_to(own[None], (8,) + own.shape), Y)
    mine, away, energy = pairs(line, shifted(line, "z", -1), columns(own))
    energy = jnp.broadcast_to(energy[None, :1], (32, 1, 128))
    energy = jnp.sum(exchanged(energy, ("x", "z")), axis=0)
    mine = mine + shifted(away, "z", 1)
    force_rows = jnp.sum(exchanged(mine, Y), axis=0)
    energy = energy + swapped(energy)
    for bit in (1, 2, 4):
        energy = energy + sent(energy, Y, lambda hi, lo: divmod((2 * hi + lo) ^ bit, 2))
    return (force_rows, energy[0, 0])


def solution(mesh):
    fine = Mesh(mesh.devices.reshape(tuple(SIZES.values())), AXES)
    placed = P(AXES, None)
    return jax.shard_map(body, mesh=fine, in_specs=(placed, placed), out_specs=(placed, P()), check_vma=False)
```

time: 183 us -> 151 us (0.83)
  the two profiles are of different devices: /device:TPU:1 before, /device:TPU:40 now
where the time goes in v2:
time: 151 us
  waiting for transfers between devices  71.1 us (47%)
  starting transfers between devices  63.6 us (42%)
  Pallas kernels  6.91 us (5%)
  local copies, waits for them, and re-layouts  6.18 us (4%)
  other arithmetic  2.09 us (1%)
    ppermute x14, waiting for transfers between devices, sent(): return lax.ppermute(value, axes, perm)  62.4 us
    ppermute x14, starting transfers between devices, sent(): return lax.ppermute(value, axes, perm)  39.7 us
    all_to_all x3, starting transfers between devices, exchanged(): return lax.all_to_all(value, axes, split_axis=0, concat_axis=0, tiled=True)  23.9 us
    all_to_all x3, waiting for transfers between devices, exchanged(): return lax.all_to_all(value, axes, split_axis=0, concat_axis=0, tiled=True)  8.77 us
    pallas_call x1, Pallas kernels, pairs(): pl.pallas_call(kernel, out_shape=(jax.ShapeDtypeStruct((members, OWN, WID...  6.91 us
    unnamed x8, local copies, waits for them, and re-layouts  3.57 us
  transfers between devices with their start and end apart: 17, of which 11 were waited for; matrix products, arithmetic and copies ran while one was open for 4% of the time, Pallas kernels for 0%

profile of v2, /device:TPU:40, one launch (start us, length us, event | category | flops | bytes accessed | tf_op | source)
XLA Modules:
  0.0 150.7 jit_solution(6805787421706523070)
XLA Ops:
  0.6 0.9 constant_dynamic-update-slice_fusion.1
  1.5 6.1 %collective-permute-start.1 = (f32[32,1024]{1,0:T(8,128)S(1)}, f32[32,1024]{1,0:T(8,128)S(1)}, u32[]{:S(2)}, u32[]{:S(2)}) collective-permute-start(f32[32,1024]{1,0:T(8,128)S(1)} %constant_dynamic-update-slice_fusion), channel_id=1, source_target_pairs={{0,8},{1,25},{4,12},{5,29},{8,16},{9,1},{12,20},{13,5},{16,24},{17... | collective-permute-start | bytes 393224 | tf_op jit(solution)/shard_map/ppermute | solution.py:130
  7.6 7.9 %collective-permute-done.1 = f32[32,1024]{1,0:T(8,128)S(1)} collective-permute-done((f32[32,1024]{1,0:T(8,128)S(1)}, f32[32,1024]{1,0:T(8,128)S(1)}, u32[]{:S(2)}, u32[]{:S(2)}) %collective-permute-start.1) | collective-permute-done | bytes 131104 | tf_op jit(solution)/shard_map/ppermute | solution.py:130
  15.5 1.9 %collective-permute-start.2 = (f32[32,1024]{1,0:T(8,128)S(1)}, f32[32,1024]{1,0:T(8,128)S(1)}, u32[]{:S(2)}, u32[]{:S(2)}) collective-permute-start(f32[32,1024]{1,0:T(8,128)S(1)} %collective-permute-done.1), channel_id=1, source_target_pairs={{0,8},{1,25},{4,12},{5,29},{8,16},{9,1},{12,20},{13,5},{16,24},{17... | collective-permute-start | bytes 393224 | tf_op jit(solution)/shard_map/ppermute | solution.py:130
  17.4 7.0 %collective-permute-done.2 = f32[32,1024]{1,0:T(8,128)S(1)} collective-permute-done((f32[32,1024]{1,0:T(8,128)S(1)}, f32[32,1024]{1,0:T(8,128)S(1)}, u32[]{:S(2)}, u32[]{:S(2)}) %collective-permute-start.2) | collective-permute-done | bytes 131104 | tf_op jit(solution)/shard_map/ppermute | solution.py:130
  24.5 2.5 %collective-permute-start.3 = (f32[32,1024]{1,0:T(8,128)S(1)}, f32[32,1024]{1,0:T(8,128)S(1)}, u32[]{:S(2)}, u32[]{:S(2)}) collective-permute-start(f32[32,1024]{1,0:T(8,128)S(1)} %collective-permute-done.2), channel_id=1, source_target_pairs={{0,8},{1,25},{4,12},{5,29},{8,16},{9,1},{12,20},{13,5},{16,24},{17... | collective-permute-start | bytes 393224 | tf_op jit(solution)/shard_map/ppermute | solution.py:130
  27.0 1.1 broadcast_in_dim.16
  28.1 7.1 %all-to-all-start = ((f32[8,32,1024]{2,1,0:T(8,128)}), f32[8,32,1024]{2,1,0:T(8,128)S(1)}, u32[]{:S(2)}, u32[]{:S(2)}) async-start(f32[8,32,1024]{2,1,0:T(8,128)} %broadcast_in_dim.16), calls=%async_computation | async-start | bytes 2097152 | tf_op jit(solution)/shard_map/all_to_all | solution.py:146
  35.2 3.4 %collective-permute-start.4 = (f32[4,32,1024]{2,1,0:T(8,128)S(1)}, f32[4,32,1024]{2,1,0:T(8,128)S(1)}, u32[]{:S(2)}, u32[]{:S(2)}) collective-permute-start(f32[4,32,1024]{2,1,0:T(8,128)S(1)} %pad_maximum_fusion), channel_id=1, source_target_pairs={{0,128},{1,385},{128,256},{129,1},{256,384},{257,129},{384,0},{385... | collective-permute-start | bytes 1572872 | tf_op jit(solution)/shard_map/ppermute | solution.py:130
  38.6 8.9 %collective-permute-done.4 = f32[4,32,1024]{2,1,0:T(8,128)S(1)} collective-permute-done((f32[4,32,1024]{2,1,0:T(8,128)S(1)}, f32[4,32,1024]{2,1,0:T(8,128)S(1)}, u32[]{:S(2)}, u32[]{:S(2)}) %collective-permute-start.4) | collective-permute-done | bytes 524320 | tf_op jit(solution)/shard_map/ppermute | solution.py:130
  47.5 2.2 %collective-permute-start.6 = (f32[4,32,1024]{2,1,0:T(8,128)S(1)}, f32[4,32,1024]{2,1,0:T(8,128)S(1)}, u32[]{:S(2)}, u32[]{:S(2)}) collective-permute-start(f32[4,32,1024]{2,1,0:T(8,128)S(1)} %collective-permute-done.4), channel_id=1, source_target_pairs={{0,128},{1,385},{128,256},{129,1},{256,384},{257,129},{384,0},{385... | collective-permute-start | bytes 1572872 | tf_op jit(solution)/shard_map/ppermute | solution.py:130
  51.0 8.8 %collective-permute-done.6 = f32[4,32,1024]{2,1,0:T(8,128)S(1)} collective-permute-done((f32[4,32,1024]{2,1,0:T(8,128)S(1)}, f32[4,32,1024]{2,1,0:T(8,128)S(1)}, u32[]{:S(2)}, u32[]{:S(2)}) %collective-permute-start.6) | collective-permute-done | bytes 524320 | tf_op jit(solution)/shard_map/ppermute | solution.py:130
  59.8 1.9 %collective-permute-start.7 = (f32[4,32,1024]{2,1,0:T(8,128)S(1)}, f32[4,32,1024]{2,1,0:T(8,128)S(1)}, u32[]{:S(2)}, u32[]{:S(2)}) collective-permute-start(f32[4,32,1024]{2,1,0:T(8,128)S(1)} %collective-permute-done.6), channel_id=1, source_target_pairs={{0,128},{1,385},{128,256},{129,1},{256,384},{257,129},{384,0},{385... | collective-permute-start | bytes 1572872 | tf_op jit(solution)/shard_map/ppermute | solution.py:130
  63.0 0.8 constant_dynamic-update-slice_fusion.2.refs_2_
  63.8 5.3 %collective-permute-start.5 = (f32[8,32,1024]{2,1,0:T(8,128)}, f32[8,32,1024]{2,1,0:T(8,128)}, u32[]{:S(2)}, u32[]{:S(2)}) collective-permute-start(f32[8,32,1024]{2,1,0:T(8,128)} %constant_dynamic-update-slice_fusion.2.refs_2_), channel_id=1, source_target_pairs={{0,1},{1,0},{2,3},{3,2},{4,5},{5,4},{6,7},{7,6},{8,9},{9,8},{10,11... | collective-permute-start | bytes 3145736 | tf_op jit(solution)/shard_map/ppermute | solution.py:130
  69.2 3.5 %collective-permute-start = (f32[8,32,1024]{2,1,0:T(8,128)S(1)}, f32[8,32,1024]{2,1,0:T(8,128)S(1)}, u32[]{:S(2)}, u32[]{:S(2)}) collective-permute-start(f32[8,32,1024]{2,1,0:T(8,128)S(1)} %all-to-all-done.refs_0_), channel_id=1, source_target_pairs={{0,28},{1,5},{4,0},{5,9},{8,4},{9,13},{12,8},{13,17},{16,12},{17,2... | collective-permute-start | bytes 3145736 | tf_op jit(solution)/shard_map/ppermute | solution.py:130
  72.7 1.9 %collective-permute-start.8 = (f32[8,32,1024]{2,1,0:T(8,128)S(1)}, f32[8,32,1024]{2,1,0:T(8,128)S(1)}, u32[]{:S(2)}, u32[]{:S(2)}) collective-permute-start(f32[8,32,1024]{2,1,0:T(8,128)S(1)} %constant_dynamic-update-slice_fusion.7.refs_4_), channel_id=1, source_target_pairs={{0,1},{1,0},{2,3},{3,2},{4,5},{5,4},{6,7},{7,6},{8,9},{9,8},{10,11... | collective-permute-start | bytes 3145736 | tf_op jit(solution)/shard_map/ppermute | solution.py:130
  74.7 11.2 %collective-permute-done.refs_1_ = f32[8,32,1024]{2,1,0:T(8,128)S(1)} collective-permute-done((f32[8,32,1024]{2,1,0:T(8,128)S(1)}, f32[8,32,1024]{2,1,0:T(8,128)S(1)}, u32[]{:S(2)}, u32[]{:S(2)}) %collective-permute-start) | collective-permute-done | bytes 1048608 | tf_op jit(solution)/shard_map/ppermute | solution.py:130
  85.9 6.9 %shard_map.41 = (f32[8,16,1024]{2,1,0:T(8,128)S(1)}, f32[8,16,1024]{2,1,0:T(8,128)S(1)}, f32[8,128]{1,0:T(8,128)S(1)}) custom-call(f32[8,32,1024]{2,1,0:T(8,128)S(1)} %all-to-all-done.refs_0_, f32[8,32,1024]{2,1,0:T(8,128)S(1)} %collective-permute-done.refs_1_, f32[8,32,1024]{2,1,0:T(8,128)} %constant_dynamic-update-slice_fusion.2.refs_2_, ...), custom_call_target="tpu_custom_call" | custom-call | flops 4000000000 | bytes 8000000 | tf_op jit(solution)/shard_map/pallas_call | solution.py:100
  92.8 1.9 %collective-permute-start.9 = (f32[8,16,1024]{2,1,0:T(8,128)S(1)}, f32[8,16,1024]{2,1,0:T(8,128)S(1)}, u32[]{:S(2)}, u32[]{:S(2)}) collective-permute-start(f32[8,16,1024]{2,1,0:T(8,128)S(1)} %get-tuple-element.6), channel_id=1, source_target_pairs={{0,4},{1,29},{4,8},{5,1},{8,12},{9,5},{12,16},{13,9},{16,20},{17,1... | collective-permute-start | bytes 1572872 | tf_op jit(solution)/shard_map/ppermute | solution.py:130
  95.3 9.6 %all-to-all-start.2 = ((f32[32,1,128]{2,1,0:T(1,128)}), f32[32,1,128]{2,1,0:T(1,128)S(1)}, u32[]{:S(2)}, u32[]{:S(2)}) async-start(f32[32,1,128]{2,1,0:T(1,128)} %broadcast_in_dim.19), calls=%async_computation.2 | async-start | bytes 32768 | tf_op jit(solution)/shard_map/all_to_all | solution.py:146
  105.1 0.9 add.15
  105.9 8.8 %all-to-all-done.2 = f32[32,1,128]{2,1,0:T(1,128)S(1)} async-done(((f32[32,1,128]{2,1,0:T(1,128)}), f32[32,1,128]{2,1,0:T(1,128)S(1)}, u32[]{:S(2)}, u32[]{:S(2)}) %all-to-all-start.2) | async-done | bytes 16416 | tf_op jit(solution)/shard_map/all_to_all | solution.py:146
  114.7 7.2 %all-to-all-start.1 = ((f32[8,16,1024]{2,1,0:T(8,128)}), f32[8,16,1024]{2,1,0:T(8,128)S(1)}, u32[]{:S(2)}, u32[]{:S(2)}) async-start(f32[8,16,1024]{2,1,0:T(8,128)} %add.15), calls=%async_computation.1 | async-start | bytes 1048576 | tf_op jit(solution)/shard_map/all_to_all | solution.py:146
  121.9 1.9 %collective-permute-start.10 = (f32[1,128]{1,0:T(1,128)S(1)}, f32[1,128]{1,0:T(1,128)S(1)}, u32[]{:S(2)}, u32[]{:S(2)}) collective-permute-start(f32[1,128]{1,0:T(1,128)S(1)} %bitcast.20), channel_id=1, source_target_pairs={{0,1},{1,0},{2,3},{3,2},{4,5},{5,4},{6,7},{7,6},{8,9},{9,8},{10,11... | collective-permute-start | bytes 1544 | tf_op jit(solution)/shard_map/ppermute | solution.py:130
  123.8 1.1 collective-permute-done.10
  124.9 3.4 %collective-permute-start.11 = (f32[1,128]{1,0:T(1,128)S(1)}, f32[1,128]{1,0:T(1,128)S(1)}, u32[]{:S(2)}, u32[]{:S(2)}) collective-permute-start(f32[1,128]{1,0:T(1,128)S(1)} %bitcast_add_fusion), channel_id=1, source_target_pairs={{0,2},{2,0},{32,34},{34,32},{64,66},{66,64},{96,98},{98,96},{1,3},... | collective-permute-start | bytes 1544 | tf_op jit(solution)/shard_map/ppermute | solution.py:130
  128.3 5.6 %collective-permute-done.11 = f32[1,128]{1,0:T(1,128)S(1)} collective-permute-done((f32[1,128]{1,0:T(1,128)S(1)}, f32[1,128]{1,0:T(1,128)S(1)}, u32[]{:S(2)}, u32[]{:S(2)}) %collective-permute-start.11) | collective-permute-done | bytes 544 | tf_op jit(solution)/shard_map/ppermute | solution.py:130
  133.9 1.9 %collective-permute-start.12 = (f32[1,128]{1,0:T(1,128)S(1)}, f32[1,128]{1,0:T(1,128)S(1)}, u32[]{:S(2)}, u32[]{:S(2)}) collective-permute-start(f32[1,128]{1,0:T(1,128)S(1)} %add.17), channel_id=1, source_target_pairs={{0,32},{2,34},{32,0},{34,2},{64,96},{66,98},{96,64},{98,66},{1,33}... | collective-permute-start | bytes 1544 | tf_op jit(solution)/shard_map/ppermute | solution.py:130
  135.8 4.4 %collective-permute-done.12 = f32[1,128]{1,0:T(1,128)S(1)} collective-permute-done((f32[1,128]{1,0:T(1,128)S(1)}, f32[1,128]{1,0:T(1,128)S(1)}, u32[]{:S(2)}, u32[]{:S(2)}) %collective-permute-start.12) | collective-permute-done | bytes 544 | tf_op jit(solution)/shard_map/ppermute | solution.py:130
  140.2 1.9 %collective-permute-start.13 = (f32[1,128]{1,0:T(1,128)S(1)}, f32[1,128]{1,0:T(1,128)S(1)}, u32[]{:S(2)}, u32[]{:S(2)}) collective-permute-start(f32[1,128]{1,0:T(1,128)S(1)} %add.18), channel_id=1, source_target_pairs={{0,64},{2,66},{32,96},{34,98},{64,0},{66,2},{96,32},{98,34},{1,65}... | collective-permute-start | bytes 1544 | tf_op jit(solution)/shard_map/ppermute | solution.py:130
  142.2 7.4 %collective-permute-done.13 = f32[1,128]{1,0:T(1,128)S(1)} collective-permute-done((f32[1,128]{1,0:T(1,128)S(1)}, f32[1,128]{1,0:T(1,128)S(1)}, u32[]{:S(2)}, u32[]{:S(2)}) %collective-permute-start.13) | collective-permute-done | bytes 544 | tf_op jit(solution)/shard_map/ppermute | solution.py:130
  (25 shorter events, 4.7 us)
Async XLA Ops:
  0.6 0.9 copy-start
  1.5 14.0 %collective-permute-start.1 = (f32[32,1024]{1,0:T(8,128)S(1)}, f32[32,1024]{1,0:T(8,128)S(1)}, u32[]{:S(2)}, u32[]{:S(2)}) collective-permute-start(f32[32,1024]{1,0:T(8,128)S(1)} %constant_dynamic-update-slice_fusion), channel_id=1, source_target_pairs={{0,8},{1,25},{4,12},{5,29},{8,16},{9,1},{12,20},{13,5},{16,24},{17... | collective-permute-start | bytes 393224 | tf_op jit(solution)/shard_map/ppermute | solution.py:130
  15.5 9.0 %collective-permute-start.2 = (f32[32,1024]{1,0:T(8,128)S(1)}, f32[32,1024]{1,0:T(8,128)S(1)}, u32[]{:S(2)}, u32[]{:S(2)}) collective-permute-start(f32[32,1024]{1,0:T(8,128)S(1)} %collective-permute-done.1), channel_id=1, source_target_pairs={{0,8},{1,25},{4,12},{5,29},{8,16},{9,1},{12,20},{13,5},{16,24},{17... | collective-permute-start | bytes 393224 | tf_op jit(solution)/shard_map/ppermute | solution.py:130
  24.5 10.7 %collective-permute-start.3 = (f32[32,1024]{1,0:T(8,128)S(1)}, f32[32,1024]{1,0:T(8,128)S(1)}, u32[]{:S(2)}, u32[]{:S(2)}) collective-permute-start(f32[32,1024]{1,0:T(8,128)S(1)} %collective-permute-done.2), channel_id=1, source_target_pairs={{0,8},{1,25},{4,12},{5,29},{8,16},{9,1},{12,20},{13,5},{16,24},{17... | collective-permute-start | bytes 393224 | tf_op jit(solution)/shard_map/ppermute | solution.py:130
  28.1 41.1 %all-to-all-start = ((f32[8,32,1024]{2,1,0:T(8,128)}), f32[8,32,1024]{2,1,0:T(8,128)S(1)}, u32[]{:S(2)}, u32[]{:S(2)}) async-start(f32[8,32,1024]{2,1,0:T(8,128)} %broadcast_in_dim.16), calls=%async_computation | async-start | bytes 2097152 | tf_op jit(solution)/shard_map/all_to_all | solution.py:146
  35.2 12.3 %collective-permute-start.4 = (f32[4,32,1024]{2,1,0:T(8,128)S(1)}, f32[4,32,1024]{2,1,0:T(8,128)S(1)}, u32[]{:S(2)}, u32[]{:S(2)}) collective-permute-start(f32[4,32,1024]{2,1,0:T(8,128)S(1)} %pad_maximum_fusion), channel_id=1, source_target_pairs={{0,128},{1,385},{128,256},{129,1},{256,384},{257,129},{384,0},{385... | collective-permute-start | bytes 1572872 | tf_op jit(solution)/shard_map/ppermute | solution.py:130
  47.5 12.3 %collective-permute-start.6 = (f32[4,32,1024]{2,1,0:T(8,128)S(1)}, f32[4,32,1024]{2,1,0:T(8,128)S(1)}, u32[]{:S(2)}, u32[]{:S(2)}) collective-permute-start(f32[4,32,1024]{2,1,0:T(8,128)S(1)} %collective-permute-done.4), channel_id=1, source_target_pairs={{0,128},{1,385},{128,256},{129,1},{256,384},{257,129},{384,0},{385... | collective-permute-start | bytes 1572872 | tf_op jit(solution)/shard_map/ppermute | solution.py:130
  59.8 12.9 %collective-permute-start.7 = (f32[4,32,1024]{2,1,0:T(8,128)S(1)}, f32[4,32,1024]{2,1,0:T(8,128)S(1)}, u32[]{:S(2)}, u32[]{:S(2)}) collective-permute-start(f32[4,32,1024]{2,1,0:T(8,128)S(1)} %collective-permute-done.6), channel_id=1, source_target_pairs={{0,128},{1,385},{128,256},{129,1},{256,384},{257,129},{384,0},{385... | collective-permute-start | bytes 1572872 | tf_op jit(solution)/shard_map/ppermute | solution.py:130
  63.8 10.8 %collective-permute-start.5 = (f32[8,32,1024]{2,1,0:T(8,128)}, f32[8,32,1024]{2,1,0:T(8,128)}, u32[]{:S(2)}, u32[]{:S(2)}) collective-permute-start(f32[8,32,1024]{2,1,0:T(8,128)} %constant_dynamic-update-slice_fusion.2.refs_2_), channel_id=1, source_target_pairs={{0,1},{1,0},{2,3},{3,2},{4,5},{5,4},{6,7},{7,6},{8,9},{9,8},{10,11... | collective-permute-start | bytes 3145736 | tf_op jit(solution)/shard_map/ppermute | solution.py:130
  69.2 16.7 %collective-permute-start = (f32[8,32,1024]{2,1,0:T(8,128)S(1)}, f32[8,32,1024]{2,1,0:T(8,128)S(1)}, u32[]{:S(2)}, u32[]{:S(2)}) collective-permute-start(f32[8,32,1024]{2,1,0:T(8,128)S(1)} %all-to-all-done.refs_0_), channel_id=1, source_target_pairs={{0,28},{1,5},{4,0},{5,9},{8,4},{9,13},{12,8},{13,17},{16,12},{17,2... | collective-permute-start | bytes 3145736 | tf_op jit(solution)/shard_map/ppermute | solution.py:130
  72.7 13.1 %collective-permute-start.8 = (f32[8,32,1024]{2,1,0:T(8,128)S(1)}, f32[8,32,1024]{2,1,0:T(8,128)S(1)}, u32[]{:S(2)}, u32[]{:S(2)}) collective-permute-start(f32[8,32,1024]{2,1,0:T(8,128)S(1)} %constant_dynamic-update-slice_fusion.7.refs_4_), channel_id=1, source_target_pairs={{0,1},{1,0},{2,3},{3,2},{4,5},{5,4},{6,7},{7,6},{8,9},{9,8},{10,11... | collective-permute-start | bytes 3145736 | tf_op jit(solution)/shard_map/ppermute | solution.py:130
  92.8 12.3 %collective-permute-start.9 = (f32[8,16,1024]{2,1,0:T(8,128)S(1)}, f32[8,16,1024]{2,1,0:T(8,128)S(1)}, u32[]{:S(2)}, u32[]{:S(2)}) collective-permute-start(f32[8,16,1024]{2,1,0:T(8,128)S(1)} %get-tuple-element.6), channel_id=1, source_target_pairs={{0,4},{1,29},{4,8},{5,1},{8,12},{9,5},{12,16},{13,9},{16,20},{17,1... | collective-permute-start | bytes 1572872 | tf_op jit(solution)/shard_map/ppermute | solution.py:130
  95.3 19.3 %all-to-all-start.2 = ((f32[32,1,128]{2,1,0:T(1,128)}), f32[32,1,128]{2,1,0:T(1,128)S(1)}, u32[]{:S(2)}, u32[]{:S(2)}) async-start(f32[32,1,128]{2,1,0:T(1,128)} %broadcast_in_dim.19), calls=%async_computation.2 | async-start | bytes 32768 | tf_op jit(solution)/shard_map/all_to_all | solution.py:146
  114.7 35.4 %all-to-all-start.1 = ((f32[8,16,1024]{2,1,0:T(8,128)}), f32[8,16,1024]{2,1,0:T(8,128)S(1)}, u32[]{:S(2)}, u32[]{:S(2)}) async-start(f32[8,16,1024]{2,1,0:T(8,128)} %add.15), calls=%async_computation.1 | async-start | bytes 1048576 | tf_op jit(solution)/shard_map/all_to_all | solution.py:146
  121.9 3.0 %collective-permute-start.10 = (f32[1,128]{1,0:T(1,128)S(1)}, f32[1,128]{1,0:T(1,128)S(1)}, u32[]{:S(2)}, u32[]{:S(2)}) collective-permute-start(f32[1,128]{1,0:T(1,128)S(1)} %bitcast.20), channel_id=1, source_target_pairs={{0,1},{1,0},{2,3},{3,2},{4,5},{5,4},{6,7},{7,6},{8,9},{9,8},{10,11... | collective-permute-start | bytes 1544 | tf_op jit(solution)/shard_map/ppermute | solution.py:130
  124.9 9.0 %collective-permute-start.11 = (f32[1,128]{1,0:T(1,128)S(1)}, f32[1,128]{1,0:T(1,128)S(1)}, u32[]{:S(2)}, u32[]{:S(2)}) collective-permute-start(f32[1,128]{1,0:T(1,128)S(1)} %bitcast_add_fusion), channel_id=1, source_target_pairs={{0,2},{2,0},{32,34},{34,32},{64,66},{66,64},{96,98},{98,96},{1,3},... | collective-permute-start | bytes 1544 | tf_op jit(solution)/shard_map/ppermute | solution.py:130
  133.9 6.3 %collective-permute-start.12 = (f32[1,128]{1,0:T(1,128)S(1)}, f32[1,128]{1,0:T(1,128)S(1)}, u32[]{:S(2)}, u32[]{:S(2)}) collective-permute-start(f32[1,128]{1,0:T(1,128)S(1)} %add.17), channel_id=1, source_target_pairs={{0,32},{2,34},{32,0},{34,2},{64,96},{66,98},{96,64},{98,66},{1,33}... | collective-permute-start | bytes 1544 | tf_op jit(solution)/shard_map/ppermute | solution.py:130
  140.2 9.3 %collective-permute-start.13 = (f32[1,128]{1,0:T(1,128)S(1)}, f32[1,128]{1,0:T(1,128)S(1)}, u32[]{:S(2)}, u32[]{:S(2)}) collective-permute-start(f32[1,128]{1,0:T(1,128)S(1)} %add.18), channel_id=1, source_target_pairs={{0,64},{2,66},{32,96},{34,98},{64,0},{66,2},{96,32},{98,34},{1,65}... | collective-permute-start | bytes 1544 | tf_op jit(solution)/shard_map/ppermute | solution.py:130

commit v3 on v2

--- a/solution.py
+++ b/solution.py
@@ -5,9 +5,11 @@
 from jax.experimental.pallas import tpu as pltpu
 from jax.sharding import Mesh, PartitionSpec as P
 
-AXES = ("x", "yh", "z", "yl", "c")
-SIZES = dict(zip(AXES, (4, 4, 8, 2, 2)))
+AXES = ("x", "yh", "zh", "zl", "yl", "c")
+SIZES = dict(zip(AXES, (4, 4, 4, 2, 2, 2)))
 Y = ("yh", "yl")
+Z = ("zh", "zl")
+STEPS = (0, 6, 2, 4)
 OWN = 16
 WIDTH = 1024
 ROOT_WIDTH = 32.0
@@ -33,7 +35,7 @@
     return block.reshape(block.shape[0] * block.shape[1], block.shape[2])
 
 
-def pair_kernel(n_cols, line_ref, other_ref, *refs):
+def pair_kernel(n_cols, place_ref, line_ref, other_ref, *refs):
     col_refs = refs[:n_cols]
     mine_ref, away_ref, energy_ref, high_ref, low_ref = refs[n_cols:]
     units = [ref[member] for ref in (line_ref, other_ref) for member in range(ref.shape[0])]
@@ -82,14 +84,15 @@
             force = force + product(halves(weight), cols_hl, NN)
     force = total * row_gen - force
     for member in range(len(units) // 2):
-        mine_ref[member] = force[member * OWN : (member + 1) * OWN]
-        away_ref[member] = force[half + member * OWN : half + (member + 1) * OWN]
+        to = lax.rem(place_ref[member // len(STEPS)] + STEPS[member % len(STEPS)], 8)
+        mine_ref[to] = force[member * OWN : (member + 1) * OWN]
+        away_ref[to] = force[half + member * OWN : half + (member + 1) * OWN]
     energy_ref[...] = jnp.broadcast_to(
         jnp.sum(energy, axis=1, keepdims=True) / (COUNT * COUNT * ROOT_WIDTH), energy_ref.shape
     )
 
 
-def pairs(line, other, cols):
+def pairs(place, line, other, cols):
     members = line.shape[0]
     depth = sum(c.shape[0] for c in cols) * OWN
     vmem = pl.BlockSpec(memory_space=pltpu.VMEM)
@@ -104,12 +107,12 @@
             jax.ShapeDtypeStruct((members, OWN, WIDTH), jnp.float32),
             jax.ShapeDtypeStruct((8, 128), jnp.float32),
         ),
-        in_specs=[vmem] * (2 + len(cols)),
+        in_specs=[pl.BlockSpec(memory_space=pltpu.SMEM)] + [vmem] * (2 + len(cols)),
         out_specs=[vmem] * 3,
         scratch_shapes=[pltpu.VMEM((2, depth, WIDTH), jnp.bfloat16)] * 2,
-        compiler_params=pltpu.CompilerParams(vmem_limit_bytes=40 * 1024 * 1024),
+        compiler_params=pltpu.CompilerParams(vmem_limit_bytes=24 * 1024 * 1024),
         cost_estimate=pl.CostEstimate(flops=4_000_000_000, bytes_accessed=8_000_000, transcendentals=400_000),
-    )(line, other, *cols)
+    )(place, line, other, *cols)
 
 
 def sent(value, axes, move):
@@ -138,45 +141,43 @@
     return sent(value, ("c",), lambda c: (1 - c,))
 
 
-def shifted(value, axis, steps):
-    return sent(value, (axis, "c"), lambda place, c: (place + steps * (1 - 2 * c), c))
+def along(value, axes, steps):
+    return sent(value, axes, lambda high, low: divmod((2 * high + low + steps) % 8, 2))
 
 
-def exchanged(value, axes):
-    return lax.all_to_all(value, axes, split_axis=0, concat_axis=0, tiled=True)
+def shifted(value, axes, steps):
+    def move(high, low, c):
+        return (*divmod((2 * high + low + steps * (1 - 2 * c)) % 8, 2), c)
 
-
-def swapped(value):
-    return sent(value, ("c",), lambda c: (1 - c,))
+    return sent(value, (*axes, "c"), move)
 
 
 def joined(*parts):
     return jnp.concatenate(parts, axis=0)
 
 
-def columns(own):
-    parity = [own]
-    for _ in range(3):
-        parity.append(shifted(parity[-1], "z", 2))
-    first = jnp.stack(parity)
-    second = shifted(first, "x", 1)
-    third = shifted(second, "x", 1)
-    fourth = shifted(third, "x", 1)
-    early, late = joined(first, second), joined(third, fourth)
-    return [early, swapped(early), late, swapped(late)]
-
-
 def body(generated, data):
     own = jnp.concatenate([generated, data], axis=0)
-    line = exchanged(jnp.broadcast_to(own[None], (8,) + own.shape), Y)
-    mine, away, energy = pairs(line, shifted(line, "z", -1), columns(own))
+    parity = exchanged(jnp.broadcast_to(own[None], (4,) + own.shape), ("zh",))
+    up, down = along(own, Y, 2), along(own, Y, -2)
+    parity, up, down = lax.optimization_barrier((parity, up, down))
+    cols = exchanged(jnp.broadcast_to(parity[None], (4,) + parity.shape), ("x",))
+    line = jnp.stack([own, up, down, along(up, Y, 2)])
+    line = joined(line, shifted(line, Y, -1))
+    near = shifted(line, Z, -1)
+    cols, near = lax.optimization_barrier((cols.reshape((16,) + own.shape), near))
+    core = lax.axis_index("c")
+    y = 2 * lax.axis_index("yh") + lax.axis_index("yl")
+    place = jnp.stack([y, y + 9 - 2 * core]).astype(jnp.int32)
+    mine, away, energy = pairs(place, line, near, [cols, swapped(cols)])
     energy = jnp.broadcast_to(energy[None, :1], (32, 1, 128))
-    energy = jnp.sum(exchanged(energy, ("x", "z")), axis=0)
-    mine = mine + shifted(away, "z", 1)
-    force_rows = jnp.sum(exchanged(mine, Y), axis=0)
+    energy = jnp.sum(exchanged(energy, ("x", "zh", "zl")), axis=0)
+    mine = mine + shifted(away, Z, 1)
+    loaded = jnp.concatenate([mine, jnp.broadcast_to(energy[None], (8, OWN, 128))], axis=2)
+    loaded = exchanged(loaded, Y)
+    force_rows = jnp.sum(loaded[:, :, :WIDTH], axis=0)
+    energy = jnp.sum(loaded[:, :1, WIDTH:], axis=0)
     energy = energy + swapped(energy)
-    for bit in (1, 2, 4):
-        energy = energy + sent(energy, Y, lambda hi, lo: divmod((2 * hi + lo) ^ bit, 2))
     return (force_rows, energy[0, 0])
 
 

time: 151 us -> 138 us (0.914)
  the two profiles are of different devices: /device:TPU:40 before, /device:TPU:1 now
where the time goes in v3:
time: 138 us; the launch traced here: 137 us
  starting transfers between devices  47.6 us (34%)
  waiting for transfers between devices  37.2 us (27%)
  blocking collectives  34.7 us (25%)
  local copies, waits for them, and re-layouts  7.51 us (5%)
  Pallas kernels  7.36 us (5%)
  other arithmetic  2.23 us (2%)
    all_to_all x2, blocking collectives, exchanged(): return lax.all_to_all(value, axes, split_axis=0, concat_axis=0, tiled=True)  34.7 us
    ppermute x8, starting transfers between devices, sent(): return lax.ppermute(value, axes, perm)  32.8 us
    ppermute x8, waiting for transfers between devices, sent(): return lax.ppermute(value, axes, perm)  23.4 us
    all_to_all x2, starting transfers between devices, exchanged(): return lax.all_to_all(value, axes, split_axis=0, concat_axis=0, tiled=True)  14.9 us
    all_to_all x2, waiting for transfers between devices, exchanged(): return lax.all_to_all(value, axes, split_axis=0, concat_axis=0, tiled=True)  13.7 us
    pallas_call x1, Pallas kernels, pairs(): pl.pallas_call(kernel, out_shape=(jax.ShapeDtypeStruct((members, OWN, WID...  7.36 us
    unnamed x9, local copies, waits for them, and re-layouts  3.1 us
  transfers between devices with their start and end apart: 10, of which 7 were waited for; matrix products, arithmetic and copies ran while one was open for 3% of the time, Pallas kernels for 0%

profile of v3, /device:TPU:1, one launch (start us, length us, event | category | flops | bytes accessed | tf_op | source)
XLA Modules:
  0.0 137.5 jit_solution(13776798261054664308)
XLA Ops:
  0.6 0.8 constant_dynamic-update-slice_fusion.1
  1.5 0.8 constant_dynamic-update-slice_fusion
  2.3 0.8 broadcast_in_dim.10
  3.2 10.8 %all-to-all-start = ((f32[4,32,1024]{2,1,0:T(8,128)}), f32[4,32,1024]{2,1,0:T(8,128)S(1)}, u32[]{:S(2)}, u32[]{:S(2)}) async-start(f32[4,32,1024]{2,1,0:T(8,128)} %broadcast_in_dim.10), calls=%async_computation | async-start | bytes 1048576 | tf_op jit(solution)/shard_map/all_to_all | solution.py:137
  14.0 5.9 %collective-permute-start.1 = (f32[32,1024]{1,0:T(8,128)S(1)}, f32[32,1024]{1,0:T(8,128)S(1)}, u32[]{:S(2)}, u32[]{:S(2)}) collective-permute-start(f32[32,1024]{1,0:T(8,128)S(1)} %constant_dynamic-update-slice_fusion), channel_id=1, source_target_pairs={{0,96},{2,98},{32,0},{34,2},{64,32},{66,34},{96,64},{98,66},{1,97}... | collective-permute-start | bytes 393224 | tf_op jit(solution)/shard_map/ppermute | solution.py:133
  19.9 1.9 %collective-permute-start = (f32[32,1024]{1,0:T(8,128)S(1)}, f32[32,1024]{1,0:T(8,128)S(1)}, u32[]{:S(2)}, u32[]{:S(2)}) collective-permute-start(f32[32,1024]{1,0:T(8,128)S(1)} %constant_dynamic-update-slice_fusion), channel_id=1, source_target_pairs={{0,32},{2,34},{32,64},{34,66},{64,96},{66,98},{96,0},{98,2},{1,33}... | collective-permute-start | bytes 393224 | tf_op jit(solution)/shard_map/ppermute | solution.py:133
  21.8 3.8 %collective-permute-done.1 = f32[32,1024]{1,0:T(8,128)S(1)} collective-permute-done((f32[32,1024]{1,0:T(8,128)S(1)}, f32[32,1024]{1,0:T(8,128)S(1)}, u32[]{:S(2)}, u32[]{:S(2)}) %collective-permute-start.1) | collective-permute-done | bytes 131104 | tf_op jit(solution)/shard_map/ppermute | solution.py:133
  25.6 3.3 %collective-permute-done = f32[32,1024]{1,0:T(8,128)S(1)} collective-permute-done((f32[32,1024]{1,0:T(8,128)S(1)}, f32[32,1024]{1,0:T(8,128)S(1)}, u32[]{:S(2)}, u32[]{:S(2)}) %collective-permute-start) | collective-permute-done | bytes 131104 | tf_op jit(solution)/shard_map/ppermute | solution.py:133
  28.9 1.9 %collective-permute-start.2 = (f32[32,1024]{1,0:T(8,128)S(1)}, f32[32,1024]{1,0:T(8,128)S(1)}, u32[]{:S(2)}, u32[]{:S(2)}) collective-permute-start(f32[32,1024]{1,0:T(8,128)S(1)} %collective-permute-done), channel_id=1, source_target_pairs={{0,32},{2,34},{32,64},{34,66},{64,96},{66,98},{96,0},{98,2},{1,33}... | collective-permute-start | bytes 393224 | tf_op jit(solution)/shard_map/ppermute | solution.py:133
  30.8 8.6 %collective-permute-done.2 = f32[32,1024]{1,0:T(8,128)S(1)} collective-permute-done((f32[32,1024]{1,0:T(8,128)S(1)}, f32[32,1024]{1,0:T(8,128)S(1)}, u32[]{:S(2)}, u32[]{:S(2)}) %collective-permute-start.2) | collective-permute-done | bytes 131104 | tf_op jit(solution)/shard_map/ppermute | solution.py:133
  39.4 0.8 pad_maximum_fusion.1
  40.3 1.9 %collective-permute-start.3 = (f32[4,32,1024]{2,1,0:T(8,128)}, f32[4,32,1024]{2,1,0:T(8,128)}, u32[]{:S(2)}, u32[]{:S(2)}) collective-permute-start(f32[4,32,1024]{2,1,0:T(8,128)} %pad_maximum_fusion.1), channel_id=1, source_target_pairs={{0,98},{1,3},{2,0},{3,33},{32,2},{33,35},{34,32},{35,65},{64,34},{... | collective-permute-start | bytes 1572872 | tf_op jit(solution)/shard_map/ppermute | solution.py:133
  42.2 1.6 %broadcast_in_dim.11 = f32[4,4,32,1024]{3,2,1,0:T(8,128)} broadcast(f32[4,32,1024]{2,1,0:T(8,128)S(1)} %all-to-all-done), dimensions={1,2,3} | broadcast | bytes 2621440 | tf_op jit(solution)/shard_map/broadcast_in_dim | solution.py:164
  43.8 4.0 %all-to-all-start.1 = ((f32[4,4,32,1024]{3,2,1,0:T(8,128)}), f32[4,4,32,1024]{3,2,1,0:T(8,128)S(1)}, u32[]{:S(2)}, u32[]{:S(2)}) async-start(f32[4,4,32,1024]{3,2,1,0:T(8,128)} %broadcast_in_dim.11), calls=%async_computation.1 | async-start | bytes 4194304 | tf_op jit(solution)/shard_map/all_to_all | solution.py:137
  47.9 3.8 %collective-permute-done.3 = f32[4,32,1024]{2,1,0:T(8,128)} collective-permute-done((f32[4,32,1024]{2,1,0:T(8,128)}, f32[4,32,1024]{2,1,0:T(8,128)}, u32[]{:S(2)}, u32[]{:S(2)}) %collective-permute-start.3) | collective-permute-done | bytes 524320 | tf_op jit(solution)/shard_map/ppermute | solution.py:133
  51.7 1.1 constant_dynamic-update-slice_fusion.2.refs_1_
  52.8 3.6 %collective-permute-start.4 = (f32[8,32,1024]{2,1,0:T(8,128)S(1)}, f32[8,32,1024]{2,1,0:T(8,128)}, u32[]{:S(2)}, u32[]{:S(2)}) collective-permute-start(f32[8,32,1024]{2,1,0:T(8,128)S(1)} %constant_dynamic-update-slice_fusion.2.refs_1_), channel_id=1, source_target_pairs={{0,28},{1,5},{4,0},{5,9},{8,4},{9,13},{12,8},{13,17},{16,12},{17,2... | collective-permute-start | bytes 3145736 | tf_op jit(solution)/shard_map/ppermute | solution.py:133
  56.4 1.0 copy-done
  57.4 13.7 %all-to-all-done.1 = f32[4,4,32,1024]{3,2,1,0:T(8,128)S(1)} async-done(((f32[4,4,32,1024]{3,2,1,0:T(8,128)}), f32[4,4,32,1024]{3,2,1,0:T(8,128)S(1)}, u32[]{:S(2)}, u32[]{:S(2)}) %all-to-all-start.1) | async-done | bytes 2097184 | tf_op jit(solution)/shard_map/all_to_all | solution.py:137
  71.1 5.9 %collective-permute-start.5 = (f32[16,32,1024]{2,1,0:T(8,128)S(1)}, f32[16,32,1024]{2,1,0:T(8,128)}, u32[]{:S(2)}, u32[]{:S(2)}) collective-permute-start(f32[16,32,1024]{2,1,0:T(8,128)S(1)} %bitcast.18), channel_id=1, source_target_pairs={{0,1},{1,0},{2,3},{3,2},{4,5},{5,4},{6,7},{7,6},{8,9},{9,8},{10,11... | collective-permute-start | bytes 6291464 | tf_op jit(solution)/shard_map/ppermute | solution.py:133
  77.0 0.1 pad_add_fusion.refs_0_
  77.1 3.8 %collective-permute-done.5.refs_4_ = f32[16,32,1024]{2,1,0:T(8,128)} collective-permute-done((f32[16,32,1024]{2,1,0:T(8,128)S(1)}, f32[16,32,1024]{2,1,0:T(8,128)}, u32[]{:S(2)}, u32[]{:S(2)}) %collective-permute-start.5) | collective-permute-done | bytes 2097184 | tf_op jit(solution)/shard_map/ppermute | solution.py:133
  80.9 1.2 copy-done.1
  82.2 7.4 %shard_map.41 = (f32[8,16,1024]{2,1,0:T(8,128)S(1)}, f32[8,16,1024]{2,1,0:T(8,128)S(1)}, f32[8,128]{1,0:T(8,128)S(1)}) custom-call(s32[2]{0:T(128)S(1)} %pad_add_fusion.refs_0_, f32[8,32,1024]{2,1,0:T(8,128)S(1)} %copy-done.1, f32[8,32,1024]{2,1,0:T(8,128)} %collective-permute-done.4.refs_2_, f32[16,32,1024]{2,1,0:T(8,128)S(1)} %bitcast.19, ...), custom_call_target="tpu_custom_call" | custom-call | flops 4000000000 | bytes 8000000 | tf_op jit(solution)/shard_map/pallas_call | solution.py:103
  89.5 5.6 %collective-permute-start.6 = (f32[8,16,1024]{2,1,0:T(8,128)S(1)}, f32[8,16,1024]{2,1,0:T(8,128)S(1)}, u32[]{:S(2)}, u32[]{:S(2)}) collective-permute-start(f32[8,16,1024]{2,1,0:T(8,128)S(1)} %get-tuple-element.16), channel_id=1, source_target_pairs={{0,4},{1,29},{4,8},{5,1},{8,12},{9,5},{12,16},{13,9},{16,20},{17,1... | collective-permute-start | bytes 1572872 | tf_op jit(solution)/shard_map/ppermute | solution.py:133
  95.2 13.0 %all_to_all.20 = f32[32,1,128]{2,1,0:T(1,128)S(1)} all-to-all(f32[32,1,128]{2,1,0:T(1,128)S(1)} %broadcast_in_dim.13), channel_id=1, replica_groups=mesh['x'=4,'yh'=4,'zh'=4,'zl'=2,'yl'=2,'c'=2] {'x','zh','zl'}, dimensions={0} | all-to-all | bytes 32768 | tf_op jit(solution)/shard_map/all_to_all | solution.py:137
  108.2 0.1 add.14
  108.3 21.7 %all_to_all.21 = f32[8,16,1152]{2,1,0:T(8,128)S(1)} all-to-all(f32[8,16,1152]{2,1,0:T(8,128)S(1)} %pad_maximum_fusion), channel_id=1, replica_groups=mesh['x'=4,'yh'=4,'zh'=4,'zl'=2,'yl'=2,'c'=2] {'yh','yl'}, dimensions={0} | all-to-all | bytes 1179648 | tf_op jit(solution)/shard_map/all_to_all | solution.py:137
  130.1 6.1 %collective-permute-start.7 = (f32[1,128]{1,0:T(1,128)S(1)}, f32[1,128]{1,0:T(1,128)S(1)}, u32[]{:S(2)}, u32[]{:S(2)}) collective-permute-start(f32[1,128]{1,0:T(1,128)S(1)} %bitcast.25), channel_id=1, source_target_pairs={{0,1},{1,0},{2,3},{3,2},{4,5},{5,4},{6,7},{7,6},{8,9},{9,8},{10,11... | collective-permute-start | bytes 1544 | tf_op jit(solution)/shard_map/ppermute | solution.py:133
  136.2 0.7 slice_reduce_fusion
  136.8 0.1 collective-permute-done.7
  137.0 0.5 bitcast_add_fusion
  (15 shorter events, 0.2 us)
Async XLA Ops:
  3.2 25.7 %all-to-all-start = ((f32[4,32,1024]{2,1,0:T(8,128)}), f32[4,32,1024]{2,1,0:T(8,128)S(1)}, u32[]{:S(2)}, u32[]{:S(2)}) async-start(f32[4,32,1024]{2,1,0:T(8,128)} %broadcast_in_dim.10), calls=%async_computation | async-start | bytes 1048576 | tf_op jit(solution)/shard_map/all_to_all | solution.py:137
  14.0 11.6 %collective-permute-start.1 = (f32[32,1024]{1,0:T(8,128)S(1)}, f32[32,1024]{1,0:T(8,128)S(1)}, u32[]{:S(2)}, u32[]{:S(2)}) collective-permute-start(f32[32,1024]{1,0:T(8,128)S(1)} %constant_dynamic-update-slice_fusion), channel_id=1, source_target_pairs={{0,96},{2,98},{32,0},{34,2},{64,32},{66,34},{96,64},{98,66},{1,97}... | collective-permute-start | bytes 393224 | tf_op jit(solution)/shard_map/ppermute | solution.py:133
  19.9 9.0 %collective-permute-start = (f32[32,1024]{1,0:T(8,128)S(1)}, f32[32,1024]{1,0:T(8,128)S(1)}, u32[]{:S(2)}, u32[]{:S(2)}) collective-permute-start(f32[32,1024]{1,0:T(8,128)S(1)} %constant_dynamic-update-slice_fusion), channel_id=1, source_target_pairs={{0,32},{2,34},{32,64},{34,66},{64,96},{66,98},{96,0},{98,2},{1,33}... | collective-permute-start | bytes 393224 | tf_op jit(solution)/shard_map/ppermute | solution.py:133
  28.9 10.5 %collective-permute-start.2 = (f32[32,1024]{1,0:T(8,128)S(1)}, f32[32,1024]{1,0:T(8,128)S(1)}, u32[]{:S(2)}, u32[]{:S(2)}) collective-permute-start(f32[32,1024]{1,0:T(8,128)S(1)} %collective-permute-done), channel_id=1, source_target_pairs={{0,32},{2,34},{32,64},{34,66},{64,96},{66,98},{96,0},{98,2},{1,33}... | collective-permute-start | bytes 393224 | tf_op jit(solution)/shard_map/ppermute | solution.py:133
  40.3 11.4 %collective-permute-start.3 = (f32[4,32,1024]{2,1,0:T(8,128)}, f32[4,32,1024]{2,1,0:T(8,128)}, u32[]{:S(2)}, u32[]{:S(2)}) collective-permute-start(f32[4,32,1024]{2,1,0:T(8,128)} %pad_maximum_fusion.1), channel_id=1, source_target_pairs={{0,98},{1,3},{2,0},{3,33},{32,2},{33,35},{34,32},{35,65},{64,34},{... | collective-permute-start | bytes 1572872 | tf_op jit(solution)/shard_map/ppermute | solution.py:133
  43.8 27.3 %all-to-all-start.1 = ((f32[4,4,32,1024]{3,2,1,0:T(8,128)}), f32[4,4,32,1024]{3,2,1,0:T(8,128)S(1)}, u32[]{:S(2)}, u32[]{:S(2)}) async-start(f32[4,4,32,1024]{3,2,1,0:T(8,128)} %broadcast_in_dim.11), calls=%async_computation.1 | async-start | bytes 4194304 | tf_op jit(solution)/shard_map/all_to_all | solution.py:137
  52.8 18.3 %collective-permute-start.4 = (f32[8,32,1024]{2,1,0:T(8,128)S(1)}, f32[8,32,1024]{2,1,0:T(8,128)}, u32[]{:S(2)}, u32[]{:S(2)}) collective-permute-start(f32[8,32,1024]{2,1,0:T(8,128)S(1)} %constant_dynamic-update-slice_fusion.2.refs_1_), channel_id=1, source_target_pairs={{0,28},{1,5},{4,0},{5,9},{8,4},{9,13},{12,8},{13,17},{16,12},{17,2... | collective-permute-start | bytes 3145736 | tf_op jit(solution)/shard_map/ppermute | solution.py:133
  56.4 1.0 copy-start
  71.1 9.8 %collective-permute-start.5 = (f32[16,32,1024]{2,1,0:T(8,128)S(1)}, f32[16,32,1024]{2,1,0:T(8,128)}, u32[]{:S(2)}, u32[]{:S(2)}) collective-permute-start(f32[16,32,1024]{2,1,0:T(8,128)S(1)} %bitcast.18), channel_id=1, source_target_pairs={{0,1},{1,0},{2,3},{3,2},{4,5},{5,4},{6,7},{7,6},{8,9},{9,8},{10,11... | collective-permute-start | bytes 6291464 | tf_op jit(solution)/shard_map/ppermute | solution.py:133
  80.9 1.2 copy-start.1
  89.5 18.7 %collective-permute-start.6 = (f32[8,16,1024]{2,1,0:T(8,128)S(1)}, f32[8,16,1024]{2,1,0:T(8,128)S(1)}, u32[]{:S(2)}, u32[]{:S(2)}) collective-permute-start(f32[8,16,1024]{2,1,0:T(8,128)S(1)} %get-tuple-element.16), channel_id=1, source_target_pairs={{0,4},{1,29},{4,8},{5,1},{8,12},{9,5},{12,16},{13,9},{16,20},{17,1... | collective-permute-start | bytes 1572872 | tf_op jit(solution)/shard_map/ppermute | solution.py:133
  130.1 6.9 %collective-permute-start.7 = (f32[1,128]{1,0:T(1,128)S(1)}, f32[1,128]{1,0:T(1,128)S(1)}, u32[]{:S(2)}, u32[]{:S(2)}) collective-permute-start(f32[1,128]{1,0:T(1,128)S(1)} %bitcast.25), channel_id=1, source_target_pairs={{0,1},{1,0},{2,3},{3,2},{4,5},{5,4},{6,7},{7,6},{8,9},{9,8},{10,11... | collective-permute-start | bytes 1544 | tf_op jit(solution)/shard_map/ppermute | solution.py:133

commit v4 on v3

v4 whole, which is shorter than its diff:
```python
import jax
import jax.numpy as jnp
from jax import lax
from jax.experimental import pallas as pl
from jax.experimental.pallas import tpu as pltpu
from jax.sharding import Mesh, PartitionSpec as P

AXES = ("x", "yh", "zh", "zl", "yl", "c")
SIZES = dict(zip(AXES, (4, 4, 4, 2, 2, 2)))
Y = ("yh", "yl")
Z = ("zh", "zl")
OWN = 16
WIDTH = 1024
LINE = 8
UNITS = 16
COUNT = LINE * 2 * OWN
DEPTH = UNITS * OWN
ROOT_WIDTH = 32.0
TOTAL = 8192.0
NT = (((1,), (1,)), ((), ()))
NN = (((1,), (0,)), ((), ()))
SMEM = pl.BlockSpec(memory_space=pltpu.SMEM)
VMEM = pl.BlockSpec(memory_space=pltpu.VMEM)
ANY = pl.BlockSpec(memory_space=pl.ANY)
PARAMS = pltpu.CompilerParams(vmem_limit_bytes=28 * 1024 * 1024)


def shape(*dims, dtype=jnp.float32):
    return jax.ShapeDtypeStruct(dims, dtype)


def cost(flops):
    return pl.CostEstimate(flops=flops, bytes_accessed=4_000_000, transcendentals=200_000)


def halves(value):
    high = value.astype(jnp.bfloat16)
    low = (value - high.astype(jnp.float32)).astype(jnp.bfloat16)
    return high, low


def product(left, right, dims):
    def dot(a, b):
        return lax.dot_general(a, b, dims, preferred_element_type=jnp.float32)

    return dot(left[0], right[0]) + (dot(left[0], right[1]) + dot(left[1], right[0]))


def flat(block):
    return block.reshape(block.shape[0] * block.shape[1], block.shape[2])


def started(copies):
    for copy in copies:
        copy.start()
    return copies


def row_copies(line_ref, near_ref, rows_buf, sems, kinds):
    return started(
        [
            pltpu.make_async_copy(
                ref.at[:, kind * OWN : (kind + 1) * OWN, :], rows_buf.at[kind, side], sems.at[2 * kind + side]
            )
            for kind in kinds
            for side, ref in enumerate((line_ref, near_ref))
        ]
    )


def col_copies(cols_ref, cols_buf, sems):
    return started(
        [
            pltpu.make_async_copy(cols_ref.at[:, kind * OWN : (kind + 1) * OWN, :], cols_buf.at[kind], sems.at[4 + kind])
            for kind in range(2)
        ]
    )


def sign(kind):
    return -1.0 if kind == 0 else 1.0


def pair_terms(line_ref, near_ref, cols_ref, rows_buf, cols_buf, sems, use):
    row_wait = row_copies(line_ref, near_ref, rows_buf, sems, range(2))
    col_wait = col_copies(cols_ref, cols_buf, sems)
    for copy in row_wait:
        copy.wait()
    rows = jnp.concatenate([flat(rows_buf[kind, side]) for kind in range(2) for side in range(2)], axis=0)
    rows_sq = jnp.sum(rows * rows, axis=1, keepdims=True)
    rows_hl = halves(rows)
    total = jnp.zeros((COUNT, 1), jnp.float32)
    energy = jnp.zeros((1, DEPTH), jnp.float32)
    for kind in range(2):
        col_wait[kind].wait()
        cols = flat(cols_buf[kind])
        cols_sq = jnp.sum(cols * cols, axis=1, keepdims=True)
        cols_sq = jnp.transpose(jnp.broadcast_to(cols_sq, (DEPTH, 128)))[0:1, :]
        cols_hl = halves(cols)
        used = COUNT if kind == 0 else 2 * COUNT
        inner = product((rows_hl[0][:used], rows_hl[1][:used]), cols_hl, NT)
        square = jnp.maximum(rows_sq[:used] + cols_sq - 2.0 * inner, 0.0) + 1.0
        inverse = lax.rsqrt(square)
        distance = square * inverse
        near = jnp.sum(distance[:COUNT], axis=0, keepdims=True)
        if kind == 0:
            energy = energy - near
        else:
            energy = energy + (2.0 * near - jnp.sum(distance[COUNT:], axis=0, keepdims=True))
        weight = (sign(kind) * ROOT_WIDTH / TOTAL) * inverse[:COUNT]
        total = total + jnp.sum(weight, axis=1, keepdims=True)
        use(kind, cols_hl, halves(weight))
    energy = jnp.sum(energy, axis=1, keepdims=True) / (TOTAL * TOTAL * ROOT_WIDTH)
    return total, energy


PAIR_SCRATCH = [
    pltpu.VMEM((2, 2, LINE, OWN, WIDTH), jnp.float32),
    pltpu.VMEM((2, UNITS, OWN, WIDTH), jnp.float32),
    pltpu.SemaphoreType.DMA((6,)),
]


def first_kernel(line_ref, near_ref, cols_ref, force_ref, total_ref, energy_ref, rows_buf, cols_buf, sems):
    force = []

    def use(kind, cols_hl, weight_hl):
        force.append(product(weight_hl, cols_hl, NN))

    total, energy = pair_terms(line_ref, near_ref, cols_ref, rows_buf, cols_buf, sems, use)
    force_ref[...] = force[0] + force[1]
    total_ref[...] = jnp.broadcast_to(total, total_ref.shape)
    energy_ref[...] = jnp.broadcast_to(energy, energy_ref.shape)


def first_pairs(line, near, cols):
    return pl.pallas_call(
        first_kernel,
        out_shape=(shape(COUNT, WIDTH), shape(COUNT, 128), shape(8, 128)),
        in_specs=[ANY] * 3,
        out_specs=[VMEM] * 3,
        scratch_shapes=PAIR_SCRATCH,
        compiler_params=PARAMS,
        cost_estimate=cost(2_000_000_000),
    )(line, near, cols)


def second_kernel(
    line_ref, near_ref, cols_ref, total_in, energy_in, high_ref, low_ref, total_ref, energy_ref, rows_buf, cols_buf, sems
):
    def use(kind, cols_hl, weight_hl):
        high_ref[kind], low_ref[kind] = weight_hl

    total, energy = pair_terms(line_ref, near_ref, cols_ref, rows_buf, cols_buf, sems, use)
    total_ref[...] = total_in[...] + total
    energy_ref[...] = energy_in[...] + energy


def second_pairs(line, near, cols, total, energy):
    weights = shape(2, COUNT, DEPTH, dtype=jnp.bfloat16)
    return pl.pallas_call(
        second_kernel,
        out_shape=(weights, weights, shape(COUNT, 128), shape(8, 128)),
        in_specs=[ANY] * 3 + [VMEM] * 2,
        out_specs=[VMEM] * 4,
        scratch_shapes=PAIR_SCRATCH,
        compiler_params=PARAMS,
        cost_estimate=cost(1_200_000_000),
    )(line, near, cols, total, energy)


def force_kernel(
    place_ref, line_ref, near_ref, cols_ref, high_ref, low_ref, total_ref, force_ref, mine_ref, away_ref, rows_buf, cols_buf, sems
):
    row_wait = row_copies(line_ref, near_ref, rows_buf, sems, range(1))
    col_wait = col_copies(cols_ref, cols_buf, sems)
    force = force_ref[...]
    for kind in range(2):
        col_wait[kind].wait()
        force = force + product((high_ref[kind], low_ref[kind]), halves(flat(cols_buf[kind])), NN)
    for copy in row_wait:
        copy.wait()
    for side, out_ref in enumerate((mine_ref, away_ref)):
        for member in range(LINE):
            at = (side * LINE + member) * OWN
            to = 2 * (member % 4) + place_ref[member // 4]
            total = total_ref[at : at + OWN, 0:1]
            out_ref[to] = total * rows_buf[0, side, member] - force[at : at + OWN]


def forces(place, line, near, cols, high, low, total, force):
    return pl.pallas_call(
        force_kernel,
        out_shape=(shape(LINE, OWN, WIDTH), shape(LINE, OWN, WIDTH)),
        in_specs=[SMEM] + [ANY] * 3 + [VMEM] * 4,
        out_specs=[VMEM] * 2,
        scratch_shapes=PAIR_SCRATCH,
        compiler_params=PARAMS,
        cost_estimate=cost(800_000_000),
    )(place, line, near, cols, high, low, total, force)


def spread_kernel(gen_ref, data_ref, own_ref, copies_ref):
    own_ref[:OWN], own_ref[OWN:] = gen_ref[...], data_ref[...]
    for peer in range(4):
        copies_ref[peer, :OWN], copies_ref[peer, OWN:] = gen_ref[...], data_ref[...]


def spread(generated, data):
    return pl.pallas_call(
        spread_kernel,
        out_shape=(shape(2 * OWN, WIDTH), shape(4, 2 * OWN, WIDTH)),
        in_specs=[VMEM] * 2,
        out_specs=[VMEM] * 2,
    )(generated, data)


def sent(value, axes, move):
    sizes = [SIZES[a] for a in axes]
    perm = []
    total = 1
    for s in sizes:
        total *= s
    for source in range(total):
        rest, place = source, []
        for s in reversed(sizes):
            place.insert(0, rest % s)
            rest //= s
        target = 0
        for s, p in zip(sizes, move(*place)):
            target = target * s + p % s
        perm.append((source, target))
    return lax.ppermute(value, axes, perm)


def exchanged(value, axes):
    return lax.all_to_all(value, axes, split_axis=0, concat_axis=0, tiled=True)


def swapped(value):
    return sent(value, ("c",), lambda c: (1 - c,))


def along(value, axes, steps):
    return sent(value, axes, lambda high, low: divmod((2 * high + low + steps) % 8, 2))


def shifted(value, axes, steps):
    def move(high, low, c):
        return (*divmod((2 * high + low + steps * (1 - 2 * c)) % 8, 2), c)

    return sent(value, (*axes, "c"), move)


def joined(*parts):
    return jnp.concatenate(parts, axis=0)


def body(generated, data):
    own, copies = spread(generated, data)
    line = exchanged(copies, ("yh",))
    parity = jnp.stack([own] + [along(own, Z, steps) for steps in (2, -2, 4)])
    parity, _ = lax.optimization_barrier((parity, line))
    cols = exchanged(jnp.broadcast_to(parity[None], (4,) + parity.shape), ("x",))
    line = joined(line, shifted(line, Y, -1))
    near = shifted(line, Z, -1)
    cols, near = lax.optimization_barrier((cols.reshape((UNITS,) + own.shape), near))
    other = swapped(cols)
    force, total, energy = first_pairs(line, near, cols)
    high, low, total, energy = second_pairs(line, near, other, total, energy)
    yl = lax.axis_index("yl")
    place = jnp.stack([yl, 1 - yl]).astype(jnp.int32)
    mine, away = forces(place, line, near, other, high, low, total, force)
    energy = jnp.broadcast_to(energy[None, :1], (32, 1, 128))
    energy = jnp.sum(exchanged(energy, ("x", "zh", "zl")), axis=0)
    mine = mine + shifted(away, Z, 1)
    loaded = jnp.concatenate([mine, jnp.broadcast_to(energy[None], (8, OWN, 128))], axis=2)
    loaded = exchanged(loaded, Y)
    force_rows = jnp.sum(loaded[:, :, :WIDTH], axis=0)
    energy = jnp.sum(loaded[:, :1, WIDTH:], axis=0)
    energy = energy + swapped(energy)
    return (force_rows, energy[0, 0])


def solution(mesh):
    fine = Mesh(mesh.devices.reshape(tuple(SIZES.values())), AXES)
    placed = P(AXES, None)
    return jax.shard_map(body, mesh=fine, in_specs=(placed, placed), out_specs=(placed, P()), check_vma=False)
```

time: 138 us -> 135 us (0.978)
  waiting for transfers between devices: 37.2 us -> 24.3 us
  Pallas kernels: 7.36 us -> 13.1 us
  starting transfers between devices: 47.6 us -> 49.9 us
  local copies, waits for them, and re-layouts: 7.51 us -> 9.67 us
    all_to_all x2, waiting for transfers between devices: 13.7 us -> 4.03 us  [exchanged(): return lax.all_to_all(value, axes, split_axis=0, concat_axis=0, tiled=True)]
    pallas_call x1 -> x4, Pallas kernels: 7.36 us -> 13.1 us  [the longest x1 4.92 us: first_pairs(): pl.pallas_call(first_kernel, out_shape=(shape(COUNT, WIDTH), shape(COUNT,...]
    ppermute x8, starting transfers between devices: 32.8 us -> 38.3 us  [sent(): return lax.ppermute(value, axes, perm)]
    unnamed x9 -> x13, local copies, waits for them, and re-layouts: 3.1 us -> 6.97 us
    all_to_all x2, starting transfers between devices: 14.9 us -> 11.7 us  [exchanged(): return lax.all_to_all(value, axes, split_axis=0, concat_axis=0, tiled=True)]
    ppermute x8, waiting for transfers between devices: 23.4 us -> 20.2 us  [sent(): return lax.ppermute(value, axes, perm)]
  transfers between devices with their start and end apart: 10 -> 10, of which waited for: 7 -> 4; matrix products, arithmetic and copies ran while one was open for 3% -> 4% of each run, Pallas kernels for 0% -> 4%
where the time goes in v4:
time: 135 us
  starting transfers between devices  49.9 us (37%)
  blocking collectives  33.5 us (25%)
  waiting for transfers between devices  24.3 us (18%)
  Pallas kernels  13.1 us (10%)
  local copies, waits for them, and re-layouts  9.67 us (7%)
  other arithmetic  3.38 us (3%)
    ppermute x8, starting transfers between devices, sent(): return lax.ppermute(value, axes, perm)  38.3 us
    all_to_all x2, blocking collectives, exchanged(): return lax.all_to_all(value, axes, split_axis=0, concat_axis=0, tiled=True)  33.5 us
    ppermute x8, waiting for transfers between devices, sent(): return lax.ppermute(value, axes, perm)  20.2 us
    all_to_all x2, starting transfers between devices, exchanged(): return lax.all_to_all(value, axes, split_axis=0, concat_axis=0, tiled=True)  11.7 us
    unnamed x13, local copies, waits for them, and re-layouts  6.97 us
    pallas_call x1, Pallas kernels, first_pairs(): pl.pallas_call(first_kernel, out_shape=(shape(COUNT, WIDTH), shape(COUNT,...  4.92 us
    all_to_all x2, waiting for transfers between devices, exchanged(): return lax.all_to_all(value, axes, split_axis=0, concat_axis=0, tiled=True)  4.03 us
    pallas_call x1, Pallas kernels, second_pairs(): pl.pallas_call(second_kernel, out_shape=(weights, weights, shape(COUNT, 1...  3.46 us
  transfers between devices with their start and end apart: 10, of which 4 were waited for; matrix products, arithmetic and copies ran while one was open for 4% of the time, Pallas kernels for 4%

profile of v4, /device:TPU:1, one launch (start us, length us, event | category | flops | bytes accessed | tf_op | source)
XLA Modules:
  0.0 134.6 jit_solution(13627331830875120594)
XLA Ops:
  0.6 1.8 %shard_map.41 = (f32[32,1024]{1,0:T(8,128)}, f32[4,32,1024]{2,1,0:T(8,128)}) custom-call(f32[16,1024]{1,0:T(8,128)} %gen_ref.1, f32[16,1024]{1,0:T(8,128)} %data_ref.1), custom_call_target="tpu_custom_call" | custom-call | tf_op jit(solution)/shard_map/pallas_call | solution.py:210
  2.4 7.6 %all-to-all-start = ((f32[4,32,1024]{2,1,0:T(8,128)}), f32[4,32,1024]{2,1,0:T(8,128)}, u32[]{:S(2)}, u32[]{:S(2)}) async-start(f32[4,32,1024]{2,1,0:T(8,128)} %get-tuple-element.16), calls=%async_computation | async-start | bytes 1048576 | tf_op jit(solution)/shard_map/all_to_all | solution.py:237
  10.0 10.6 %collective-permute-start.3 = (f32[32,1024]{1,0:T(8,128)}, f32[32,1024]{1,0:T(8,128)S(1)}, u32[]{:S(2)}, u32[]{:S(2)}) collective-permute-start(f32[32,1024]{1,0:T(8,128)} %get-tuple-element.17), channel_id=1, source_target_pairs={{0,16},{4,20},{8,24},{12,28},{16,0},{20,4},{24,8},{28,12},{1,17},{... | collective-permute-start | bytes 393224 | tf_op jit(solution)/shard_map/ppermute | solution.py:233
  20.7 1.9 %collective-permute-start.2 = (f32[32,1024]{1,0:T(8,128)}, f32[32,1024]{1,0:T(8,128)S(1)}, u32[]{:S(2)}, u32[]{:S(2)}) collective-permute-start(f32[32,1024]{1,0:T(8,128)} %get-tuple-element.17), channel_id=1, source_target_pairs={{0,24},{4,28},{8,0},{12,4},{16,8},{20,12},{24,16},{28,20},{1,25},{... | collective-permute-start | bytes 393224 | tf_op jit(solution)/shard_map/ppermute | solution.py:233
  22.6 4.2 %collective-permute-start.1 = (f32[32,1024]{1,0:T(8,128)}, f32[32,1024]{1,0:T(8,128)S(1)}, u32[]{:S(2)}, u32[]{:S(2)}) collective-permute-start(f32[32,1024]{1,0:T(8,128)} %get-tuple-element.17), channel_id=1, source_target_pairs={{0,8},{4,12},{8,16},{12,20},{16,24},{20,28},{24,0},{28,4},{1,9},{5... | collective-permute-start | bytes 393224 | tf_op jit(solution)/shard_map/ppermute | solution.py:233
  26.9 2.3 %collective-permute-start = (f32[4,32,1024]{2,1,0:T(8,128)}, f32[4,32,1024]{2,1,0:T(8,128)}, u32[]{:S(2)}, u32[]{:S(2)}) collective-permute-start(f32[4,32,1024]{2,1,0:T(8,128)} %all-to-all-done), channel_id=1, source_target_pairs={{0,98},{1,3},{2,0},{3,33},{32,2},{33,35},{34,32},{35,65},{64,34},{... | collective-permute-start | bytes 1572872 | tf_op jit(solution)/shard_map/ppermute | solution.py:233
  29.2 5.2 %collective-permute-done.2 = f32[32,1024]{1,0:T(8,128)S(1)} collective-permute-done((f32[32,1024]{1,0:T(8,128)}, f32[32,1024]{1,0:T(8,128)S(1)}, u32[]{:S(2)}, u32[]{:S(2)}) %collective-permute-start.2) | collective-permute-done | bytes 131104 | tf_op jit(solution)/shard_map/ppermute | solution.py:233
  34.4 0.9 pad_maximum_fusion.1
  35.4 1.6 %broadcast_in_dim.8 = f32[4,4,32,1024]{3,2,1,0:T(8,128)} broadcast(f32[4,32,1024]{2,1,0:T(8,128)S(1)} %pad_maximum_fusion.1), dimensions={1,2,3} | broadcast | bytes 2621440 | tf_op jit(solution)/shard_map/broadcast_in_dim | solution.py:264
  37.0 4.0 %all-to-all-start.1 = ((f32[4,4,32,1024]{3,2,1,0:T(8,128)}), f32[4,4,32,1024]{3,2,1,0:T(8,128)S(1)}, u32[]{:S(2)}, u32[]{:S(2)}) async-start(f32[4,4,32,1024]{3,2,1,0:T(8,128)} %broadcast_in_dim.8), calls=%async_computation.1 | async-start | bytes 4194304 | tf_op jit(solution)/shard_map/all_to_all | solution.py:237
  41.0 1.1 constant_dynamic-update-slice_fusion.1
  42.1 1.1 constant_dynamic-update-slice_fusion.line_ref
  43.1 3.5 %collective-permute-start.4 = (f32[8,32,1024]{2,1,0:T(8,128)S(1)}, f32[8,32,1024]{2,1,0:T(8,128)S(1)}, u32[]{:S(2)}, u32[]{:S(2)}) collective-permute-start(f32[8,32,1024]{2,1,0:T(8,128)S(1)} %constant_dynamic-update-slice_fusion.line_ref), channel_id=1, source_target_pairs={{0,28},{1,5},{4,0},{5,9},{8,4},{9,13},{12,8},{13,17},{16,12},{17,2... | collective-permute-start | bytes 3145736 | tf_op jit(solution)/shard_map/ppermute | solution.py:233
  46.7 14.9 %collective-permute-done.4.near_ref = f32[8,32,1024]{2,1,0:T(8,128)S(1)} collective-permute-done((f32[8,32,1024]{2,1,0:T(8,128)S(1)}, f32[8,32,1024]{2,1,0:T(8,128)S(1)}, u32[]{:S(2)}, u32[]{:S(2)}) %collective-permute-start.4) | collective-permute-done | bytes 1048608 | tf_op jit(solution)/shard_map/ppermute | solution.py:233
  61.6 1.0 copy-done.2
  62.5 4.0 %all-to-all-done.1 = f32[4,4,32,1024]{3,2,1,0:T(8,128)S(1)} async-done(((f32[4,4,32,1024]{3,2,1,0:T(8,128)}), f32[4,4,32,1024]{3,2,1,0:T(8,128)S(1)}, u32[]{:S(2)}, u32[]{:S(2)}) %all-to-all-start.1) | async-done | bytes 2097184 | tf_op jit(solution)/shard_map/all_to_all | solution.py:237
  66.6 1.3 copy-done
  67.9 3.6 %collective-permute-start.5 = (f32[16,32,1024]{2,1,0:T(8,128)}, f32[16,32,1024]{2,1,0:T(8,128)S(1)}, u32[]{:S(2)}, u32[]{:S(2)}) collective-permute-start(f32[16,32,1024]{2,1,0:T(8,128)} %bitcast.14), channel_id=1, source_target_pairs={{0,1},{1,0},{2,3},{3,2},{4,5},{5,4},{6,7},{7,6},{8,9},{9,8},{10,11... | collective-permute-start | bytes 6291464 | tf_op jit(solution)/shard_map/ppermute | solution.py:233
  71.6 1.6 %copy-done.1 = f32[4,4,32,1024]{3,2,1,0:T(8,128)S(1)} copy-done((f32[4,4,32,1024]{3,2,1,0:T(8,128)S(1)}, f32[4,4,32,1024]{3,2,1,0:T(8,128)}, u32[]{:S(2)}) %copy-start.1) | copy-done | bytes 2097176
  73.2 1.2 copy-done.3
  74.4 4.9 %shard_map.42 = (f32[256,1024]{1,0:T(8,128)S(1)}, f32[256,128]{1,0:T(8,128)S(1)}, f32[8,128]{1,0:T(8,128)S(1)}) custom-call(f32[8,32,1024]{2,1,0:T(8,128)S(1)} %constant_dynamic-update-slice_fusion.line_ref, f32[8,32,1024]{2,1,0:T(8,128)S(1)} %copy-done.3, f32[16,32,1024]{2,1,0:T(8,128)S(1)} %bitcast.15), custom_call_target="tpu_custom_call" | custom-call | flops 2000000000 | bytes 4000000 | tf_op jit(solution)/shard_map/pallas_call | solution.py:137
  79.3 3.5 %shard_map.43 = (bf16[2,256,256]{2,1,0:T(8,128)(2,1)S(1)}, bf16[2,256,256]{2,1,0:T(8,128)(2,1)S(1)}, f32[256,128]{1,0:T(8,128)S(1)}, f32[8,128]{1,0:T(8,128)S(1)}) custom-call(f32[8,32,1024]{2,1,0:T(8,128)S(1)} %constant_dynamic-update-slice_fusion.line_ref, f32[8,32,1024]{2,1,0:T(8,128)S(1)} %copy-done.3, ...), custom_call_target="tpu_custom_call" | custom-call | flops 1200000000 | bytes 4000000 | tf_op jit(solution)/shard_map/pallas_call | solution.py:161
  82.8 2.9 %shard_map.44 = (f32[8,16,1024]{2,1,0:T(8,128)S(1)}, f32[8,16,1024]{2,1,0:T(8,128)}) custom-call(s32[2]{0:T(128)S(1)} %pad_add_fusion.place_ref, f32[8,32,1024]{2,1,0:T(8,128)S(1)} %constant_dynamic-update-slice_fusion.line_ref, f32[8,32,1024]{2,1,0:T(8,128)S(1)} %copy-done.4, f32[16,32,1024]{2,1,0:T(8,128)S(1)} %collective-permute-done.5.cols_ref, ...), custom_call_target="tpu_custom_call" | custom-call | flops 800000000 | bytes 4000000 | tf_op jit(solution)/shard_map/pallas_call | solution.py:192
  85.8 0.8 copy-done.5
  86.5 5.9 %collective-permute-start.6 = (f32[8,16,1024]{2,1,0:T(8,128)}, f32[8,16,1024]{2,1,0:T(8,128)S(1)}, u32[]{:S(2)}, u32[]{:S(2)}) collective-permute-start(f32[8,16,1024]{2,1,0:T(8,128)} %get-tuple-element.28), channel_id=1, source_target_pairs={{0,4},{1,29},{4,8},{5,1},{8,12},{9,5},{12,16},{13,9},{16,20},{17,1... | collective-permute-start | bytes 1572872 | tf_op jit(solution)/shard_map/ppermute | solution.py:233
  92.5 11.6 %all_to_all.20 = f32[32,1,128]{2,1,0:T(1,128)S(1)} all-to-all(f32[32,1,128]{2,1,0:T(1,128)S(1)} %broadcast_in_dim.10), channel_id=1, replica_groups=mesh['x'=4,'yh'=4,'zh'=4,'zl'=2,'yl'=2,'c'=2] {'x','zh','zl'}, dimensions={0} | all-to-all | bytes 32768 | tf_op jit(solution)/shard_map/all_to_all | solution.py:237
  104.2 1.1 add.6
  105.3 21.9 %all_to_all.21 = f32[8,16,1152]{2,1,0:T(8,128)S(1)} all-to-all(f32[8,16,1152]{2,1,0:T(8,128)S(1)} %pad_maximum_fusion), channel_id=1, replica_groups=mesh['x'=4,'yh'=4,'zh'=4,'zl'=2,'yl'=2,'c'=2] {'yh','yl'}, dimensions={0} | all-to-all | bytes 1179648 | tf_op jit(solution)/shard_map/all_to_all | solution.py:237
  127.2 6.1 %collective-permute-start.7 = (f32[1,128]{1,0:T(1,128)S(1)}, f32[1,128]{1,0:T(1,128)S(1)}, u32[]{:S(2)}, u32[]{:S(2)}) collective-permute-start(f32[1,128]{1,0:T(1,128)S(1)} %bitcast.21), channel_id=1, source_target_pairs={{0,1},{1,0},{2,3},{3,2},{4,5},{5,4},{6,7},{7,6},{8,9},{9,8},{10,11... | collective-permute-start | bytes 1544 | tf_op jit(solution)/shard_map/ppermute | solution.py:233
  133.3 0.7 slice_reduce_fusion
  134.0 0.1 collective-permute-done.7
  134.1 0.5 bitcast_add_fusion
  (20 shorter events, 0.2 us)
Async XLA Ops:
  2.4 24.5 %all-to-all-start = ((f32[4,32,1024]{2,1,0:T(8,128)}), f32[4,32,1024]{2,1,0:T(8,128)}, u32[]{:S(2)}, u32[]{:S(2)}) async-start(f32[4,32,1024]{2,1,0:T(8,128)} %get-tuple-element.16), calls=%async_computation | async-start | bytes 1048576 | tf_op jit(solution)/shard_map/all_to_all | solution.py:237
  10.0 19.2 %collective-permute-start.3 = (f32[32,1024]{1,0:T(8,128)}, f32[32,1024]{1,0:T(8,128)S(1)}, u32[]{:S(2)}, u32[]{:S(2)}) collective-permute-start(f32[32,1024]{1,0:T(8,128)} %get-tuple-element.17), channel_id=1, source_target_pairs={{0,16},{4,20},{8,24},{12,28},{16,0},{20,4},{24,8},{28,12},{1,17},{... | collective-permute-start | bytes 393224 | tf_op jit(solution)/shard_map/ppermute | solution.py:233
  20.7 13.7 %collective-permute-start.2 = (f32[32,1024]{1,0:T(8,128)}, f32[32,1024]{1,0:T(8,128)S(1)}, u32[]{:S(2)}, u32[]{:S(2)}) collective-permute-start(f32[32,1024]{1,0:T(8,128)} %get-tuple-element.17), channel_id=1, source_target_pairs={{0,24},{4,28},{8,0},{12,4},{16,8},{20,12},{24,16},{28,20},{1,25},{... | collective-permute-start | bytes 393224 | tf_op jit(solution)/shard_map/ppermute | solution.py:233
  22.6 11.8 %collective-permute-start.1 = (f32[32,1024]{1,0:T(8,128)}, f32[32,1024]{1,0:T(8,128)S(1)}, u32[]{:S(2)}, u32[]{:S(2)}) collective-permute-start(f32[32,1024]{1,0:T(8,128)} %get-tuple-element.17), channel_id=1, source_target_pairs={{0,8},{4,12},{8,16},{12,20},{16,24},{20,28},{24,0},{28,4},{1,9},{5... | collective-permute-start | bytes 393224 | tf_op jit(solution)/shard_map/ppermute | solution.py:233
  26.9 15.2 %collective-permute-start = (f32[4,32,1024]{2,1,0:T(8,128)}, f32[4,32,1024]{2,1,0:T(8,128)}, u32[]{:S(2)}, u32[]{:S(2)}) collective-permute-start(f32[4,32,1024]{2,1,0:T(8,128)} %all-to-all-done), channel_id=1, source_target_pairs={{0,98},{1,3},{2,0},{3,33},{32,2},{33,35},{34,32},{35,65},{64,34},{... | collective-permute-start | bytes 1572872 | tf_op jit(solution)/shard_map/ppermute | solution.py:233
  37.0 29.6 %all-to-all-start.1 = ((f32[4,4,32,1024]{3,2,1,0:T(8,128)}), f32[4,4,32,1024]{3,2,1,0:T(8,128)S(1)}, u32[]{:S(2)}, u32[]{:S(2)}) async-start(f32[4,4,32,1024]{3,2,1,0:T(8,128)} %broadcast_in_dim.8), calls=%async_computation.1 | async-start | bytes 4194304 | tf_op jit(solution)/shard_map/all_to_all | solution.py:237
  43.1 18.4 %collective-permute-start.4 = (f32[8,32,1024]{2,1,0:T(8,128)S(1)}, f32[8,32,1024]{2,1,0:T(8,128)S(1)}, u32[]{:S(2)}, u32[]{:S(2)}) collective-permute-start(f32[8,32,1024]{2,1,0:T(8,128)S(1)} %constant_dynamic-update-slice_fusion.line_ref), channel_id=1, source_target_pairs={{0,28},{1,5},{4,0},{5,9},{8,4},{9,13},{12,8},{13,17},{16,12},{17,2... | collective-permute-start | bytes 3145736 | tf_op jit(solution)/shard_map/ppermute | solution.py:233
  61.6 1.0 copy-start.2
  66.6 1.3 copy-start
  67.9 11.4 %collective-permute-start.5 = (f32[16,32,1024]{2,1,0:T(8,128)}, f32[16,32,1024]{2,1,0:T(8,128)S(1)}, u32[]{:S(2)}, u32[]{:S(2)}) collective-permute-start(f32[16,32,1024]{2,1,0:T(8,128)} %bitcast.14), channel_id=1, source_target_pairs={{0,1},{1,0},{2,3},{3,2},{4,5},{5,4},{6,7},{7,6},{8,9},{9,8},{10,11... | collective-permute-start | bytes 6291464 | tf_op jit(solution)/shard_map/ppermute | solution.py:233
  71.6 1.6 %copy-start.1 = (f32[4,4,32,1024]{3,2,1,0:T(8,128)S(1)}, f32[4,4,32,1024]{3,2,1,0:T(8,128)}, u32[]{:S(2)}) copy-start(f32[4,4,32,1024]{3,2,1,0:T(8,128)} %copy-done) | copy-start | bytes 6291460
  73.2 1.2 copy-start.3
  79.3 3.5 %copy-start.4 = (f32[8,32,1024]{2,1,0:T(8,128)S(1)}, f32[8,32,1024]{2,1,0:T(8,128)}, u32[]{:S(2)}) copy-start(f32[8,32,1024]{2,1,0:T(8,128)} %copy-done.2) | copy-start | bytes 3145732
  85.7 0.8 copy-start.5
  86.5 17.6 %collective-permute-start.6 = (f32[8,16,1024]{2,1,0:T(8,128)}, f32[8,16,1024]{2,1,0:T(8,128)S(1)}, u32[]{:S(2)}, u32[]{:S(2)}) collective-permute-start(f32[8,16,1024]{2,1,0:T(8,128)} %get-tuple-element.28), channel_id=1, source_target_pairs={{0,4},{1,29},{4,8},{5,1},{8,12},{9,5},{12,16},{13,9},{16,20},{17,1... | collective-permute-start | bytes 1572872 | tf_op jit(solution)/shard_map/ppermute | solution.py:233
  127.2 6.9 %collective-permute-start.7 = (f32[1,128]{1,0:T(1,128)S(1)}, f32[1,128]{1,0:T(1,128)S(1)}, u32[]{:S(2)}, u32[]{:S(2)}) collective-permute-start(f32[1,128]{1,0:T(1,128)S(1)} %bitcast.21), channel_id=1, source_target_pairs={{0,1},{1,0},{2,3},{3,2},{4,5},{5,4},{6,7},{7,6},{8,9},{9,8},{10,11... | collective-permute-start | bytes 1544 | tf_op jit(solution)/shard_map/ppermute | solution.py:233

commit v5 on v3

v5 whole, which is shorter than its diff:
```python
import jax
import jax.numpy as jnp
from jax import lax
from jax.experimental import pallas as pl
from jax.experimental.pallas import tpu as pltpu
from jax.sharding import Mesh, PartitionSpec as P

AXES = ("x", "yh", "zh", "zl", "yl", "c")
SIZES = dict(zip(AXES, (4, 4, 4, 2, 2, 2)))
Y = ("yh", "yl")
Z = ("zh", "zl")
OWN = 16
WIDTH = 1024
LINE = 8
UNITS = 16
COUNT = LINE * 2 * OWN
DEPTH = UNITS * OWN
ROOT_WIDTH = 32.0
TOTAL = 8192.0
NT = (((1,), (1,)), ((), ()))
NN = (((1,), (0,)), ((), ()))
SMEM = pl.BlockSpec(memory_space=pltpu.SMEM)
VMEM = pl.BlockSpec(memory_space=pltpu.VMEM)
HBM = pl.BlockSpec(memory_space=pltpu.HBM)
STEPS = (0, 2, 6, 4)
PARAMS = pltpu.CompilerParams(vmem_limit_bytes=28 * 1024 * 1024)


def shape(*dims, dtype=jnp.float32):
    return jax.ShapeDtypeStruct(dims, dtype)


def cost(flops):
    return pl.CostEstimate(flops=flops, bytes_accessed=4_000_000, transcendentals=200_000)


def halves(value):
    high = value.astype(jnp.bfloat16)
    low = (value - high.astype(jnp.float32)).astype(jnp.bfloat16)
    return high, low


def product(left, right, dims):
    def dot(a, b):
        return lax.dot_general(a, b, dims, preferred_element_type=jnp.float32)

    return dot(left[0], right[0]) + (dot(left[0], right[1]) + dot(left[1], right[0]))


def flat(block):
    return block.reshape(block.shape[0] * block.shape[1], block.shape[2])


def sign(kind):
    return -1.0 if kind == 0 else 1.0


def pair_kernel(place_ref, line_ref, near_ref, cols_ref, other_ref, mine_ref, away_ref, energy_ref, rows_buf, cols_buf, sems):
    def by_kind(kind):
        return slice(kind * OWN, (kind + 1) * OWN)

    row_wait = [
        pltpu.make_async_copy(ref.at[:, by_kind(kind), :], rows_buf.at[kind, side], sems.at[2 * kind + side])
        for kind in range(2)
        for side, ref in enumerate((line_ref, near_ref))
    ]
    col_wait = [
        pltpu.make_async_copy(ref.at[:, by_kind(kind), :], cols_buf.at[kind, side], sems.at[4 + 2 * kind + side])
        for kind in range(2)
        for side, ref in enumerate((cols_ref, other_ref))
    ]
    for copy in row_wait + col_wait:
        copy.start()
    for copy in row_wait:
        copy.wait()
    row_gen = jnp.concatenate([flat(rows_buf[0, side]) for side in range(2)], axis=0)
    row_data = jnp.concatenate([flat(rows_buf[1, side]) for side in range(2)], axis=0)
    rows = jnp.concatenate([row_gen, row_data], axis=0)
    rows_sq = jnp.sum(rows * rows, axis=1, keepdims=True)
    rows_hl = halves(rows)
    total = jnp.zeros((COUNT, 1), jnp.float32)
    energy = jnp.zeros((1, DEPTH), jnp.float32)
    force = jnp.zeros((COUNT, WIDTH), jnp.float32)
    for kind in range(2):
        for side in range(2):
            col_wait[2 * kind + side].wait()
            cols = flat(cols_buf[kind, side])
            cols_sq = jnp.sum(cols * cols, axis=1, keepdims=True)
            cols_sq = jnp.transpose(jnp.broadcast_to(cols_sq, (DEPTH, 128)))[0:1, :]
            cols_hl = halves(cols)
            used = COUNT if kind == 0 else 2 * COUNT
            inner = product((rows_hl[0][:used], rows_hl[1][:used]), cols_hl, NT)
            square = jnp.maximum(rows_sq[:used] + cols_sq - 2.0 * inner, 0.0) + 1.0
            inverse = lax.rsqrt(square)
            distance = square * inverse
            near = jnp.sum(distance[:COUNT], axis=0, keepdims=True)
            if kind == 0:
                energy = energy - near
            else:
                energy = energy + (2.0 * near - jnp.sum(distance[COUNT:], axis=0, keepdims=True))
            weight = (sign(kind) * ROOT_WIDTH / TOTAL) * inverse[:COUNT]
            total = total + jnp.sum(weight, axis=1, keepdims=True)
            force = force + product(halves(weight), cols_hl, NN)
    force = total * row_gen - force
    for side, out_ref in enumerate((mine_ref, away_ref)):
        for member in range(LINE):
            at = (side * LINE + member) * OWN
            to = lax.rem(place_ref[member // len(STEPS)] + STEPS[member % len(STEPS)], LINE)
            out_ref[to] = force[at : at + OWN]
    energy = jnp.sum(energy, axis=1, keepdims=True) / (TOTAL * TOTAL * ROOT_WIDTH)
    energy_ref[...] = jnp.broadcast_to(energy, energy_ref.shape)


def pairs(place, line, near, cols, other):
    return pl.pallas_call(
        pair_kernel,
        out_shape=(shape(LINE, OWN, WIDTH), shape(LINE, OWN, WIDTH), shape(8, 128)),
        in_specs=[SMEM] + [HBM] * 4,
        out_specs=[VMEM] * 3,
        scratch_shapes=[
            pltpu.VMEM((2, 2, LINE, OWN, WIDTH), jnp.float32),
            pltpu.VMEM((2, 2, UNITS, OWN, WIDTH), jnp.float32),
            pltpu.SemaphoreType.DMA((8,)),
        ],
        compiler_params=PARAMS,
        cost_estimate=cost(4_000_000_000),
    )(place, line, near, cols, other)


def sent(value, axes, move):
    sizes = [SIZES[a] for a in axes]
    perm = []
    total = 1
    for s in sizes:
        total *= s
    for source in range(total):
        rest, place = source, []
        for s in reversed(sizes):
            place.insert(0, rest % s)
            rest //= s
        target = 0
        for s, p in zip(sizes, move(*place)):
            target = target * s + p % s
        perm.append((source, target))
    return lax.ppermute(value, axes, perm)


def exchanged(value, axes):
    return lax.all_to_all(value, axes, split_axis=0, concat_axis=0, tiled=True)


def swapped(value):
    return sent(value, ("c",), lambda c: (1 - c,))


def along(value, axes, steps):
    return sent(value, axes, lambda high, low: divmod((2 * high + low + steps) % 8, 2))


def shifted(value, axes, steps):
    def move(high, low, c):
        return (*divmod((2 * high + low + steps * (1 - 2 * c)) % 8, 2), c)

    return sent(value, (*axes, "c"), move)


def joined(*parts):
    return jnp.concatenate(parts, axis=0)


def body(generated, data):
    own = joined(generated, data)
    parity = jnp.stack([own] + [along(own, Z, steps) for steps in (2, -2, 4)])
    line = jnp.stack([own] + [along(own, Y, -steps) for steps in STEPS[1:]])
    cols = exchanged(jnp.broadcast_to(parity[None], (4,) + parity.shape), ("x",))
    line = joined(line, shifted(line, Y, -1))
    near = shifted(line, Z, -1)
    cols, near = lax.optimization_barrier((cols.reshape((UNITS,) + own.shape), near))
    y = 2 * lax.axis_index("yh") + lax.axis_index("yl")
    place = jnp.stack([y, y + 9 - 2 * lax.axis_index("c")]).astype(jnp.int32)
    mine, away, energy = pairs(place, line, near, cols, swapped(cols))
    energy = jnp.broadcast_to(energy[None, :1], (32, 1, 128))
    energy = jnp.sum(exchanged(energy, ("x", "zh", "zl")), axis=0)
    mine = mine + shifted(away, Z, 1)
    loaded = jnp.concatenate([mine, jnp.broadcast_to(energy[None], (8, OWN, 128))], axis=2)
    loaded = exchanged(loaded, Y)
    force_rows = jnp.sum(loaded[:, :, :WIDTH], axis=0)
    energy = jnp.sum(loaded[:, :1, WIDTH:], axis=0)
    energy = energy + swapped(energy)
    return (force_rows, energy[0, 0])


def solution(mesh):
    fine = Mesh(mesh.devices.reshape(tuple(SIZES.values())), AXES)
    placed = P(AXES, None)
    return jax.shard_map(body, mesh=fine, in_specs=(placed, placed), out_specs=(placed, P()), check_vma=False)
```

time: 138 us -> 143 us (1.036)
  waiting for transfers between devices: 37.2 us -> 23.9 us
  starting transfers between devices: 47.6 us -> 56.3 us
  blocking collectives: 34.7 us -> 40.4 us
  Pallas kernels: 7.36 us -> 10.2 us
    ppermute x8 -> x11, starting transfers between devices: 32.8 us -> 52.2 us  [sent(): return lax.ppermute(value, axes, perm)]
    all_to_all x2 -> x1, waiting for transfers between devices: 13.7 us -> 0.01 us  [exchanged(): return lax.all_to_all(value, axes, split_axis=0, concat_axis=0, tiled=True)]
    all_to_all x2 -> x1, starting transfers between devices: 14.9 us -> 4.01 us  [exchanged(): return lax.all_to_all(value, axes, split_axis=0, concat_axis=0, tiled=True)]
    all_to_all x2, blocking collectives: 34.7 us -> 40.4 us  [exchanged(): return lax.all_to_all(value, axes, split_axis=0, concat_axis=0, tiled=True)]
    pallas_call x1, Pallas kernels: 7.36 us -> 10.2 us  [pairs(): pl.pallas_call(pair_kernel, out_shape=(shape(LINE, OWN, WIDTH), shape(LIN...]
    unnamed x9 -> x13, local copies, waits for them, and re-layouts: 3.1 us -> 5.31 us
    ppermute x8 -> x11, waiting for transfers between devices: 23.4 us -> 23.9 us  [sent(): return lax.ppermute(value, axes, perm)]
  transfers between devices with their start and end apart: 10 -> 12, of which waited for: 7 -> 6; matrix products, arithmetic and copies ran while one was open for 3% -> 2% of each run, Pallas kernels for 0% -> 0%
where the time goes in v5:
time: 143 us
  starting transfers between devices  56.3 us (39%)
  blocking collectives  40.4 us (28%)
  waiting for transfers between devices  23.9 us (17%)
  Pallas kernels  10.2 us (7%)
  local copies, waits for them, and re-layouts  8.86 us (6%)
  other arithmetic  2.32 us (2%)
    ppermute x11, starting transfers between devices, sent(): return lax.ppermute(value, axes, perm)  52.2 us
    all_to_all x2, blocking collectives, exchanged(): return lax.all_to_all(value, axes, split_axis=0, concat_axis=0, tiled=True)  40.4 us
    ppermute x11, waiting for transfers between devices, sent(): return lax.ppermute(value, axes, perm)  23.9 us
    pallas_call x1, Pallas kernels, pairs(): pl.pallas_call(pair_kernel, out_shape=(shape(LINE, OWN, WIDTH), shape(LIN...  10.2 us
    unnamed x13, local copies, waits for them, and re-layouts  5.31 us
    all_to_all x1, starting transfers between devices, exchanged(): return lax.all_to_all(value, axes, split_axis=0, concat_axis=0, tiled=True)  4.01 us
  transfers between devices with their start and end apart: 12, of which 6 were waited for; matrix products, arithmetic and copies ran while one was open for 2% of the time, Pallas kernels for 0%

profile of v5, /device:TPU:1, one launch (start us, length us, event | category | flops | bytes accessed | tf_op | source)
XLA Modules:
  0.0 142.7 jit_solution(5606728909268517173)
XLA Ops:
  0.6 0.8 constant_dynamic-update-slice_fusion.1
  1.5 0.8 constant_dynamic-update-slice_fusion
  2.3 11.5 %collective-permute-start.6 = (f32[32,1024]{1,0:T(8,128)S(1)}, f32[32,1024]{1,0:T(8,128)S(1)}, u32[]{:S(2)}, u32[]{:S(2)}) collective-permute-start(f32[32,1024]{1,0:T(8,128)S(1)} %constant_dynamic-update-slice_fusion), channel_id=1, source_target_pairs={{0,16},{4,20},{8,24},{12,28},{16,0},{20,4},{24,8},{28,12},{1,17},{... | collective-permute-start | bytes 393224 | tf_op jit(solution)/shard_map/ppermute | solution.py:145
  13.8 1.9 %collective-permute-start.5 = (f32[32,1024]{1,0:T(8,128)S(1)}, f32[32,1024]{1,0:T(8,128)S(1)}, u32[]{:S(2)}, u32[]{:S(2)}) collective-permute-start(f32[32,1024]{1,0:T(8,128)S(1)} %constant_dynamic-update-slice_fusion), channel_id=1, source_target_pairs={{0,24},{4,28},{8,0},{12,4},{16,8},{20,12},{24,16},{28,20},{1,25},{... | collective-permute-start | bytes 393224 | tf_op jit(solution)/shard_map/ppermute | solution.py:145
  15.7 4.2 %collective-permute-start.4 = (f32[32,1024]{1,0:T(8,128)S(1)}, f32[32,1024]{1,0:T(8,128)S(1)}, u32[]{:S(2)}, u32[]{:S(2)}) collective-permute-start(f32[32,1024]{1,0:T(8,128)S(1)} %constant_dynamic-update-slice_fusion), channel_id=1, source_target_pairs={{0,8},{4,12},{8,16},{12,20},{16,24},{20,28},{24,0},{28,4},{1,9},{5... | collective-permute-start | bytes 393224 | tf_op jit(solution)/shard_map/ppermute | solution.py:145
  20.0 7.5 %collective-permute-start.2 = (f32[32,1024]{1,0:T(8,128)S(1)}, f32[32,1024]{1,0:T(8,128)S(1)}, u32[]{:S(2)}, u32[]{:S(2)}) collective-permute-start(f32[32,1024]{1,0:T(8,128)S(1)} %constant_dynamic-update-slice_fusion), channel_id=1, source_target_pairs={{0,64},{2,66},{32,96},{34,98},{64,0},{66,2},{96,32},{98,34},{1,65}... | collective-permute-start | bytes 393224 | tf_op jit(solution)/shard_map/ppermute | solution.py:145
  27.4 2.4 %collective-permute-start.1 = (f32[32,1024]{1,0:T(8,128)S(1)}, f32[32,1024]{1,0:T(8,128)S(1)}, u32[]{:S(2)}, u32[]{:S(2)}) collective-permute-start(f32[32,1024]{1,0:T(8,128)S(1)} %constant_dynamic-update-slice_fusion), channel_id=1, source_target_pairs={{0,32},{2,34},{32,64},{34,66},{64,96},{66,98},{96,0},{98,2},{1,33}... | collective-permute-start | bytes 393224 | tf_op jit(solution)/shard_map/ppermute | solution.py:145
  29.9 5.0 %collective-permute-start = (f32[32,1024]{1,0:T(8,128)S(1)}, f32[32,1024]{1,0:T(8,128)S(1)}, u32[]{:S(2)}, u32[]{:S(2)}) collective-permute-start(f32[32,1024]{1,0:T(8,128)S(1)} %constant_dynamic-update-slice_fusion), channel_id=1, source_target_pairs={{0,96},{2,98},{32,0},{34,2},{64,32},{66,34},{96,64},{98,66},{1,97}... | collective-permute-start | bytes 393224 | tf_op jit(solution)/shard_map/ppermute | solution.py:145
  34.9 1.1 collective-permute-done.1
  36.0 2.7 %collective-permute-done = f32[32,1024]{1,0:T(8,128)S(1)} collective-permute-done((f32[32,1024]{1,0:T(8,128)S(1)}, f32[32,1024]{1,0:T(8,128)S(1)}, u32[]{:S(2)}, u32[]{:S(2)}) %collective-permute-start) | collective-permute-done | bytes 131104 | tf_op jit(solution)/shard_map/ppermute | solution.py:145
  38.7 0.9 fusion.3
  39.6 4.2 %collective-permute-start.3 = (f32[4,32,1024]{2,1,0:T(8,128)}, f32[4,32,1024]{2,1,0:T(8,128)}, u32[]{:S(2)}, u32[]{:S(2)}) collective-permute-start(f32[4,32,1024]{2,1,0:T(8,128)} %get-tuple-element.13), channel_id=1, source_target_pairs={{0,98},{1,3},{2,0},{3,33},{32,2},{33,35},{34,32},{35,65},{64,34},{... | collective-permute-start | bytes 1572872 | tf_op jit(solution)/shard_map/ppermute | solution.py:145
  43.9 1.6 %broadcast_in_dim.8 = f32[4,4,32,1024]{3,2,1,0:T(8,128)} broadcast(f32[4,32,1024]{2,1,0:T(8,128)S(1)} %get-tuple-element.12), dimensions={1,2,3} | broadcast | bytes 2621440 | tf_op jit(solution)/shard_map/broadcast_in_dim | solution.py:175
  45.5 4.0 %all-to-all-start = ((f32[4,4,32,1024]{3,2,1,0:T(8,128)}), f32[4,4,32,1024]{3,2,1,0:T(8,128)S(1)}, u32[]{:S(2)}, u32[]{:S(2)}) async-start(f32[4,4,32,1024]{3,2,1,0:T(8,128)} %broadcast_in_dim.8), calls=%async_computation | async-start | bytes 4194304 | tf_op jit(solution)/shard_map/all_to_all | solution.py:149
  49.5 3.1 %collective-permute-done.3 = f32[4,32,1024]{2,1,0:T(8,128)} collective-permute-done((f32[4,32,1024]{2,1,0:T(8,128)}, f32[4,32,1024]{2,1,0:T(8,128)}, u32[]{:S(2)}, u32[]{:S(2)}) %collective-permute-start.3) | collective-permute-done | bytes 524320 | tf_op jit(solution)/shard_map/ppermute | solution.py:145
  52.7 1.1 constant_dynamic-update-slice_fusion.2.line_ref
  53.8 3.1 %collective-permute-start.7 = (f32[8,32,1024]{2,1,0:T(8,128)S(1)}, f32[8,32,1024]{2,1,0:T(8,128)S(1)}, u32[]{:S(2)}, u32[]{:S(2)}) collective-permute-start(f32[8,32,1024]{2,1,0:T(8,128)S(1)} %constant_dynamic-update-slice_fusion.2.line_ref), channel_id=1, source_target_pairs={{0,28},{1,5},{4,0},{5,9},{8,4},{9,13},{12,8},{13,17},{16,12},{17,2... | collective-permute-start | bytes 3145736 | tf_op jit(solution)/shard_map/ppermute | solution.py:145
  56.9 1.0 copy-done
  57.9 12.9 %collective-permute-done.7.near_ref = f32[8,32,1024]{2,1,0:T(8,128)S(1)} collective-permute-done((f32[8,32,1024]{2,1,0:T(8,128)S(1)}, f32[8,32,1024]{2,1,0:T(8,128)S(1)}, u32[]{:S(2)}, u32[]{:S(2)}) %collective-permute-start.7) | collective-permute-done | bytes 1048608 | tf_op jit(solution)/shard_map/ppermute | solution.py:145
  70.8 1.0 copy-done.2
  71.8 6.9 %collective-permute-start.8 = (f32[16,32,1024]{2,1,0:T(8,128)S(1)}, f32[16,32,1024]{2,1,0:T(8,128)}, u32[]{:S(2)}, u32[]{:S(2)}) collective-permute-start(f32[16,32,1024]{2,1,0:T(8,128)S(1)} %bitcast.21), channel_id=1, source_target_pairs={{0,1},{1,0},{2,3},{3,2},{4,5},{5,4},{6,7},{7,6},{8,9},{9,8},{10,11... | collective-permute-start | bytes 6291464 | tf_op jit(solution)/shard_map/ppermute | solution.py:145
  78.8 3.8 %collective-permute-done.8.other_ref = f32[16,32,1024]{2,1,0:T(8,128)} collective-permute-done((f32[16,32,1024]{2,1,0:T(8,128)S(1)}, f32[16,32,1024]{2,1,0:T(8,128)}, u32[]{:S(2)}, u32[]{:S(2)}) %collective-permute-start.8) | collective-permute-done | bytes 2097184 | tf_op jit(solution)/shard_map/ppermute | solution.py:145
  82.6 1.2 copy-done.1
  83.8 1.2 copy-done.3
  85.0 10.2 %shard_map.41 = (f32[8,16,1024]{2,1,0:T(8,128)S(1)}, f32[8,16,1024]{2,1,0:T(8,128)S(1)}, f32[8,128]{1,0:T(8,128)S(1)}) custom-call(s32[2]{0:T(128)S(1)} %pad_add_fusion.place_ref, f32[8,32,1024]{2,1,0:T(8,128)S(1)} %copy-done.1, f32[8,32,1024]{2,1,0:T(8,128)S(1)} %copy-done.3, f32[16,32,1024]{2,1,0:T(8,128)S(1)} %bitcast.22, ...), custom_call_target="tpu_custom_call" | custom-call | flops 4000000000 | bytes 4000000 | tf_op jit(solution)/shard_map/pallas_call | solution.py:115
  95.2 3.2 %collective-permute-start.9 = (f32[8,16,1024]{2,1,0:T(8,128)S(1)}, f32[8,16,1024]{2,1,0:T(8,128)S(1)}, u32[]{:S(2)}, u32[]{:S(2)}) collective-permute-start(f32[8,16,1024]{2,1,0:T(8,128)S(1)} %get-tuple-element.10), channel_id=1, source_target_pairs={{0,4},{1,29},{4,8},{5,1},{8,12},{9,5},{12,16},{13,9},{16,20},{17,1... | collective-permute-start | bytes 1572872 | tf_op jit(solution)/shard_map/ppermute | solution.py:145
  98.5 16.0 %all_to_all.15 = f32[32,1,128]{2,1,0:T(1,128)S(1)} all-to-all(f32[32,1,128]{2,1,0:T(1,128)S(1)} %broadcast_in_dim.10), channel_id=1, replica_groups=mesh['x'=4,'yh'=4,'zh'=4,'zl'=2,'yl'=2,'c'=2] {'x','zh','zl'}, dimensions={0} | all-to-all | bytes 32768 | tf_op jit(solution)/shard_map/all_to_all | solution.py:149
  114.7 24.4 %all_to_all.16 = f32[8,16,1152]{2,1,0:T(8,128)S(1)} all-to-all(f32[8,16,1152]{2,1,0:T(8,128)S(1)} %pad_maximum_fusion.2), channel_id=1, replica_groups=mesh['x'=4,'yh'=4,'zh'=4,'zl'=2,'yl'=2,'c'=2] {'yh','yl'}, dimensions={0} | all-to-all | bytes 1179648 | tf_op jit(solution)/shard_map/all_to_all | solution.py:149
  139.0 2.4 %collective-permute-start.10 = (f32[1,128]{1,0:T(1,128)S(1)}, f32[1,128]{1,0:T(1,128)S(1)}, u32[]{:S(2)}, u32[]{:S(2)}) collective-permute-start(f32[1,128]{1,0:T(1,128)S(1)} %bitcast.31), channel_id=1, source_target_pairs={{0,1},{1,0},{2,3},{3,2},{4,5},{5,4},{6,7},{7,6},{8,9},{9,8},{10,11... | collective-permute-start | bytes 1544 | tf_op jit(solution)/shard_map/ppermute | solution.py:145
  141.4 0.7 slice_reduce_fusion
  142.1 0.1 collective-permute-done.10
  142.2 0.5 bitcast_add_fusion
  (22 shorter events, 0.3 us)
Async XLA Ops:
  2.3 27.6 %collective-permute-start.6 = (f32[32,1024]{1,0:T(8,128)S(1)}, f32[32,1024]{1,0:T(8,128)S(1)}, u32[]{:S(2)}, u32[]{:S(2)}) collective-permute-start(f32[32,1024]{1,0:T(8,128)S(1)} %constant_dynamic-update-slice_fusion), channel_id=1, source_target_pairs={{0,16},{4,20},{8,24},{12,28},{16,0},{20,4},{24,8},{28,12},{1,17},{... | collective-permute-start | bytes 393224 | tf_op jit(solution)/shard_map/ppermute | solution.py:145
  13.8 21.1 %collective-permute-start.5 = (f32[32,1024]{1,0:T(8,128)S(1)}, f32[32,1024]{1,0:T(8,128)S(1)}, u32[]{:S(2)}, u32[]{:S(2)}) collective-permute-start(f32[32,1024]{1,0:T(8,128)S(1)} %constant_dynamic-update-slice_fusion), channel_id=1, source_target_pairs={{0,24},{4,28},{8,0},{12,4},{16,8},{20,12},{24,16},{28,20},{1,25},{... | collective-permute-start | bytes 393224 | tf_op jit(solution)/shard_map/ppermute | solution.py:145
  15.7 19.2 %collective-permute-start.4 = (f32[32,1024]{1,0:T(8,128)S(1)}, f32[32,1024]{1,0:T(8,128)S(1)}, u32[]{:S(2)}, u32[]{:S(2)}) collective-permute-start(f32[32,1024]{1,0:T(8,128)S(1)} %constant_dynamic-update-slice_fusion), channel_id=1, source_target_pairs={{0,8},{4,12},{8,16},{12,20},{16,24},{20,28},{24,0},{28,4},{1,9},{5... | collective-permute-start | bytes 393224 | tf_op jit(solution)/shard_map/ppermute | solution.py:145
  20.0 14.9 %collective-permute-start.2 = (f32[32,1024]{1,0:T(8,128)S(1)}, f32[32,1024]{1,0:T(8,128)S(1)}, u32[]{:S(2)}, u32[]{:S(2)}) collective-permute-start(f32[32,1024]{1,0:T(8,128)S(1)} %constant_dynamic-update-slice_fusion), channel_id=1, source_target_pairs={{0,64},{2,66},{32,96},{34,98},{64,0},{66,2},{96,32},{98,34},{1,65}... | collective-permute-start | bytes 393224 | tf_op jit(solution)/shard_map/ppermute | solution.py:145
  27.4 8.6 %collective-permute-start.1 = (f32[32,1024]{1,0:T(8,128)S(1)}, f32[32,1024]{1,0:T(8,128)S(1)}, u32[]{:S(2)}, u32[]{:S(2)}) collective-permute-start(f32[32,1024]{1,0:T(8,128)S(1)} %constant_dynamic-update-slice_fusion), channel_id=1, source_target_pairs={{0,32},{2,34},{32,64},{34,66},{64,96},{66,98},{96,0},{98,2},{1,33}... | collective-permute-start | bytes 393224 | tf_op jit(solution)/shard_map/ppermute | solution.py:145
  29.9 8.8 %collective-permute-start = (f32[32,1024]{1,0:T(8,128)S(1)}, f32[32,1024]{1,0:T(8,128)S(1)}, u32[]{:S(2)}, u32[]{:S(2)}) collective-permute-start(f32[32,1024]{1,0:T(8,128)S(1)} %constant_dynamic-update-slice_fusion), channel_id=1, source_target_pairs={{0,96},{2,98},{32,0},{34,2},{64,32},{66,34},{96,64},{98,66},{1,97}... | collective-permute-start | bytes 393224 | tf_op jit(solution)/shard_map/ppermute | solution.py:145
  39.6 13.0 %collective-permute-start.3 = (f32[4,32,1024]{2,1,0:T(8,128)}, f32[4,32,1024]{2,1,0:T(8,128)}, u32[]{:S(2)}, u32[]{:S(2)}) collective-permute-start(f32[4,32,1024]{2,1,0:T(8,128)} %get-tuple-element.13), channel_id=1, source_target_pairs={{0,98},{1,3},{2,0},{3,33},{32,2},{33,35},{34,32},{35,65},{64,34},{... | collective-permute-start | bytes 1572872 | tf_op jit(solution)/shard_map/ppermute | solution.py:145
  45.5 26.3 %all-to-all-start = ((f32[4,4,32,1024]{3,2,1,0:T(8,128)}), f32[4,4,32,1024]{3,2,1,0:T(8,128)S(1)}, u32[]{:S(2)}, u32[]{:S(2)}) async-start(f32[4,4,32,1024]{3,2,1,0:T(8,128)} %broadcast_in_dim.8), calls=%async_computation | async-start | bytes 4194304 | tf_op jit(solution)/shard_map/all_to_all | solution.py:149
  53.8 17.0 %collective-permute-start.7 = (f32[8,32,1024]{2,1,0:T(8,128)S(1)}, f32[8,32,1024]{2,1,0:T(8,128)S(1)}, u32[]{:S(2)}, u32[]{:S(2)}) collective-permute-start(f32[8,32,1024]{2,1,0:T(8,128)S(1)} %constant_dynamic-update-slice_fusion.2.line_ref), channel_id=1, source_target_pairs={{0,28},{1,5},{4,0},{5,9},{8,4},{9,13},{12,8},{13,17},{16,12},{17,2... | collective-permute-start | bytes 3145736 | tf_op jit(solution)/shard_map/ppermute | solution.py:145
  56.9 1.0 copy-start
  70.8 1.0 copy-start.2
  71.8 10.8 %collective-permute-start.8 = (f32[16,32,1024]{2,1,0:T(8,128)S(1)}, f32[16,32,1024]{2,1,0:T(8,128)}, u32[]{:S(2)}, u32[]{:S(2)}) collective-permute-start(f32[16,32,1024]{2,1,0:T(8,128)S(1)} %bitcast.21), channel_id=1, source_target_pairs={{0,1},{1,0},{2,3},{3,2},{4,5},{5,4},{6,7},{7,6},{8,9},{9,8},{10,11... | collective-permute-start | bytes 6291464 | tf_op jit(solution)/shard_map/ppermute | solution.py:145
  82.6 1.2 copy-start.1
  83.8 1.2 copy-start.3
  95.2 19.3 %collective-permute-start.9 = (f32[8,16,1024]{2,1,0:T(8,128)S(1)}, f32[8,16,1024]{2,1,0:T(8,128)S(1)}, u32[]{:S(2)}, u32[]{:S(2)}) collective-permute-start(f32[8,16,1024]{2,1,0:T(8,128)S(1)} %get-tuple-element.10), channel_id=1, source_target_pairs={{0,4},{1,29},{4,8},{5,1},{8,12},{9,5},{12,16},{13,9},{16,20},{17,1... | collective-permute-start | bytes 1572872 | tf_op jit(solution)/shard_map/ppermute | solution.py:145
  139.0 3.2 %collective-permute-start.10 = (f32[1,128]{1,0:T(1,128)S(1)}, f32[1,128]{1,0:T(1,128)S(1)}, u32[]{:S(2)}, u32[]{:S(2)}) collective-permute-start(f32[1,128]{1,0:T(1,128)S(1)} %bitcast.31), channel_id=1, source_target_pairs={{0,1},{1,0},{2,3},{3,2},{4,5},{5,4},{6,7},{7,6},{8,9},{9,8},{10,11... | collective-permute-start | bytes 1544 | tf_op jit(solution)/shard_map/ppermute | solution.py:145

commit v6 on v5

v6 whole, which is shorter than its diff:
```python
import jax
import jax.numpy as jnp
from jax import lax
from jax.experimental import pallas as pl
from jax.experimental.pallas import tpu as pltpu
from jax.sharding import Mesh, PartitionSpec as P

AXES = ("x", "yh", "zh", "zl", "yl", "c")
SIZES = dict(zip(AXES, (4, 4, 4, 2, 2, 2)))
Y = ("yh", "yl")
Z = ("zh", "zl")
OWN = 16
WIDTH = 1024
LINE = 8
UNITS = 16
COUNT = LINE * 4 * OWN
DEPTH = UNITS * OWN
ROOT_WIDTH = 32.0
TOTAL = 8192.0
NT = (((1,), (1,)), ((), ()))
NN = (((1,), (0,)), ((), ()))
SMEM = pl.BlockSpec(memory_space=pltpu.SMEM)
VMEM = pl.BlockSpec(memory_space=pltpu.VMEM)
PARAMS = pltpu.CompilerParams(vmem_limit_bytes=28 * 1024 * 1024)


def shape(*dims, dtype=jnp.float32):
    return jax.ShapeDtypeStruct(dims, dtype)


def cost(flops):
    return pl.CostEstimate(flops=flops, bytes_accessed=4_000_000, transcendentals=200_000)


def halves(value):
    high = value.astype(jnp.bfloat16)
    low = (value - high.astype(jnp.float32)).astype(jnp.bfloat16)
    return high, low


def product(left, right, dims):
    def dot(a, b):
        return lax.dot_general(a, b, dims, preferred_element_type=jnp.float32)

    return dot(left[0], right[0]) + (dot(left[0], right[1]) + dot(left[1], right[0]))


def flat(block):
    return block.reshape(block.shape[0] * block.shape[1], block.shape[2])


def sign(kind):
    return -1.0 if kind == 0 else 1.0


def pair_kernel(place_ref, *refs):
    row_refs, (cols_ref, mine_ref, away_ref, back_ref, energy_ref) = refs[:4], refs[4:]

    def rows_of(kind):
        return jnp.concatenate([flat(ref[:, kind * OWN : (kind + 1) * OWN, :]) for ref in row_refs], axis=0)

    row_gen = rows_of(0)
    rows = jnp.concatenate([row_gen, rows_of(1)], axis=0)
    rows_sq = jnp.sum(rows * rows, axis=1, keepdims=True)
    rows_hl = halves(rows)
    total = jnp.zeros((COUNT, 1), jnp.float32)
    energy = jnp.zeros((1, DEPTH), jnp.float32)
    force = jnp.zeros((COUNT, WIDTH), jnp.float32)
    for kind in range(2):
        cols = flat(cols_ref[:, kind * OWN : (kind + 1) * OWN, :])
        cols_sq = jnp.sum(cols * cols, axis=1, keepdims=True)
        cols_sq = jnp.transpose(jnp.broadcast_to(cols_sq, (DEPTH, 128)))[0:1, :]
        cols_hl = halves(cols)
        used = COUNT if kind == 0 else 2 * COUNT
        inner = product((rows_hl[0][:used], rows_hl[1][:used]), cols_hl, NT)
        square = jnp.maximum(rows_sq[:used] + cols_sq - 2.0 * inner, 0.0) + 1.0
        inverse = lax.rsqrt(square)
        distance = square * inverse
        near = jnp.sum(distance[:COUNT], axis=0, keepdims=True)
        if kind == 0:
            energy = energy - near
        else:
            energy = energy + (2.0 * near - jnp.sum(distance[COUNT:], axis=0, keepdims=True))
        weight = (sign(kind) * ROOT_WIDTH / TOTAL) * inverse[:COUNT]
        total = total + jnp.sum(weight, axis=1, keepdims=True)
        force = force + product(halves(weight), cols_hl, NN)
    force = total * row_gen - force
    outs = (mine_ref, away_ref, back_ref.at[0], back_ref.at[1])
    for group, out_ref in enumerate(outs):
        for member in range(LINE):
            at = (group * LINE + member) * OWN
            to = 2 * (member % 4) + place_ref[member // 4]
            out_ref[to] = force[at : at + OWN]
    energy = jnp.sum(energy, axis=1, keepdims=True) / (TOTAL * TOTAL * ROOT_WIDTH)
    energy_ref[...] = jnp.broadcast_to(energy, energy_ref.shape)


def pairs(place, rows, cols):
    part = shape(LINE, OWN, WIDTH)
    return pl.pallas_call(
        pair_kernel,
        out_shape=(part, part, shape(2, LINE, OWN, WIDTH), shape(8, 128)),
        in_specs=[SMEM] + [VMEM] * 5,
        out_specs=[VMEM] * 4,
        compiler_params=PARAMS,
        cost_estimate=cost(4_000_000_000),
    )(place, *rows, cols)


def spread_kernel(gen_ref, data_ref, own_ref, copies_ref):
    own_ref[:OWN], own_ref[OWN:] = gen_ref[...], data_ref[...]
    for peer in range(4):
        copies_ref[peer, :OWN], copies_ref[peer, OWN:] = gen_ref[...], data_ref[...]


def spread(generated, data):
    return pl.pallas_call(
        spread_kernel,
        out_shape=(shape(2 * OWN, WIDTH), shape(4, 2 * OWN, WIDTH)),
        in_specs=[VMEM] * 2,
        out_specs=[VMEM] * 2,
    )(generated, data)


def sent(value, axes, move):
    sizes = [SIZES[a] for a in axes]
    perm = []
    total = 1
    for s in sizes:
        total *= s
    for source in range(total):
        rest, place = source, []
        for s in reversed(sizes):
            place.insert(0, rest % s)
            rest //= s
        target = 0
        for s, p in zip(sizes, move(*place)):
            target = target * s + p % s
        perm.append((source, target))
    return lax.ppermute(value, axes, perm)


def exchanged(value, axes):
    return lax.all_to_all(value, axes, split_axis=0, concat_axis=0, tiled=True)


def swapped(value):
    return sent(value, ("c",), lambda c: (1 - c,))


def along(value, axes, steps):
    return sent(value, axes, lambda high, low: divmod((2 * high + low + steps) % 8, 2))


def shifted(value, axes, steps):
    def move(high, low, c):
        return (*divmod((2 * high + low + steps * (1 - 2 * c)) % 8, 2), c)

    return sent(value, (*axes, "c"), move)


def joined(*parts):
    return jnp.concatenate(parts, axis=0)


def body(generated, data):
    own, copies = spread(generated, data)
    line = exchanged(copies, ("yh",))
    parity = jnp.stack([own] + [along(own, Z, steps) for steps in (2, -2, 4)])
    parity, _ = lax.optimization_barrier((parity, line))
    cols = exchanged(jnp.broadcast_to(parity[None], (4,) + parity.shape), ("x",))
    line = joined(line, shifted(line, Y, -1))
    near = shifted(line, Z, -1)
    line_away = swapped(line)
    cols, near = lax.optimization_barrier((cols.reshape((UNITS,) + own.shape), near))
    yl = lax.axis_index("yl")
    place = jnp.stack([yl, 1 - yl]).astype(jnp.int32)
    mine, away, back, energy = pairs(place, (line, near, line_away, swapped(near)), cols)
    energy = jnp.broadcast_to(energy[None, :1], (64, 1, 128))
    energy = jnp.sum(exchanged(energy, ("x", "zh", "zl", "c")), axis=0)
    back = swapped(back)
    mine = mine + back[0] + shifted(away + back[1], Z, 1)
    loaded = jnp.concatenate([mine, jnp.broadcast_to(energy[None], (LINE, OWN, 128))], axis=2)
    loaded = exchanged(loaded, Y)
    force_rows = jnp.sum(loaded[:, :, :WIDTH], axis=0)
    energy = jnp.sum(loaded[:, 0, WIDTH:], axis=0)
    return (force_rows, energy[0])


def solution(mesh):
    fine = Mesh(mesh.devices.reshape(tuple(SIZES.values())), AXES)
    placed = P(AXES, None)
    return jax.shard_map(body, mesh=fine, in_specs=(placed, placed), out_specs=(placed, P()), check_vma=False)
```

time: 143 us -> 132 us (0.923)
  starting transfers between devices: 56.3 us -> 51.6 us
  blocking collectives: 40.4 us -> 37.4 us
  local copies, waits for them, and re-layouts: 8.86 us -> 5.98 us
    ppermute x11 -> x9, starting transfers between devices: 52.2 us -> 40 us  [sent(): return lax.ppermute(value, axes, perm)]
    all_to_all x1 -> x2, starting transfers between devices: 4.01 us -> 11.7 us  [exchanged(): return lax.all_to_all(value, axes, split_axis=0, concat_axis=0, tiled=True)]
    ppermute x11 -> x9, waiting for transfers between devices: 23.9 us -> 18.4 us  [sent(): return lax.ppermute(value, axes, perm)]
    all_to_all x1 -> x2, waiting for transfers between devices: 0.01 us -> 5 us  [exchanged(): return lax.all_to_all(value, axes, split_axis=0, concat_axis=0, tiled=True)]
    all_to_all x2, blocking collectives: 40.4 us -> 37.4 us  [exchanged(): return lax.all_to_all(value, axes, split_axis=0, concat_axis=0, tiled=True)]
    unnamed x13 -> x5, local copies, waits for them, and re-layouts: 5.31 us -> 3.26 us
    pallas_call x1 -> x2, Pallas kernels: 10.2 us -> 9.94 us  [the longest x1 8.18 us: pairs(): pl.pallas_call(pair_kernel, out_shape=(part, part, shape(2, LINE, OWN, WI...]
  transfers between devices with their start and end apart: 12 -> 11, of which waited for: 6 -> 5; matrix products, arithmetic and copies ran while one was open for 2% -> 4% of each run, Pallas kernels for 0% -> 0%
where the time goes in v6:
time: 132 us
  starting transfers between devices  51.6 us (39%)
  blocking collectives  37.4 us (28%)
  waiting for transfers between devices  23.4 us (18%)
  Pallas kernels  9.94 us (8%)
  local copies, waits for them, and re-layouts  5.98 us (5%)
  other arithmetic  2.45 us (2%)
    ppermute x9, starting transfers between devices, sent(): return lax.ppermute(value, axes, perm)  40 us
    all_to_all x2, blocking collectives, exchanged(): return lax.all_to_all(value, axes, split_axis=0, concat_axis=0, tiled=True)  37.4 us
    ppermute x9, waiting for transfers between devices, sent(): return lax.ppermute(value, axes, perm)  18.4 us
    all_to_all x2, starting transfers between devices, exchanged(): return lax.all_to_all(value, axes, split_axis=0, concat_axis=0, tiled=True)  11.7 us
    pallas_call x1, Pallas kernels, pairs(): pl.pallas_call(pair_kernel, out_shape=(part, part, shape(2, LINE, OWN, WI...  8.18 us
    all_to_all x2, waiting for transfers between devices, exchanged(): return lax.all_to_all(value, axes, split_axis=0, concat_axis=0, tiled=True)  5 us
    unnamed x5, local copies, waits for them, and re-layouts  3.26 us
  transfers between devices with their start and end apart: 11, of which 5 were waited for; matrix products, arithmetic and copies ran while one was open for 4% of the time, Pallas kernels for 0%

profile of v6, /device:TPU:1, one launch (start us, length us, event | category | flops | bytes accessed | tf_op | source)
XLA Modules:
  0.0 131.6 jit_solution(11896662551483299854)
XLA Ops:
  0.6 1.8 %shard_map.41 = (f32[32,1024]{1,0:T(8,128)}, f32[4,32,1024]{2,1,0:T(8,128)}) custom-call(f32[16,1024]{1,0:T(8,128)} %gen_ref.1, f32[16,1024]{1,0:T(8,128)} %data_ref.1), custom_call_target="tpu_custom_call" | custom-call | tf_op jit(solution)/shard_map/pallas_call | solution.py:117
  2.4 7.6 %all-to-all-start = ((f32[4,32,1024]{2,1,0:T(8,128)}), f32[4,32,1024]{2,1,0:T(8,128)}, u32[]{:S(2)}, u32[]{:S(2)}) async-start(f32[4,32,1024]{2,1,0:T(8,128)} %get-tuple-element.11), calls=%async_computation | async-start | bytes 1048576 | tf_op jit(solution)/shard_map/all_to_all | solution.py:144
  10.0 10.6 %collective-permute-start.3 = (f32[32,1024]{1,0:T(8,128)}, f32[32,1024]{1,0:T(8,128)S(1)}, u32[]{:S(2)}, u32[]{:S(2)}) collective-permute-start(f32[32,1024]{1,0:T(8,128)} %get-tuple-element.12), channel_id=1, source_target_pairs={{0,16},{4,20},{8,24},{12,28},{16,0},{20,4},{24,8},{28,12},{1,17},{... | collective-permute-start | bytes 393224 | tf_op jit(solution)/shard_map/ppermute | solution.py:140
  20.7 1.9 %collective-permute-start.2 = (f32[32,1024]{1,0:T(8,128)}, f32[32,1024]{1,0:T(8,128)S(1)}, u32[]{:S(2)}, u32[]{:S(2)}) collective-permute-start(f32[32,1024]{1,0:T(8,128)} %get-tuple-element.12), channel_id=1, source_target_pairs={{0,24},{4,28},{8,0},{12,4},{16,8},{20,12},{24,16},{28,20},{1,25},{... | collective-permute-start | bytes 393224 | tf_op jit(solution)/shard_map/ppermute | solution.py:140
  22.6 4.2 %collective-permute-start.1 = (f32[32,1024]{1,0:T(8,128)}, f32[32,1024]{1,0:T(8,128)S(1)}, u32[]{:S(2)}, u32[]{:S(2)}) collective-permute-start(f32[32,1024]{1,0:T(8,128)} %get-tuple-element.12), channel_id=1, source_target_pairs={{0,8},{4,12},{8,16},{12,20},{16,24},{20,28},{24,0},{28,4},{1,9},{5... | collective-permute-start | bytes 393224 | tf_op jit(solution)/shard_map/ppermute | solution.py:140
  26.9 0.0 all-to-all-done
  26.9 2.3 %collective-permute-start = (f32[4,32,1024]{2,1,0:T(8,128)}, f32[4,32,1024]{2,1,0:T(8,128)}, u32[]{:S(2)}, u32[]{:S(2)}) collective-permute-start(f32[4,32,1024]{2,1,0:T(8,128)} %all-to-all-done), channel_id=1, source_target_pairs={{0,98},{1,3},{2,0},{3,33},{32,2},{33,35},{34,32},{35,65},{64,34},{... | collective-permute-start | bytes 1572872 | tf_op jit(solution)/shard_map/ppermute | solution.py:140
  29.2 5.2 %collective-permute-done.2 = f32[32,1024]{1,0:T(8,128)S(1)} collective-permute-done((f32[32,1024]{1,0:T(8,128)}, f32[32,1024]{1,0:T(8,128)S(1)}, u32[]{:S(2)}, u32[]{:S(2)}) %collective-permute-start.2) | collective-permute-done | bytes 131104 | tf_op jit(solution)/shard_map/ppermute | solution.py:140
  34.4 0.9 pad_maximum_fusion.1
  35.4 1.6 %broadcast_in_dim.8 = f32[4,4,32,1024]{3,2,1,0:T(8,128)} broadcast(f32[4,32,1024]{2,1,0:T(8,128)S(1)} %pad_maximum_fusion.1), dimensions={1,2,3} | broadcast | bytes 2621440 | tf_op jit(solution)/shard_map/broadcast_in_dim | solution.py:171
  37.0 4.0 %all-to-all-start.1 = ((f32[4,4,32,1024]{3,2,1,0:T(8,128)}), f32[4,4,32,1024]{3,2,1,0:T(8,128)S(1)}, u32[]{:S(2)}, u32[]{:S(2)}) async-start(f32[4,4,32,1024]{3,2,1,0:T(8,128)} %broadcast_in_dim.8), calls=%async_computation.1 | async-start | bytes 4194304 | tf_op jit(solution)/shard_map/all_to_all | solution.py:144
  41.0 1.1 constant_dynamic-update-slice_fusion.1
  42.1 1.1 constant_dynamic-update-slice_fusion.refs_0_
  43.2 3.5 %collective-permute-start.4 = (f32[8,32,1024]{2,1,0:T(8,128)S(1)}, f32[8,32,1024]{2,1,0:T(8,128)}, u32[]{:S(2)}, u32[]{:S(2)}) collective-permute-start(f32[8,32,1024]{2,1,0:T(8,128)S(1)} %constant_dynamic-update-slice_fusion.refs_0_), channel_id=1, source_target_pairs={{0,28},{1,5},{4,0},{5,9},{8,4},{9,13},{12,8},{13,17},{16,12},{17,2... | collective-permute-start | bytes 3145736 | tf_op jit(solution)/shard_map/ppermute | solution.py:140
  46.7 5.5 %collective-permute-start.5 = (f32[8,32,1024]{2,1,0:T(8,128)S(1)}, f32[8,32,1024]{2,1,0:T(8,128)}, u32[]{:S(2)}, u32[]{:S(2)}) collective-permute-start(f32[8,32,1024]{2,1,0:T(8,128)S(1)} %constant_dynamic-update-slice_fusion.refs_0_), channel_id=1, source_target_pairs={{0,1},{1,0},{2,3},{3,2},{4,5},{5,4},{6,7},{7,6},{8,9},{9,8},{10,11... | collective-permute-start | bytes 3145736 | tf_op jit(solution)/shard_map/ppermute | solution.py:140
  52.2 1.0 copy-done
  53.2 8.4 %collective-permute-done.4.refs_1_ = f32[8,32,1024]{2,1,0:T(8,128)} collective-permute-done((f32[8,32,1024]{2,1,0:T(8,128)S(1)}, f32[8,32,1024]{2,1,0:T(8,128)}, u32[]{:S(2)}, u32[]{:S(2)}) %collective-permute-start.4) | collective-permute-done | bytes 1048608 | tf_op jit(solution)/shard_map/ppermute | solution.py:140
  61.6 5.0 %all-to-all-done.1 = f32[4,4,32,1024]{3,2,1,0:T(8,128)S(1)} async-done(((f32[4,4,32,1024]{3,2,1,0:T(8,128)}), f32[4,4,32,1024]{3,2,1,0:T(8,128)S(1)}, u32[]{:S(2)}, u32[]{:S(2)}) %all-to-all-start.1) | async-done | bytes 2097184 | tf_op jit(solution)/shard_map/all_to_all | solution.py:144
  66.6 3.6 %collective-permute-start.6 = (f32[8,32,1024]{2,1,0:T(8,128)}, f32[8,32,1024]{2,1,0:T(8,128)}, u32[]{:S(2)}, u32[]{:S(2)}) collective-permute-start(f32[8,32,1024]{2,1,0:T(8,128)} %collective-permute-done.4.refs_1_), channel_id=1, source_target_pairs={{0,1},{1,0},{2,3},{3,2},{4,5},{5,4},{6,7},{7,6},{8,9},{9,8},{10,11... | collective-permute-start | bytes 3145736 | tf_op jit(solution)/shard_map/ppermute | solution.py:140
  70.2 0.1 pad_add_fusion.place_ref
  70.3 2.5 %collective-permute-done.6.refs_3_ = f32[8,32,1024]{2,1,0:T(8,128)} collective-permute-done((f32[8,32,1024]{2,1,0:T(8,128)}, f32[8,32,1024]{2,1,0:T(8,128)}, u32[]{:S(2)}, u32[]{:S(2)}) %collective-permute-start.6) | collective-permute-done | bytes 1048608 | tf_op jit(solution)/shard_map/ppermute | solution.py:140
  72.8 1.2 copy-done.1
  74.0 8.2 %shard_map.42 = (f32[8,16,1024]{2,1,0:T(8,128)S(1)}, f32[8,16,1024]{2,1,0:T(8,128)S(1)}, f32[2,8,16,1024]{3,2,1,0:T(8,128)S(1)}, f32[8,128]{1,0:T(8,128)S(1)}) custom-call(s32[2]{0:T(128)S(1)} %pad_add_fusion.place_ref, f32[8,32,1024]{2,1,0:T(8,128)S(1)} %copy-done.1, f32[8,32,1024]{2,1,0:T(8,128)} %collective-permute-done.4.refs_1_, ...), custom_call_target="tpu_custom_call" | custom-call | flops 4000000000 | bytes 4000000 | tf_op jit(solution)/shard_map/pallas_call | solution.py:100
  82.2 2.3 %collective-permute-start.7 = (f32[2,8,16,1024]{3,2,1,0:T(8,128)S(1)}, f32[2,8,16,1024]{3,2,1,0:T(8,128)S(1)}, u32[]{:S(2)}, u32[]{:S(2)}) collective-permute-start(f32[2,8,16,1024]{3,2,1,0:T(8,128)S(1)} %get-tuple-element.17), channel_id=1, source_target_pairs={{0,1},{1,0},{2,3},{3,2},{4,5},{5,4},{6,7},{7,6},{8,9},{9,8},{10,11... | collective-permute-start | bytes 3145736 | tf_op jit(solution)/shard_map/ppermute | solution.py:140
  84.5 2.3 %collective-permute-done.7 = f32[2,8,16,1024]{3,2,1,0:T(8,128)S(1)} collective-permute-done((f32[2,8,16,1024]{3,2,1,0:T(8,128)S(1)}, f32[2,8,16,1024]{3,2,1,0:T(8,128)S(1)}, u32[]{:S(2)}, u32[]{:S(2)}) %collective-permute-start.7) | collective-permute-done | bytes 1048608 | tf_op jit(solution)/shard_map/ppermute | solution.py:140
  86.8 0.1 fusion
  86.8 6.0 %collective-permute-start.8 = (f32[8,16,1024]{2,1,0:T(8,128)S(1)}, f32[8,16,1024]{2,1,0:T(8,128)S(1)}, u32[]{:S(2)}, u32[]{:S(2)}) collective-permute-start(f32[8,16,1024]{2,1,0:T(8,128)S(1)} %fusion), channel_id=1, source_target_pairs={{0,4},{1,29},{4,8},{5,1},{8,12},{9,5},{12,16},{13,9},{16,20},{17,1... | collective-permute-start | bytes 1572872 | tf_op jit(solution)/shard_map/ppermute | solution.py:140
  92.8 13.8 %all_to_all.20 = f32[64,1,128]{2,1,0:T(1,128)S(1)} all-to-all(f32[64,1,128]{2,1,0:T(1,128)S(1)} %broadcast_in_dim.10), channel_id=1, replica_groups=mesh['x'=4,'yh'=4,'zh'=4,'zl'=2,'yl'=2,'c'=2] {'x','zh','zl','c'}, dimensions={0} | all-to-all | bytes 65536 | tf_op jit(solution)/shard_map/all_to_all | solution.py:144
  106.7 0.1 fusion.2
  106.8 23.6 %all_to_all.21 = f32[8,16,1152]{2,1,0:T(8,128)S(1)} all-to-all(f32[8,16,1152]{2,1,0:T(8,128)S(1)} %pad_maximum_fusion), channel_id=1, replica_groups=mesh['x'=4,'yh'=4,'zh'=4,'zl'=2,'yl'=2,'c'=2] {'yh','yl'}, dimensions={0} | all-to-all | bytes 1179648 | tf_op jit(solution)/shard_map/all_to_all | solution.py:144
  130.4 0.5 slice_reduce_fusion.1
  130.9 0.7 slice_reduce_fusion
  (12 shorter events, 0.1 us)
Async XLA Ops:
  2.4 24.5 %all-to-all-start = ((f32[4,32,1024]{2,1,0:T(8,128)}), f32[4,32,1024]{2,1,0:T(8,128)}, u32[]{:S(2)}, u32[]{:S(2)}) async-start(f32[4,32,1024]{2,1,0:T(8,128)} %get-tuple-element.11), calls=%async_computation | async-start | bytes 1048576 | tf_op jit(solution)/shard_map/all_to_all | solution.py:144
  10.0 19.2 %collective-permute-start.3 = (f32[32,1024]{1,0:T(8,128)}, f32[32,1024]{1,0:T(8,128)S(1)}, u32[]{:S(2)}, u32[]{:S(2)}) collective-permute-start(f32[32,1024]{1,0:T(8,128)} %get-tuple-element.12), channel_id=1, source_target_pairs={{0,16},{4,20},{8,24},{12,28},{16,0},{20,4},{24,8},{28,12},{1,17},{... | collective-permute-start | bytes 393224 | tf_op jit(solution)/shard_map/ppermute | solution.py:140
  20.7 13.7 %collective-permute-start.2 = (f32[32,1024]{1,0:T(8,128)}, f32[32,1024]{1,0:T(8,128)S(1)}, u32[]{:S(2)}, u32[]{:S(2)}) collective-permute-start(f32[32,1024]{1,0:T(8,128)} %get-tuple-element.12), channel_id=1, source_target_pairs={{0,24},{4,28},{8,0},{12,4},{16,8},{20,12},{24,16},{28,20},{1,25},{... | collective-permute-start | bytes 393224 | tf_op jit(solution)/shard_map/ppermute | solution.py:140
  22.6 11.8 %collective-permute-start.1 = (f32[32,1024]{1,0:T(8,128)}, f32[32,1024]{1,0:T(8,128)S(1)}, u32[]{:S(2)}, u32[]{:S(2)}) collective-permute-start(f32[32,1024]{1,0:T(8,128)} %get-tuple-element.12), channel_id=1, source_target_pairs={{0,8},{4,12},{8,16},{12,20},{16,24},{20,28},{24,0},{28,4},{1,9},{5... | collective-permute-start | bytes 393224 | tf_op jit(solution)/shard_map/ppermute | solution.py:140
  26.9 15.2 %collective-permute-start = (f32[4,32,1024]{2,1,0:T(8,128)}, f32[4,32,1024]{2,1,0:T(8,128)}, u32[]{:S(2)}, u32[]{:S(2)}) collective-permute-start(f32[4,32,1024]{2,1,0:T(8,128)} %all-to-all-done), channel_id=1, source_target_pairs={{0,98},{1,3},{2,0},{3,33},{32,2},{33,35},{34,32},{35,65},{64,34},{... | collective-permute-start | bytes 1572872 | tf_op jit(solution)/shard_map/ppermute | solution.py:140
  37.0 29.6 %all-to-all-start.1 = ((f32[4,4,32,1024]{3,2,1,0:T(8,128)}), f32[4,4,32,1024]{3,2,1,0:T(8,128)S(1)}, u32[]{:S(2)}, u32[]{:S(2)}) async-start(f32[4,4,32,1024]{3,2,1,0:T(8,128)} %broadcast_in_dim.8), calls=%async_computation.1 | async-start | bytes 4194304 | tf_op jit(solution)/shard_map/all_to_all | solution.py:144
  43.2 18.4 %collective-permute-start.4 = (f32[8,32,1024]{2,1,0:T(8,128)S(1)}, f32[8,32,1024]{2,1,0:T(8,128)}, u32[]{:S(2)}, u32[]{:S(2)}) collective-permute-start(f32[8,32,1024]{2,1,0:T(8,128)S(1)} %constant_dynamic-update-slice_fusion.refs_0_), channel_id=1, source_target_pairs={{0,28},{1,5},{4,0},{5,9},{8,4},{9,13},{12,8},{13,17},{16,12},{17,2... | collective-permute-start | bytes 3145736 | tf_op jit(solution)/shard_map/ppermute | solution.py:140
  46.7 23.6 %collective-permute-start.5 = (f32[8,32,1024]{2,1,0:T(8,128)S(1)}, f32[8,32,1024]{2,1,0:T(8,128)}, u32[]{:S(2)}, u32[]{:S(2)}) collective-permute-start(f32[8,32,1024]{2,1,0:T(8,128)S(1)} %constant_dynamic-update-slice_fusion.refs_0_), channel_id=1, source_target_pairs={{0,1},{1,0},{2,3},{3,2},{4,5},{5,4},{6,7},{7,6},{8,9},{9,8},{10,11... | collective-permute-start | bytes 3145736 | tf_op jit(solution)/shard_map/ppermute | solution.py:140
  52.2 1.0 copy-start
  66.6 6.2 %collective-permute-start.6 = (f32[8,32,1024]{2,1,0:T(8,128)}, f32[8,32,1024]{2,1,0:T(8,128)}, u32[]{:S(2)}, u32[]{:S(2)}) collective-permute-start(f32[8,32,1024]{2,1,0:T(8,128)} %collective-permute-done.4.refs_1_), channel_id=1, source_target_pairs={{0,1},{1,0},{2,3},{3,2},{4,5},{5,4},{6,7},{7,6},{8,9},{9,8},{10,11... | collective-permute-start | bytes 3145736 | tf_op jit(solution)/shard_map/ppermute | solution.py:140
  72.8 1.2 copy-start.1
  82.2 4.6 %collective-permute-start.7 = (f32[2,8,16,1024]{3,2,1,0:T(8,128)S(1)}, f32[2,8,16,1024]{3,2,1,0:T(8,128)S(1)}, u32[]{:S(2)}, u32[]{:S(2)}) collective-permute-start(f32[2,8,16,1024]{3,2,1,0:T(8,128)S(1)} %get-tuple-element.17), channel_id=1, source_target_pairs={{0,1},{1,0},{2,3},{3,2},{4,5},{5,4},{6,7},{7,6},{8,9},{9,8},{10,11... | collective-permute-start | bytes 3145736 | tf_op jit(solution)/shard_map/ppermute | solution.py:140
  86.8 19.8 %collective-permute-start.8 = (f32[8,16,1024]{2,1,0:T(8,128)S(1)}, f32[8,16,1024]{2,1,0:T(8,128)S(1)}, u32[]{:S(2)}, u32[]{:S(2)}) collective-permute-start(f32[8,16,1024]{2,1,0:T(8,128)S(1)} %fusion), channel_id=1, source_target_pairs={{0,4},{1,29},{4,8},{5,1},{8,12},{9,5},{12,16},{13,9},{16,20},{17,1... | collective-permute-start | bytes 1572872 | tf_op jit(solution)/shard_map/ppermute | solution.py:140

commit v7 on v6

--- a/solution.py
+++ b/solution.py
@@ -90,16 +90,17 @@
         for member in range(LINE):
             at = (group * LINE + member) * OWN
             to = 2 * (member % 4) + place_ref[member // 4]
-            out_ref[to] = force[at : at + OWN]
+            out_ref[to, :, :WIDTH] = force[at : at + OWN]
     energy = jnp.sum(energy, axis=1, keepdims=True) / (TOTAL * TOTAL * ROOT_WIDTH)
     energy_ref[...] = jnp.broadcast_to(energy, energy_ref.shape)
+    back_ref[:, :, :, WIDTH:] = jnp.broadcast_to(energy, (*back_ref.shape[:3], 128))
 
 
 def pairs(place, rows, cols):
     part = shape(LINE, OWN, WIDTH)
     return pl.pallas_call(
         pair_kernel,
-        out_shape=(part, part, shape(2, LINE, OWN, WIDTH), shape(8, 128)),
+        out_shape=(part, part, shape(2, LINE, OWN, WIDTH + 128), shape(8, 128)),
         in_specs=[SMEM] + [VMEM] * 5,
         out_specs=[VMEM] * 4,
         compiler_params=PARAMS,
@@ -176,9 +177,10 @@
     yl = lax.axis_index("yl")
     place = jnp.stack([yl, 1 - yl]).astype(jnp.int32)
     mine, away, back, energy = pairs(place, (line, near, line_away, swapped(near)), cols)
-    energy = jnp.broadcast_to(energy[None, :1], (64, 1, 128))
-    energy = jnp.sum(exchanged(energy, ("x", "zh", "zl", "c")), axis=0)
     back = swapped(back)
+    energy = energy[:1] + back[0, 0, :1, WIDTH:]
+    back = back[:, :, :, :WIDTH]
+    energy = jnp.sum(exchanged(jnp.broadcast_to(energy[None], (32, 1, 128)), ("x", "zh", "zl")), axis=0)
     mine = mine + back[0] + shifted(away + back[1], Z, 1)
     loaded = jnp.concatenate([mine, jnp.broadcast_to(energy[None], (LINE, OWN, 128))], axis=2)
     loaded = exchanged(loaded, Y)

time: 132 us -> 130 us (0.985); the launches traced: 132 us -> 128 us
  blocking collectives: 37.4 us -> 33.5 us
    all_to_all x2, blocking collectives: 37.4 us -> 33.5 us  [exchanged(): return lax.all_to_all(value, axes, split_axis=0, concat_axis=0, tiled=True)]
where the time goes in v7:
time: 130 us; the launch traced here: 128 us
  starting transfers between devices  51.6 us (40%)
  blocking collectives  33.5 us (26%)
  waiting for transfers between devices  23.6 us (18%)
  Pallas kernels  9.94 us (8%)
  local copies, waits for them, and re-layouts  5.97 us (5%)
  other arithmetic  2.44 us (2%)
    ppermute x9, starting transfers between devices, sent(): return lax.ppermute(value, axes, perm)  40 us
    all_to_all x2, blocking collectives, exchanged(): return lax.all_to_all(value, axes, split_axis=0, concat_axis=0, tiled=True)  33.5 us
    ppermute x9, waiting for transfers between devices, sent(): return lax.ppermute(value, axes, perm)  18.6 us
    all_to_all x2, starting transfers between devices, exchanged(): return lax.all_to_all(value, axes, split_axis=0, concat_axis=0, tiled=True)  11.7 us
    pallas_call x1, Pallas kernels, pairs(): pl.pallas_call(pair_kernel, out_shape=(part, part, shape(2, LINE, OWN, WI...  8.19 us
    all_to_all x2, waiting for transfers between devices, exchanged(): return lax.all_to_all(value, axes, split_axis=0, concat_axis=0, tiled=True)  5 us
    unnamed x5, local copies, waits for them, and re-layouts  3.26 us
  transfers between devices with their start and end apart: 11, of which 5 were waited for; matrix products, arithmetic and copies ran while one was open for 4% of the time, Pallas kernels for 0%

profile of v7, /device:TPU:1, one launch (start us, length us, event | category | flops | bytes accessed | tf_op | source)
XLA Modules:
  0.0 127.9 jit_solution(3728536678356314378)
XLA Ops:
  0.6 1.8 %shard_map.41 = (f32[32,1024]{1,0:T(8,128)}, f32[4,32,1024]{2,1,0:T(8,128)}) custom-call(f32[16,1024]{1,0:T(8,128)} %gen_ref.1, f32[16,1024]{1,0:T(8,128)} %data_ref.1), custom_call_target="tpu_custom_call" | custom-call | tf_op jit(solution)/shard_map/pallas_call | solution.py:118
  2.4 7.6 %all-to-all-start = ((f32[4,32,1024]{2,1,0:T(8,128)}), f32[4,32,1024]{2,1,0:T(8,128)}, u32[]{:S(2)}, u32[]{:S(2)}) async-start(f32[4,32,1024]{2,1,0:T(8,128)} %get-tuple-element.11), calls=%async_computation | async-start | bytes 1048576 | tf_op jit(solution)/shard_map/all_to_all | solution.py:145
  10.0 10.6 %collective-permute-start.3 = (f32[32,1024]{1,0:T(8,128)}, f32[32,1024]{1,0:T(8,128)S(1)}, u32[]{:S(2)}, u32[]{:S(2)}) collective-permute-start(f32[32,1024]{1,0:T(8,128)} %get-tuple-element.12), channel_id=1, source_target_pairs={{0,16},{4,20},{8,24},{12,28},{16,0},{20,4},{24,8},{28,12},{1,17},{... | collective-permute-start | bytes 393224 | tf_op jit(solution)/shard_map/ppermute | solution.py:141
  20.7 1.9 %collective-permute-start.2 = (f32[32,1024]{1,0:T(8,128)}, f32[32,1024]{1,0:T(8,128)S(1)}, u32[]{:S(2)}, u32[]{:S(2)}) collective-permute-start(f32[32,1024]{1,0:T(8,128)} %get-tuple-element.12), channel_id=1, source_target_pairs={{0,24},{4,28},{8,0},{12,4},{16,8},{20,12},{24,16},{28,20},{1,25},{... | collective-permute-start | bytes 393224 | tf_op jit(solution)/shard_map/ppermute | solution.py:141
  22.6 4.2 %collective-permute-start.1 = (f32[32,1024]{1,0:T(8,128)}, f32[32,1024]{1,0:T(8,128)S(1)}, u32[]{:S(2)}, u32[]{:S(2)}) collective-permute-start(f32[32,1024]{1,0:T(8,128)} %get-tuple-element.12), channel_id=1, source_target_pairs={{0,8},{4,12},{8,16},{12,20},{16,24},{20,28},{24,0},{28,4},{1,9},{5... | collective-permute-start | bytes 393224 | tf_op jit(solution)/shard_map/ppermute | solution.py:141
  26.9 0.0 all-to-all-done
  26.9 2.3 %collective-permute-start = (f32[4,32,1024]{2,1,0:T(8,128)}, f32[4,32,1024]{2,1,0:T(8,128)}, u32[]{:S(2)}, u32[]{:S(2)}) collective-permute-start(f32[4,32,1024]{2,1,0:T(8,128)} %all-to-all-done), channel_id=1, source_target_pairs={{0,98},{1,3},{2,0},{3,33},{32,2},{33,35},{34,32},{35,65},{64,34},{... | collective-permute-start | bytes 1572872 | tf_op jit(solution)/shard_map/ppermute | solution.py:141
  29.2 5.2 %collective-permute-done.2 = f32[32,1024]{1,0:T(8,128)S(1)} collective-permute-done((f32[32,1024]{1,0:T(8,128)}, f32[32,1024]{1,0:T(8,128)S(1)}, u32[]{:S(2)}, u32[]{:S(2)}) %collective-permute-start.2) | collective-permute-done | bytes 131104 | tf_op jit(solution)/shard_map/ppermute | solution.py:141
  34.4 0.9 pad_maximum_fusion.1
  35.4 1.6 %broadcast_in_dim.8 = f32[4,4,32,1024]{3,2,1,0:T(8,128)} broadcast(f32[4,32,1024]{2,1,0:T(8,128)S(1)} %pad_maximum_fusion.1), dimensions={1,2,3} | broadcast | bytes 2621440 | tf_op jit(solution)/shard_map/broadcast_in_dim | solution.py:172
  37.0 4.0 %all-to-all-start.1 = ((f32[4,4,32,1024]{3,2,1,0:T(8,128)}), f32[4,4,32,1024]{3,2,1,0:T(8,128)S(1)}, u32[]{:S(2)}, u32[]{:S(2)}) async-start(f32[4,4,32,1024]{3,2,1,0:T(8,128)} %broadcast_in_dim.8), calls=%async_computation.1 | async-start | bytes 4194304 | tf_op jit(solution)/shard_map/all_to_all | solution.py:145
  41.0 1.1 constant_dynamic-update-slice_fusion.1
  42.1 1.1 constant_dynamic-update-slice_fusion.refs_0_
  43.2 3.5 %collective-permute-start.4 = (f32[8,32,1024]{2,1,0:T(8,128)S(1)}, f32[8,32,1024]{2,1,0:T(8,128)}, u32[]{:S(2)}, u32[]{:S(2)}) collective-permute-start(f32[8,32,1024]{2,1,0:T(8,128)S(1)} %constant_dynamic-update-slice_fusion.refs_0_), channel_id=1, source_target_pairs={{0,28},{1,5},{4,0},{5,9},{8,4},{9,13},{12,8},{13,17},{16,12},{17,2... | collective-permute-start | bytes 3145736 | tf_op jit(solution)/shard_map/ppermute | solution.py:141
  46.7 5.5 %collective-permute-start.5 = (f32[8,32,1024]{2,1,0:T(8,128)S(1)}, f32[8,32,1024]{2,1,0:T(8,128)}, u32[]{:S(2)}, u32[]{:S(2)}) collective-permute-start(f32[8,32,1024]{2,1,0:T(8,128)S(1)} %constant_dynamic-update-slice_fusion.refs_0_), channel_id=1, source_target_pairs={{0,1},{1,0},{2,3},{3,2},{4,5},{5,4},{6,7},{7,6},{8,9},{9,8},{10,11... | collective-permute-start | bytes 3145736 | tf_op jit(solution)/shard_map/ppermute | solution.py:141
  52.2 1.0 copy-done
  53.2 8.4 %collective-permute-done.4.refs_1_ = f32[8,32,1024]{2,1,0:T(8,128)} collective-permute-done((f32[8,32,1024]{2,1,0:T(8,128)S(1)}, f32[8,32,1024]{2,1,0:T(8,128)}, u32[]{:S(2)}, u32[]{:S(2)}) %collective-permute-start.4) | collective-permute-done | bytes 1048608 | tf_op jit(solution)/shard_map/ppermute | solution.py:141
  61.6 5.0 %all-to-all-done.1 = f32[4,4,32,1024]{3,2,1,0:T(8,128)S(1)} async-done(((f32[4,4,32,1024]{3,2,1,0:T(8,128)}), f32[4,4,32,1024]{3,2,1,0:T(8,128)S(1)}, u32[]{:S(2)}, u32[]{:S(2)}) %all-to-all-start.1) | async-done | bytes 2097184 | tf_op jit(solution)/shard_map/all_to_all | solution.py:145
  66.6 3.6 %collective-permute-start.6 = (f32[8,32,1024]{2,1,0:T(8,128)}, f32[8,32,1024]{2,1,0:T(8,128)}, u32[]{:S(2)}, u32[]{:S(2)}) collective-permute-start(f32[8,32,1024]{2,1,0:T(8,128)} %collective-permute-done.4.refs_1_), channel_id=1, source_target_pairs={{0,1},{1,0},{2,3},{3,2},{4,5},{5,4},{6,7},{7,6},{8,9},{9,8},{10,11... | collective-permute-start | bytes 3145736 | tf_op jit(solution)/shard_map/ppermute | solution.py:141
  70.2 0.1 pad_add_fusion.place_ref
  70.3 2.5 %collective-permute-done.6.refs_3_ = f32[8,32,1024]{2,1,0:T(8,128)} collective-permute-done((f32[8,32,1024]{2,1,0:T(8,128)}, f32[8,32,1024]{2,1,0:T(8,128)}, u32[]{:S(2)}, u32[]{:S(2)}) %collective-permute-start.6) | collective-permute-done | bytes 1048608 | tf_op jit(solution)/shard_map/ppermute | solution.py:141
  72.8 1.2 copy-done.1
  74.0 8.2 %shard_map.42 = (f32[8,16,1024]{2,1,0:T(8,128)S(1)}, f32[8,16,1024]{2,1,0:T(8,128)S(1)}, f32[2,8,16,1152]{3,2,1,0:T(8,128)S(1)}, f32[8,128]{1,0:T(8,128)S(1)}) custom-call(s32[2]{0:T(128)S(1)} %pad_add_fusion.place_ref, f32[8,32,1024]{2,1,0:T(8,128)S(1)} %copy-done.1, f32[8,32,1024]{2,1,0:T(8,128)} %collective-permute-done.4.refs_1_, ...), custom_call_target="tpu_custom_call" | custom-call | flops 4000000000 | bytes 4000000 | tf_op jit(solution)/shard_map/pallas_call | solution.py:101
  82.2 2.3 %collective-permute-start.7 = (f32[2,8,16,1152]{3,2,1,0:T(8,128)S(1)}, f32[2,8,16,1152]{3,2,1,0:T(8,128)S(1)}, u32[]{:S(2)}, u32[]{:S(2)}) collective-permute-start(f32[2,8,16,1152]{3,2,1,0:T(8,128)S(1)} %get-tuple-element.17), channel_id=1, source_target_pairs={{0,1},{1,0},{2,3},{3,2},{4,5},{5,4},{6,7},{7,6},{8,9},{9,8},{10,11... | collective-permute-start | bytes 3538952 | tf_op jit(solution)/shard_map/ppermute | solution.py:141
  84.5 2.5 %collective-permute-done.7 = f32[2,8,16,1152]{3,2,1,0:T(8,128)S(1)} collective-permute-done((f32[2,8,16,1152]{3,2,1,0:T(8,128)S(1)}, f32[2,8,16,1152]{3,2,1,0:T(8,128)S(1)}, u32[]{:S(2)}, u32[]{:S(2)}) %collective-permute-start.7) | collective-permute-done | bytes 1179680 | tf_op jit(solution)/shard_map/ppermute | solution.py:141
  87.0 0.1 fusion
  87.0 6.0 %collective-permute-start.8 = (f32[8,16,1024]{2,1,0:T(8,128)S(1)}, f32[8,16,1024]{2,1,0:T(8,128)S(1)}, u32[]{:S(2)}, u32[]{:S(2)}) collective-permute-start(f32[8,16,1024]{2,1,0:T(8,128)S(1)} %fusion), channel_id=1, source_target_pairs={{0,4},{1,29},{4,8},{5,1},{8,12},{9,5},{12,16},{13,9},{16,20},{17,1... | collective-permute-start | bytes 1572872 | tf_op jit(solution)/shard_map/ppermute | solution.py:141
  93.0 11.6 %all_to_all.20 = f32[32,1,128]{2,1,0:T(1,128)S(1)} all-to-all(f32[32,1,128]{2,1,0:T(1,128)S(1)} %broadcast_in_dim.10), channel_id=1, replica_groups=mesh['x'=4,'yh'=4,'zh'=4,'zl'=2,'yl'=2,'c'=2] {'x','zh','zl'}, dimensions={0} | all-to-all | bytes 32768 | tf_op jit(solution)/shard_map/all_to_all | solution.py:145
  104.7 0.1 fusion.2
  104.8 21.9 %all_to_all.21 = f32[8,16,1152]{2,1,0:T(8,128)S(1)} all-to-all(f32[8,16,1152]{2,1,0:T(8,128)S(1)} %pad_maximum_fusion), channel_id=1, replica_groups=mesh['x'=4,'yh'=4,'zh'=4,'zl'=2,'yl'=2,'c'=2] {'yh','yl'}, dimensions={0} | all-to-all | bytes 1179648 | tf_op jit(solution)/shard_map/all_to_all | solution.py:145
  126.7 0.5 slice_reduce_fusion.1
  127.3 0.7 slice_reduce_fusion
  (12 shorter events, 0.1 us)
Async XLA Ops:
  2.4 24.5 %all-to-all-start = ((f32[4,32,1024]{2,1,0:T(8,128)}), f32[4,32,1024]{2,1,0:T(8,128)}, u32[]{:S(2)}, u32[]{:S(2)}) async-start(f32[4,32,1024]{2,1,0:T(8,128)} %get-tuple-element.11), calls=%async_computation | async-start | bytes 1048576 | tf_op jit(solution)/shard_map/all_to_all | solution.py:145
  10.0 19.2 %collective-permute-start.3 = (f32[32,1024]{1,0:T(8,128)}, f32[32,1024]{1,0:T(8,128)S(1)}, u32[]{:S(2)}, u32[]{:S(2)}) collective-permute-start(f32[32,1024]{1,0:T(8,128)} %get-tuple-element.12), channel_id=1, source_target_pairs={{0,16},{4,20},{8,24},{12,28},{16,0},{20,4},{24,8},{28,12},{1,17},{... | collective-permute-start | bytes 393224 | tf_op jit(solution)/shard_map/ppermute | solution.py:141
  20.7 13.7 %collective-permute-start.2 = (f32[32,1024]{1,0:T(8,128)}, f32[32,1024]{1,0:T(8,128)S(1)}, u32[]{:S(2)}, u32[]{:S(2)}) collective-permute-start(f32[32,1024]{1,0:T(8,128)} %get-tuple-element.12), channel_id=1, source_target_pairs={{0,24},{4,28},{8,0},{12,4},{16,8},{20,12},{24,16},{28,20},{1,25},{... | collective-permute-start | bytes 393224 | tf_op jit(solution)/shard_map/ppermute | solution.py:141
  22.6 11.8 %collective-permute-start.1 = (f32[32,1024]{1,0:T(8,128)}, f32[32,1024]{1,0:T(8,128)S(1)}, u32[]{:S(2)}, u32[]{:S(2)}) collective-permute-start(f32[32,1024]{1,0:T(8,128)} %get-tuple-element.12), channel_id=1, source_target_pairs={{0,8},{4,12},{8,16},{12,20},{16,24},{20,28},{24,0},{28,4},{1,9},{5... | collective-permute-start | bytes 393224 | tf_op jit(solution)/shard_map/ppermute | solution.py:141
  26.9 15.2 %collective-permute-start = (f32[4,32,1024]{2,1,0:T(8,128)}, f32[4,32,1024]{2,1,0:T(8,128)}, u32[]{:S(2)}, u32[]{:S(2)}) collective-permute-start(f32[4,32,1024]{2,1,0:T(8,128)} %all-to-all-done), channel_id=1, source_target_pairs={{0,98},{1,3},{2,0},{3,33},{32,2},{33,35},{34,32},{35,65},{64,34},{... | collective-permute-start | bytes 1572872 | tf_op jit(solution)/shard_map/ppermute | solution.py:141
  37.0 29.6 %all-to-all-start.1 = ((f32[4,4,32,1024]{3,2,1,0:T(8,128)}), f32[4,4,32,1024]{3,2,1,0:T(8,128)S(1)}, u32[]{:S(2)}, u32[]{:S(2)}) async-start(f32[4,4,32,1024]{3,2,1,0:T(8,128)} %broadcast_in_dim.8), calls=%async_computation.1 | async-start | bytes 4194304 | tf_op jit(solution)/shard_map/all_to_all | solution.py:145
  43.2 18.4 %collective-permute-start.4 = (f32[8,32,1024]{2,1,0:T(8,128)S(1)}, f32[8,32,1024]{2,1,0:T(8,128)}, u32[]{:S(2)}, u32[]{:S(2)}) collective-permute-start(f32[8,32,1024]{2,1,0:T(8,128)S(1)} %constant_dynamic-update-slice_fusion.refs_0_), channel_id=1, source_target_pairs={{0,28},{1,5},{4,0},{5,9},{8,4},{9,13},{12,8},{13,17},{16,12},{17,2... | collective-permute-start | bytes 3145736 | tf_op jit(solution)/shard_map/ppermute | solution.py:141
  46.7 23.6 %collective-permute-start.5 = (f32[8,32,1024]{2,1,0:T(8,128)S(1)}, f32[8,32,1024]{2,1,0:T(8,128)}, u32[]{:S(2)}, u32[]{:S(2)}) collective-permute-start(f32[8,32,1024]{2,1,0:T(8,128)S(1)} %constant_dynamic-update-slice_fusion.refs_0_), channel_id=1, source_target_pairs={{0,1},{1,0},{2,3},{3,2},{4,5},{5,4},{6,7},{7,6},{8,9},{9,8},{10,11... | collective-permute-start | bytes 3145736 | tf_op jit(solution)/shard_map/ppermute | solution.py:141
  52.2 1.0 copy-start
  66.6 6.2 %collective-permute-start.6 = (f32[8,32,1024]{2,1,0:T(8,128)}, f32[8,32,1024]{2,1,0:T(8,128)}, u32[]{:S(2)}, u32[]{:S(2)}) collective-permute-start(f32[8,32,1024]{2,1,0:T(8,128)} %collective-permute-done.4.refs_1_), channel_id=1, source_target_pairs={{0,1},{1,0},{2,3},{3,2},{4,5},{5,4},{6,7},{7,6},{8,9},{9,8},{10,11... | collective-permute-start | bytes 3145736 | tf_op jit(solution)/shard_map/ppermute | solution.py:141
  72.8 1.2 copy-start.1
  82.2 4.7 %collective-permute-start.7 = (f32[2,8,16,1152]{3,2,1,0:T(8,128)S(1)}, f32[2,8,16,1152]{3,2,1,0:T(8,128)S(1)}, u32[]{:S(2)}, u32[]{:S(2)}) collective-permute-start(f32[2,8,16,1152]{3,2,1,0:T(8,128)S(1)} %get-tuple-element.17), channel_id=1, source_target_pairs={{0,1},{1,0},{2,3},{3,2},{4,5},{5,4},{6,7},{7,6},{8,9},{9,8},{10,11... | collective-permute-start | bytes 3538952 | tf_op jit(solution)/shard_map/ppermute | solution.py:141
  87.0 17.6 %collective-permute-start.8 = (f32[8,16,1024]{2,1,0:T(8,128)S(1)}, f32[8,16,1024]{2,1,0:T(8,128)S(1)}, u32[]{:S(2)}, u32[]{:S(2)}) collective-permute-start(f32[8,16,1024]{2,1,0:T(8,128)S(1)} %fusion), channel_id=1, source_target_pairs={{0,4},{1,29},{4,8},{5,1},{8,12},{9,5},{12,16},{13,9},{16,20},{17,1... | collective-permute-start | bytes 1572872 | tf_op jit(solution)/shard_map/ppermute | solution.py:141

commit v8 on v7

--- a/solution.py
+++ b/solution.py
@@ -13,7 +13,7 @@
 WIDTH = 1024
 LINE = 8
 UNITS = 16
-COUNT = LINE * 4 * OWN
+COUNT = LINE * 2 * OWN
 DEPTH = UNITS * OWN
 ROOT_WIDTH = 32.0
 TOTAL = 8192.0
@@ -53,8 +53,9 @@
     return -1.0 if kind == 0 else 1.0
 
 
-def pair_kernel(place_ref, *refs):
-    row_refs, (cols_ref, mine_ref, away_ref, back_ref, energy_ref) = refs[:4], refs[4:]
+def pair_kernel(place_ref, first_ref, second_ref, cols_ref, *refs):
+    row_refs, (out_refs, energy_ref) = (first_ref, second_ref), refs[-2:]
+    before = refs[0][0:1, 0:1] if len(refs) == 3 else 0.0
 
     def rows_of(kind):
         return jnp.concatenate([flat(ref[:, kind * OWN : (kind + 1) * OWN, :]) for ref in row_refs], axis=0)
@@ -85,27 +86,27 @@
         total = total + jnp.sum(weight, axis=1, keepdims=True)
         force = force + product(halves(weight), cols_hl, NN)
     force = total * row_gen - force
-    outs = (mine_ref, away_ref, back_ref.at[0], back_ref.at[1])
-    for group, out_ref in enumerate(outs):
+    for group in range(2):
         for member in range(LINE):
             at = (group * LINE + member) * OWN
             to = 2 * (member % 4) + place_ref[member // 4]
-            out_ref[to, :, :WIDTH] = force[at : at + OWN]
-    energy = jnp.sum(energy, axis=1, keepdims=True) / (TOTAL * TOTAL * ROOT_WIDTH)
+            out_refs[group, to, :, :WIDTH] = force[at : at + OWN]
+    energy = before + jnp.sum(energy, axis=1, keepdims=True) / (TOTAL * TOTAL * ROOT_WIDTH)
     energy_ref[...] = jnp.broadcast_to(energy, energy_ref.shape)
-    back_ref[:, :, :, WIDTH:] = jnp.broadcast_to(energy, (*back_ref.shape[:3], 128))
+    if out_refs.shape[-1] > WIDTH:
+        out_refs[:, :, :, WIDTH:] = jnp.broadcast_to(energy, (*out_refs.shape[:3], 128))
 
 
-def pairs(place, rows, cols):
-    part = shape(LINE, OWN, WIDTH)
+def pairs(place, first, second, cols, *before, flops):
+    extra = 128 * len(before)
     return pl.pallas_call(
         pair_kernel,
-        out_shape=(part, part, shape(2, LINE, OWN, WIDTH + 128), shape(8, 128)),
-        in_specs=[SMEM] + [VMEM] * 5,
-        out_specs=[VMEM] * 4,
+        out_shape=(shape(2, LINE, OWN, WIDTH + extra), shape(8, 128)),
+        in_specs=[SMEM] + [VMEM] * (3 + len(before)),
+        out_specs=[VMEM] * 2,
         compiler_params=PARAMS,
-        cost_estimate=cost(4_000_000_000),
-    )(place, *rows, cols)
+        cost_estimate=cost(flops),
+    )(place, first, second, cols, *before)
 
 
 def spread_kernel(gen_ref, data_ref, own_ref, copies_ref):
@@ -167,19 +168,22 @@
 def body(generated, data):
     own, copies = spread(generated, data)
     line = exchanged(copies, ("yh",))
-    parity = jnp.stack([own] + [along(own, Z, steps) for steps in (2, -2, 4)])
-    parity, _ = lax.optimization_barrier((parity, line))
+    up, down, far = (along(own, Z, steps) for steps in (2, -2, 4))
+    line, up, down = lax.optimization_barrier((line, up, down))
+    parity = jnp.stack([own, up, down, far])
     cols = exchanged(jnp.broadcast_to(parity[None], (4,) + parity.shape), ("x",))
     line = joined(line, shifted(line, Y, -1))
     near = shifted(line, Z, -1)
-    line_away = swapped(line)
-    cols, near = lax.optimization_barrier((cols.reshape((UNITS,) + own.shape), near))
+    line_away, near_away = swapped(line), swapped(near)
+    cols = cols.reshape((UNITS,) + own.shape)
     yl = lax.axis_index("yl")
     place = jnp.stack([yl, 1 - yl]).astype(jnp.int32)
-    mine, away, back, energy = pairs(place, (line, near, line_away, swapped(near)), cols)
+    mine, energy = pairs(place, line, near, cols, flops=6_000_000_000)
+    back, energy = pairs(place, line_away, near_away, cols, energy, flops=2_000_000_000)
     back = swapped(back)
     energy = energy[:1] + back[0, 0, :1, WIDTH:]
     back = back[:, :, :, :WIDTH]
+    mine, away = mine[0], mine[1]
     energy = jnp.sum(exchanged(jnp.broadcast_to(energy[None], (32, 1, 128)), ("x", "zh", "zl")), axis=0)
     mine = mine + back[0] + shifted(away + back[1], Z, 1)
     loaded = jnp.concatenate([mine, jnp.broadcast_to(energy[None], (LINE, OWN, 128))], axis=2)

time: 130 us -> 141 us (1.085)
  starting transfers between devices: 51.6 us -> 61.3 us
  blocking collectives: 33.5 us -> 42.2 us
  waiting for transfers between devices: 23.6 us -> 17.4 us
  local copies, waits for them, and re-layouts: 5.97 us -> 3.32 us
    ppermute x9, starting transfers between devices: 40 us -> 49.7 us  [sent(): return lax.ppermute(value, axes, perm)]
    all_to_all x2, blocking collectives: 33.5 us -> 42.2 us  [exchanged(): return lax.all_to_all(value, axes, split_axis=0, concat_axis=0, tiled=True)]
    all_to_all x2, waiting for transfers between devices: 5 us -> 0.01 us  [exchanged(): return lax.all_to_all(value, axes, split_axis=0, concat_axis=0, tiled=True)]
    unnamed x5 -> x1, local copies, waits for them, and re-layouts: 3.26 us -> 0.85 us
    pallas_call x1 -> x2, Pallas kernels: 8.19 us -> 9.58 us  [pairs(): pl.pallas_call(pair_kernel, out_shape=(shape(2, LINE, OWN, WIDTH + extra)...]
  transfers between devices with their start and end apart: 11 -> 11, of which waited for: 5 -> 5; matrix products, arithmetic and copies ran while one was open for 4% -> 3% of each run, Pallas kernels for 0% -> 3%
where the time goes in v8:
time: 141 us; the launch traced here: 140 us
  starting transfers between devices  61.3 us (43%)
  blocking collectives  42.2 us (30%)
  waiting for transfers between devices  17.4 us (12%)
  Pallas kernels  11.3 us (8%)
  other arithmetic  3.46 us (2%)
  local copies, waits for them, and re-layouts  3.32 us (2%)
    ppermute x9, starting transfers between devices, sent(): return lax.ppermute(value, axes, perm)  49.7 us
    all_to_all x2, blocking collectives, exchanged(): return lax.all_to_all(value, axes, split_axis=0, concat_axis=0, tiled=True)  42.2 us
    ppermute x9, waiting for transfers between devices, sent(): return lax.ppermute(value, axes, perm)  17.4 us
    all_to_all x2, starting transfers between devices, exchanged(): return lax.all_to_all(value, axes, split_axis=0, concat_axis=0, tiled=True)  11.7 us
    pallas_call x2, Pallas kernels, pairs(): pl.pallas_call(pair_kernel, out_shape=(shape(2, LINE, OWN, WIDTH + extra)...  9.58 us
  transfers between devices with their start and end apart: 11, of which 5 were waited for; matrix products, arithmetic and copies ran while one was open for 3% of the time, Pallas kernels for 3%

profile of v8, /device:TPU:1, one launch (start us, length us, event | category | flops | bytes accessed | tf_op | source)
XLA Modules:
  0.0 139.8 jit_solution(15056346829513119747)
XLA Ops:
  0.6 1.8 %shard_map.41 = (f32[32,1024]{1,0:T(8,128)}, f32[4,32,1024]{2,1,0:T(8,128)}) custom-call(f32[16,1024]{1,0:T(8,128)} %gen_ref.1, f32[16,1024]{1,0:T(8,128)} %data_ref.1), custom_call_target="tpu_custom_call" | custom-call | tf_op jit(solution)/shard_map/pallas_call | solution.py:119
  2.4 7.6 %all-to-all-start = ((f32[4,32,1024]{2,1,0:T(8,128)}), f32[4,32,1024]{2,1,0:T(8,128)S(1)}, u32[]{:S(2)}, u32[]{:S(2)}) async-start(f32[4,32,1024]{2,1,0:T(8,128)} %get-tuple-element.11), calls=%async_computation | async-start | bytes 1048576 | tf_op jit(solution)/shard_map/all_to_all | solution.py:146
  10.0 5.8 %collective-permute-start = (f32[32,1024]{1,0:T(8,128)}, f32[32,1024]{1,0:T(8,128)S(1)}, u32[]{:S(2)}, u32[]{:S(2)}) collective-permute-start(f32[32,1024]{1,0:T(8,128)} %get-tuple-element.12), channel_id=1, source_target_pairs={{0,8},{4,12},{8,16},{12,20},{16,24},{20,28},{24,0},{28,4},{1,9},{5... | collective-permute-start | bytes 393224 | tf_op jit(solution)/shard_map/ppermute | solution.py:142
  15.8 6.8 %collective-permute-start.1 = (f32[32,1024]{1,0:T(8,128)}, f32[32,1024]{1,0:T(8,128)S(1)}, u32[]{:S(2)}, u32[]{:S(2)}) collective-permute-start(f32[32,1024]{1,0:T(8,128)} %get-tuple-element.12), channel_id=1, source_target_pairs={{0,24},{4,28},{8,0},{12,4},{16,8},{20,12},{24,16},{28,20},{1,25},{... | collective-permute-start | bytes 393224 | tf_op jit(solution)/shard_map/ppermute | solution.py:142
  22.6 1.2 collective-permute-done
  23.8 4.7 %collective-permute-done.1 = f32[32,1024]{1,0:T(8,128)S(1)} collective-permute-done((f32[32,1024]{1,0:T(8,128)}, f32[32,1024]{1,0:T(8,128)S(1)}, u32[]{:S(2)}, u32[]{:S(2)}) %collective-permute-start.1) | collective-permute-done | bytes 131104 | tf_op jit(solution)/shard_map/ppermute | solution.py:142
  28.5 0.0 all-to-all-done
  28.5 2.3 %collective-permute-start.2 = (f32[4,32,1024]{2,1,0:T(8,128)S(1)}, f32[4,32,1024]{2,1,0:T(8,128)S(1)}, u32[]{:S(2)}, u32[]{:S(2)}) collective-permute-start(f32[4,32,1024]{2,1,0:T(8,128)S(1)} %all-to-all-done), channel_id=1, source_target_pairs={{0,98},{1,3},{2,0},{3,33},{32,2},{33,35},{34,32},{35,65},{64,34},{... | collective-permute-start | bytes 1572872 | tf_op jit(solution)/shard_map/ppermute | solution.py:142
  30.8 6.0 %collective-permute-start.4 = (f32[32,1024]{1,0:T(8,128)}, f32[32,1024]{1,0:T(8,128)S(1)}, u32[]{:S(2)}, u32[]{:S(2)}) collective-permute-start(f32[32,1024]{1,0:T(8,128)} %get-tuple-element.12), channel_id=1, source_target_pairs={{0,16},{4,20},{8,24},{12,28},{16,0},{20,4},{24,8},{28,12},{1,17},{... | collective-permute-start | bytes 393224 | tf_op jit(solution)/shard_map/ppermute | solution.py:142
  36.8 3.9 %collective-permute-done.4 = f32[32,1024]{1,0:T(8,128)S(1)} collective-permute-done((f32[32,1024]{1,0:T(8,128)}, f32[32,1024]{1,0:T(8,128)S(1)}, u32[]{:S(2)}, u32[]{:S(2)}) %collective-permute-start.4) | collective-permute-done | bytes 131104 | tf_op jit(solution)/shard_map/ppermute | solution.py:142
  40.7 0.9 pad_maximum_fusion.1
  41.7 1.6 %broadcast_in_dim.8 = f32[4,4,32,1024]{3,2,1,0:T(8,128)} broadcast(f32[4,32,1024]{2,1,0:T(8,128)S(1)} %pad_maximum_fusion.1), dimensions={1,2,3} | broadcast | bytes 2621440 | tf_op jit(solution)/shard_map/broadcast_in_dim | solution.py:174
  43.3 4.0 %all-to-all-start.1 = ((f32[4,4,32,1024]{3,2,1,0:T(8,128)}), f32[4,4,32,1024]{3,2,1,0:T(8,128)S(1)}, u32[]{:S(2)}, u32[]{:S(2)}) async-start(f32[4,4,32,1024]{3,2,1,0:T(8,128)} %broadcast_in_dim.8), calls=%async_computation.1 | async-start | bytes 4194304 | tf_op jit(solution)/shard_map/all_to_all | solution.py:146
  47.3 0.8 constant_dynamic-update-slice_fusion.1
  48.1 0.8 constant_dynamic-update-slice_fusion.first_ref
  49.0 2.2 %collective-permute-start.3 = (f32[8,32,1024]{2,1,0:T(8,128)}, f32[8,32,1024]{2,1,0:T(8,128)}, u32[]{:S(2)}, u32[]{:S(2)}) collective-permute-start(f32[8,32,1024]{2,1,0:T(8,128)} %constant_dynamic-update-slice_fusion.first_ref), channel_id=1, source_target_pairs={{0,28},{1,5},{4,0},{5,9},{8,4},{9,13},{12,8},{13,17},{16,12},{17,2... | collective-permute-start | bytes 3145736 | tf_op jit(solution)/shard_map/ppermute | solution.py:142
  51.1 11.6 %collective-permute-start.5 = (f32[8,32,1024]{2,1,0:T(8,128)}, f32[8,32,1024]{2,1,0:T(8,128)}, u32[]{:S(2)}, u32[]{:S(2)}) collective-permute-start(f32[8,32,1024]{2,1,0:T(8,128)} %constant_dynamic-update-slice_fusion.first_ref), channel_id=1, source_target_pairs={{0,1},{1,0},{2,3},{3,2},{4,5},{5,4},{6,7},{7,6},{8,9},{9,8},{10,11... | collective-permute-start | bytes 3145736 | tf_op jit(solution)/shard_map/ppermute | solution.py:142
  62.8 4.8 %collective-permute-done.3.second_ref = f32[8,32,1024]{2,1,0:T(8,128)} collective-permute-done((f32[8,32,1024]{2,1,0:T(8,128)}, f32[8,32,1024]{2,1,0:T(8,128)}, u32[]{:S(2)}, u32[]{:S(2)}) %collective-permute-start.3) | collective-permute-done | bytes 1048608 | tf_op jit(solution)/shard_map/ppermute | solution.py:142
  67.6 7.8 %collective-permute-start.6 = (f32[8,32,1024]{2,1,0:T(8,128)}, f32[8,32,1024]{2,1,0:T(8,128)}, u32[]{:S(2)}, u32[]{:S(2)}) collective-permute-start(f32[8,32,1024]{2,1,0:T(8,128)} %collective-permute-done.3.second_ref), channel_id=1, source_target_pairs={{0,1},{1,0},{2,3},{3,2},{4,5},{5,4},{6,7},{7,6},{8,9},{9,8},{10,11... | collective-permute-start | bytes 3145736 | tf_op jit(solution)/shard_map/ppermute | solution.py:142
  75.4 0.1 pad_add_fusion.place_ref
  75.5 0.0 all-to-all-done.1
  75.5 4.8 %shard_map.42 = (f32[2,8,16,1024]{3,2,1,0:T(8,128)S(1)}, f32[8,128]{1,0:T(8,128)S(1)}) custom-call(s32[2]{0:T(128)S(1)} %pad_add_fusion.place_ref, f32[8,32,1024]{2,1,0:T(8,128)} %constant_dynamic-update-slice_fusion.first_ref, f32[8,32,1024]{2,1,0:T(8,128)} %collective-permute-done.3.second_ref, f32[16,32,1024]{2,1,0:T(8,128)S(1)} %bitcast.24), custom_call_target="tpu_custom_call" | custom-call | flops 6000000000 | bytes 4000000 | tf_op jit(solution)/shard_map/pallas_call | solution.py:102
  80.3 4.8 %shard_map.43 = (f32[2,8,16,1152]{3,2,1,0:T(8,128)S(1)}, f32[8,128]{1,0:T(8,128)S(1)}) custom-call(s32[2]{0:T(128)S(1)} %pad_add_fusion.place_ref, f32[8,32,1024]{2,1,0:T(8,128)} %collective-permute-done.5.first_ref, f32[8,32,1024]{2,1,0:T(8,128)} %collective-permute-done.6.second_ref, f32[16,32,1024]{2,1,0:T(8,128)S(1)} %bitcast.25, ...), custom_call_target="tpu_custom_call" | custom-call | flops 2000000000 | bytes 4000000 | tf_op jit(solution)/shard_map/pallas_call | solution.py:102
  85.1 1.9 %collective-permute-start.7 = (f32[2,8,16,1152]{3,2,1,0:T(8,128)S(1)}, f32[2,8,16,1152]{3,2,1,0:T(8,128)S(1)}, u32[]{:S(2)}, u32[]{:S(2)}) collective-permute-start(f32[2,8,16,1152]{3,2,1,0:T(8,128)S(1)} %get-tuple-element.18), channel_id=1, source_target_pairs={{0,1},{1,0},{2,3},{3,2},{4,5},{5,4},{6,7},{7,6},{8,9},{9,8},{10,11... | collective-permute-start | bytes 3538952 | tf_op jit(solution)/shard_map/ppermute | solution.py:142
  87.0 2.8 %collective-permute-done.7 = f32[2,8,16,1152]{3,2,1,0:T(8,128)S(1)} collective-permute-done((f32[2,8,16,1152]{3,2,1,0:T(8,128)S(1)}, f32[2,8,16,1152]{3,2,1,0:T(8,128)S(1)}, u32[]{:S(2)}, u32[]{:S(2)}) %collective-permute-start.7) | collective-permute-done | bytes 1179680 | tf_op jit(solution)/shard_map/ppermute | solution.py:142
  89.8 0.1 fusion
  89.9 5.3 %collective-permute-start.8 = (f32[8,16,1024]{2,1,0:T(8,128)S(1)}, f32[8,16,1024]{2,1,0:T(8,128)}, u32[]{:S(2)}, u32[]{:S(2)}) collective-permute-start(f32[8,16,1024]{2,1,0:T(8,128)S(1)} %fusion), channel_id=1, source_target_pairs={{0,4},{1,29},{4,8},{5,1},{8,12},{9,5},{12,16},{13,9},{16,20},{17,1... | collective-permute-start | bytes 1572872 | tf_op jit(solution)/shard_map/ppermute | solution.py:142
  95.2 17.1 %all_to_all.20 = f32[32,1,128]{2,1,0:T(1,128)S(1)} all-to-all(f32[32,1,128]{2,1,0:T(1,128)S(1)} %broadcast_in_dim.10), channel_id=1, replica_groups=mesh['x'=4,'yh'=4,'zh'=4,'zl'=2,'yl'=2,'c'=2] {'x','zh','zl'}, dimensions={0} | all-to-all | bytes 32768 | tf_op jit(solution)/shard_map/all_to_all | solution.py:146
  112.4 1.1 fusion.2
  113.6 25.1 %all_to_all.21 = f32[8,16,1152]{2,1,0:T(8,128)S(1)} all-to-all(f32[8,16,1152]{2,1,0:T(8,128)S(1)} %pad_maximum_fusion), channel_id=1, replica_groups=mesh['x'=4,'yh'=4,'zh'=4,'zl'=2,'yl'=2,'c'=2] {'yh','yl'}, dimensions={0} | all-to-all | bytes 1179648 | tf_op jit(solution)/shard_map/all_to_all | solution.py:146
  138.7 0.7 slice_reduce_fusion
  139.3 0.5 slice_reduce_fusion.1
  (9 shorter events, 0.1 us)
Async XLA Ops:
  2.4 26.1 %all-to-all-start = ((f32[4,32,1024]{2,1,0:T(8,128)}), f32[4,32,1024]{2,1,0:T(8,128)S(1)}, u32[]{:S(2)}, u32[]{:S(2)}) async-start(f32[4,32,1024]{2,1,0:T(8,128)} %get-tuple-element.11), calls=%async_computation | async-start | bytes 1048576 | tf_op jit(solution)/shard_map/all_to_all | solution.py:146
  10.0 13.8 %collective-permute-start = (f32[32,1024]{1,0:T(8,128)}, f32[32,1024]{1,0:T(8,128)S(1)}, u32[]{:S(2)}, u32[]{:S(2)}) collective-permute-start(f32[32,1024]{1,0:T(8,128)} %get-tuple-element.12), channel_id=1, source_target_pairs={{0,8},{4,12},{8,16},{12,20},{16,24},{20,28},{24,0},{28,4},{1,9},{5... | collective-permute-start | bytes 393224 | tf_op jit(solution)/shard_map/ppermute | solution.py:142
  15.8 12.6 %collective-permute-start.1 = (f32[32,1024]{1,0:T(8,128)}, f32[32,1024]{1,0:T(8,128)S(1)}, u32[]{:S(2)}, u32[]{:S(2)}) collective-permute-start(f32[32,1024]{1,0:T(8,128)} %get-tuple-element.12), channel_id=1, source_target_pairs={{0,24},{4,28},{8,0},{12,4},{16,8},{20,12},{24,16},{28,20},{1,25},{... | collective-permute-start | bytes 393224 | tf_op jit(solution)/shard_map/ppermute | solution.py:142
  28.5 19.7 %collective-permute-start.2 = (f32[4,32,1024]{2,1,0:T(8,128)S(1)}, f32[4,32,1024]{2,1,0:T(8,128)S(1)}, u32[]{:S(2)}, u32[]{:S(2)}) collective-permute-start(f32[4,32,1024]{2,1,0:T(8,128)S(1)} %all-to-all-done), channel_id=1, source_target_pairs={{0,98},{1,3},{2,0},{3,33},{32,2},{33,35},{34,32},{35,65},{64,34},{... | collective-permute-start | bytes 1572872 | tf_op jit(solution)/shard_map/ppermute | solution.py:142
  30.8 9.9 %collective-permute-start.4 = (f32[32,1024]{1,0:T(8,128)}, f32[32,1024]{1,0:T(8,128)S(1)}, u32[]{:S(2)}, u32[]{:S(2)}) collective-permute-start(f32[32,1024]{1,0:T(8,128)} %get-tuple-element.12), channel_id=1, source_target_pairs={{0,16},{4,20},{8,24},{12,28},{16,0},{20,4},{24,8},{28,12},{1,17},{... | collective-permute-start | bytes 393224 | tf_op jit(solution)/shard_map/ppermute | solution.py:142
  43.3 32.2 %all-to-all-start.1 = ((f32[4,4,32,1024]{3,2,1,0:T(8,128)}), f32[4,4,32,1024]{3,2,1,0:T(8,128)S(1)}, u32[]{:S(2)}, u32[]{:S(2)}) async-start(f32[4,4,32,1024]{3,2,1,0:T(8,128)} %broadcast_in_dim.8), calls=%async_computation.1 | async-start | bytes 4194304 | tf_op jit(solution)/shard_map/all_to_all | solution.py:146
  49.0 18.6 %collective-permute-start.3 = (f32[8,32,1024]{2,1,0:T(8,128)}, f32[8,32,1024]{2,1,0:T(8,128)}, u32[]{:S(2)}, u32[]{:S(2)}) collective-permute-start(f32[8,32,1024]{2,1,0:T(8,128)} %constant_dynamic-update-slice_fusion.first_ref), channel_id=1, source_target_pairs={{0,28},{1,5},{4,0},{5,9},{8,4},{9,13},{12,8},{13,17},{16,12},{17,2... | collective-permute-start | bytes 3145736 | tf_op jit(solution)/shard_map/ppermute | solution.py:142
  51.1 29.1 %collective-permute-start.5 = (f32[8,32,1024]{2,1,0:T(8,128)}, f32[8,32,1024]{2,1,0:T(8,128)}, u32[]{:S(2)}, u32[]{:S(2)}) collective-permute-start(f32[8,32,1024]{2,1,0:T(8,128)} %constant_dynamic-update-slice_fusion.first_ref), channel_id=1, source_target_pairs={{0,1},{1,0},{2,3},{3,2},{4,5},{5,4},{6,7},{7,6},{8,9},{9,8},{10,11... | collective-permute-start | bytes 3145736 | tf_op jit(solution)/shard_map/ppermute | solution.py:142
  67.6 12.6 %collective-permute-start.6 = (f32[8,32,1024]{2,1,0:T(8,128)}, f32[8,32,1024]{2,1,0:T(8,128)}, u32[]{:S(2)}, u32[]{:S(2)}) collective-permute-start(f32[8,32,1024]{2,1,0:T(8,128)} %collective-permute-done.3.second_ref), channel_id=1, source_target_pairs={{0,1},{1,0},{2,3},{3,2},{4,5},{5,4},{6,7},{7,6},{8,9},{9,8},{10,11... | collective-permute-start | bytes 3145736 | tf_op jit(solution)/shard_map/ppermute | solution.py:142
  85.1 4.7 %collective-permute-start.7 = (f32[2,8,16,1152]{3,2,1,0:T(8,128)S(1)}, f32[2,8,16,1152]{3,2,1,0:T(8,128)S(1)}, u32[]{:S(2)}, u32[]{:S(2)}) collective-permute-start(f32[2,8,16,1152]{3,2,1,0:T(8,128)S(1)} %get-tuple-element.18), channel_id=1, source_target_pairs={{0,1},{1,0},{2,3},{3,2},{4,5},{5,4},{6,7},{7,6},{8,9},{9,8},{10,11... | collective-permute-start | bytes 3538952 | tf_op jit(solution)/shard_map/ppermute | solution.py:142
  89.9 22.5 %collective-permute-start.8 = (f32[8,16,1024]{2,1,0:T(8,128)S(1)}, f32[8,16,1024]{2,1,0:T(8,128)}, u32[]{:S(2)}, u32[]{:S(2)}) collective-permute-start(f32[8,16,1024]{2,1,0:T(8,128)S(1)} %fusion), channel_id=1, source_target_pairs={{0,4},{1,29},{4,8},{5,1},{8,12},{9,5},{12,16},{13,9},{16,20},{17,1... | collective-permute-start | bytes 1572872 | tf_op jit(solution)/shard_map/ppermute | solution.py:142

commit v9 on v8

--- a/solution.py
+++ b/solution.py
@@ -168,14 +168,14 @@
 def body(generated, data):
     own, copies = spread(generated, data)
     line = exchanged(copies, ("yh",))
-    up, down, far = (along(own, Z, steps) for steps in (2, -2, 4))
-    line, up, down = lax.optimization_barrier((line, up, down))
-    parity = jnp.stack([own, up, down, far])
+    parity = jnp.stack([own] + [along(own, Z, steps) for steps in (2, -2, 4)])
+    parity, _ = lax.optimization_barrier((parity, line))
     cols = exchanged(jnp.broadcast_to(parity[None], (4,) + parity.shape), ("x",))
     line = joined(line, shifted(line, Y, -1))
     near = shifted(line, Z, -1)
-    line_away, near_away = swapped(line), swapped(near)
-    cols = cols.reshape((UNITS,) + own.shape)
+    line_away = swapped(line)
+    cols, near = lax.optimization_barrier((cols.reshape((UNITS,) + own.shape), near))
+    near_away = swapped(near)
     yl = lax.axis_index("yl")
     place = jnp.stack([yl, 1 - yl]).astype(jnp.int32)
     mine, energy = pairs(place, line, near, cols, flops=6_000_000_000)

time: 141 us -> 131 us (0.929)
  starting transfers between devices: 61.3 us -> 56.6 us
  waiting for transfers between devices: 17.4 us -> 14.1 us
  blocking collectives: 42.2 us -> 40.7 us
    ppermute x9, starting transfers between devices: 49.7 us -> 45 us  [sent(): return lax.ppermute(value, axes, perm)]
    ppermute x9, waiting for transfers between devices: 17.4 us -> 14 us  [sent(): return lax.ppermute(value, axes, perm)]
    all_to_all x2, blocking collectives: 42.2 us -> 40.7 us  [exchanged(): return lax.all_to_all(value, axes, split_axis=0, concat_axis=0, tiled=True)]
  transfers between devices with their start and end apart: 11 -> 11, of which waited for: 5 -> 3; matrix products, arithmetic and copies ran while one was open for 3% -> 3% of each run, Pallas kernels for 3% -> 4%
where the time goes in v9:
time: 131 us; the launch traced here: 130 us
  starting transfers between devices  56.6 us (43%)
  blocking collectives  40.7 us (31%)
  waiting for transfers between devices  14.1 us (11%)
  Pallas kernels  11.3 us (9%)
  other arithmetic  3.46 us (3%)
  local copies, waits for them, and re-layouts  3.31 us (3%)
    ppermute x9, starting transfers between devices, sent(): return lax.ppermute(value, axes, perm)  45 us
    all_to_all x2, blocking collectives, exchanged(): return lax.all_to_all(value, axes, split_axis=0, concat_axis=0, tiled=True)  40.7 us
    ppermute x9, waiting for transfers between devices, sent(): return lax.ppermute(value, axes, perm)  14 us
    all_to_all x2, starting transfers between devices, exchanged(): return lax.all_to_all(value, axes, split_axis=0, concat_axis=0, tiled=True)  11.7 us
    pallas_call x2, Pallas kernels, pairs(): pl.pallas_call(pair_kernel, out_shape=(shape(2, LINE, OWN, WIDTH + extra)...  9.58 us
  transfers between devices with their start and end apart: 11, of which 3 were waited for; matrix products, arithmetic and copies ran while one was open for 3% of the time, Pallas kernels for 4%

profile of v9, /device:TPU:1, one launch (start us, length us, event | category | flops | bytes accessed | tf_op | source)
XLA Modules:
  0.0 130.3 jit_solution(14891040027936268945)
XLA Ops:
  0.6 1.8 %shard_map.41 = (f32[32,1024]{1,0:T(8,128)}, f32[4,32,1024]{2,1,0:T(8,128)}) custom-call(f32[16,1024]{1,0:T(8,128)} %gen_ref.1, f32[16,1024]{1,0:T(8,128)} %data_ref.1), custom_call_target="tpu_custom_call" | custom-call | tf_op jit(solution)/shard_map/pallas_call | solution.py:119
  2.4 7.6 %all-to-all-start = ((f32[4,32,1024]{2,1,0:T(8,128)}), f32[4,32,1024]{2,1,0:T(8,128)S(1)}, u32[]{:S(2)}, u32[]{:S(2)}) async-start(f32[4,32,1024]{2,1,0:T(8,128)} %get-tuple-element.11), calls=%async_computation | async-start | bytes 1048576 | tf_op jit(solution)/shard_map/all_to_all | solution.py:146
  10.0 5.8 %collective-permute-start.1 = (f32[32,1024]{1,0:T(8,128)}, f32[32,1024]{1,0:T(8,128)S(1)}, u32[]{:S(2)}, u32[]{:S(2)}) collective-permute-start(f32[32,1024]{1,0:T(8,128)} %get-tuple-element.12), channel_id=1, source_target_pairs={{0,8},{4,12},{8,16},{12,20},{16,24},{20,28},{24,0},{28,4},{1,9},{5... | collective-permute-start | bytes 393224 | tf_op jit(solution)/shard_map/ppermute | solution.py:142
  15.8 6.8 %collective-permute-start.2 = (f32[32,1024]{1,0:T(8,128)}, f32[32,1024]{1,0:T(8,128)S(1)}, u32[]{:S(2)}, u32[]{:S(2)}) collective-permute-start(f32[32,1024]{1,0:T(8,128)} %get-tuple-element.12), channel_id=1, source_target_pairs={{0,24},{4,28},{8,0},{12,4},{16,8},{20,12},{24,16},{28,20},{1,25},{... | collective-permute-start | bytes 393224 | tf_op jit(solution)/shard_map/ppermute | solution.py:142
  22.6 5.5 %collective-permute-start.3 = (f32[32,1024]{1,0:T(8,128)}, f32[32,1024]{1,0:T(8,128)S(1)}, u32[]{:S(2)}, u32[]{:S(2)}) collective-permute-start(f32[32,1024]{1,0:T(8,128)} %get-tuple-element.12), channel_id=1, source_target_pairs={{0,16},{4,20},{8,24},{12,28},{16,0},{20,4},{24,8},{28,12},{1,17},{... | collective-permute-start | bytes 393224 | tf_op jit(solution)/shard_map/ppermute | solution.py:142
  28.1 0.0 all-to-all-done
  28.1 2.3 %collective-permute-start = (f32[4,32,1024]{2,1,0:T(8,128)S(1)}, f32[4,32,1024]{2,1,0:T(8,128)S(1)}, u32[]{:S(2)}, u32[]{:S(2)}) collective-permute-start(f32[4,32,1024]{2,1,0:T(8,128)S(1)} %all-to-all-done), channel_id=1, source_target_pairs={{0,98},{1,3},{2,0},{3,33},{32,2},{33,35},{34,32},{35,65},{64,34},{... | collective-permute-start | bytes 1572872 | tf_op jit(solution)/shard_map/ppermute | solution.py:142
  30.4 2.1 %collective-permute-done.3 = f32[32,1024]{1,0:T(8,128)S(1)} collective-permute-done((f32[32,1024]{1,0:T(8,128)}, f32[32,1024]{1,0:T(8,128)S(1)}, u32[]{:S(2)}, u32[]{:S(2)}) %collective-permute-start.3) | collective-permute-done | bytes 131104 | tf_op jit(solution)/shard_map/ppermute | solution.py:142
  32.5 0.9 pad_maximum_fusion.1
  33.5 1.6 %broadcast_in_dim.8 = f32[4,4,32,1024]{3,2,1,0:T(8,128)} broadcast(f32[4,32,1024]{2,1,0:T(8,128)S(1)} %pad_maximum_fusion.1), dimensions={1,2,3} | broadcast | bytes 2621440 | tf_op jit(solution)/shard_map/broadcast_in_dim | solution.py:173
  35.1 4.0 %all-to-all-start.1 = ((f32[4,4,32,1024]{3,2,1,0:T(8,128)}), f32[4,4,32,1024]{3,2,1,0:T(8,128)S(1)}, u32[]{:S(2)}, u32[]{:S(2)}) async-start(f32[4,4,32,1024]{3,2,1,0:T(8,128)} %broadcast_in_dim.8), calls=%async_computation.1 | async-start | bytes 4194304 | tf_op jit(solution)/shard_map/all_to_all | solution.py:146
  39.1 0.8 constant_dynamic-update-slice_fusion.1
  40.0 0.0 collective-permute-done
  40.0 0.8 constant_dynamic-update-slice_fusion.first_ref
  40.8 8.2 %collective-permute-start.4 = (f32[8,32,1024]{2,1,0:T(8,128)}, f32[8,32,1024]{2,1,0:T(8,128)}, u32[]{:S(2)}, u32[]{:S(2)}) collective-permute-start(f32[8,32,1024]{2,1,0:T(8,128)} %constant_dynamic-update-slice_fusion.first_ref), channel_id=1, source_target_pairs={{0,28},{1,5},{4,0},{5,9},{8,4},{9,13},{12,8},{13,17},{16,12},{17,2... | collective-permute-start | bytes 3145736 | tf_op jit(solution)/shard_map/ppermute | solution.py:142
  49.0 2.9 %collective-permute-start.5 = (f32[8,32,1024]{2,1,0:T(8,128)}, f32[8,32,1024]{2,1,0:T(8,128)}, u32[]{:S(2)}, u32[]{:S(2)}) collective-permute-start(f32[8,32,1024]{2,1,0:T(8,128)} %constant_dynamic-update-slice_fusion.first_ref), channel_id=1, source_target_pairs={{0,1},{1,0},{2,3},{3,2},{4,5},{5,4},{6,7},{7,6},{8,9},{9,8},{10,11... | collective-permute-start | bytes 3145736 | tf_op jit(solution)/shard_map/ppermute | solution.py:142
  52.0 9.1 %collective-permute-done.4.second_ref = f32[8,32,1024]{2,1,0:T(8,128)} collective-permute-done((f32[8,32,1024]{2,1,0:T(8,128)}, f32[8,32,1024]{2,1,0:T(8,128)}, u32[]{:S(2)}, u32[]{:S(2)}) %collective-permute-start.4) | collective-permute-done | bytes 1048608 | tf_op jit(solution)/shard_map/ppermute | solution.py:142
  61.1 0.0 all-to-all-done.1
  61.1 7.2 %collective-permute-start.6 = (f32[8,32,1024]{2,1,0:T(8,128)}, f32[8,32,1024]{2,1,0:T(8,128)}, u32[]{:S(2)}, u32[]{:S(2)}) collective-permute-start(f32[8,32,1024]{2,1,0:T(8,128)} %collective-permute-done.4.second_ref), channel_id=1, source_target_pairs={{0,1},{1,0},{2,3},{3,2},{4,5},{5,4},{6,7},{7,6},{8,9},{9,8},{10,11... | collective-permute-start | bytes 3145736 | tf_op jit(solution)/shard_map/ppermute | solution.py:142
  68.3 0.1 pad_add_fusion.place_ref
  68.4 4.8 %shard_map.42 = (f32[2,8,16,1024]{3,2,1,0:T(8,128)S(1)}, f32[8,128]{1,0:T(8,128)S(1)}) custom-call(s32[2]{0:T(128)S(1)} %pad_add_fusion.place_ref, f32[8,32,1024]{2,1,0:T(8,128)} %constant_dynamic-update-slice_fusion.first_ref, f32[8,32,1024]{2,1,0:T(8,128)} %collective-permute-done.4.second_ref, f32[16,32,1024]{2,1,0:T(8,128)S(1)} %bitcast.24), custom_call_target="tpu_custom_call" | custom-call | flops 6000000000 | bytes 4000000 | tf_op jit(solution)/shard_map/pallas_call | solution.py:102
  73.2 0.0 collective-permute-done.5.first_ref
  73.2 4.8 %shard_map.43 = (f32[2,8,16,1152]{3,2,1,0:T(8,128)S(1)}, f32[8,128]{1,0:T(8,128)S(1)}) custom-call(s32[2]{0:T(128)S(1)} %pad_add_fusion.place_ref, f32[8,32,1024]{2,1,0:T(8,128)} %collective-permute-done.5.first_ref, f32[8,32,1024]{2,1,0:T(8,128)} %collective-permute-done.6.second_ref, f32[16,32,1024]{2,1,0:T(8,128)S(1)} %bitcast.25, ...), custom_call_target="tpu_custom_call" | custom-call | flops 2000000000 | bytes 4000000 | tf_op jit(solution)/shard_map/pallas_call | solution.py:102
  78.0 1.9 %collective-permute-start.7 = (f32[2,8,16,1152]{3,2,1,0:T(8,128)S(1)}, f32[2,8,16,1152]{3,2,1,0:T(8,128)S(1)}, u32[]{:S(2)}, u32[]{:S(2)}) collective-permute-start(f32[2,8,16,1152]{3,2,1,0:T(8,128)S(1)} %get-tuple-element.18), channel_id=1, source_target_pairs={{0,1},{1,0},{2,3},{3,2},{4,5},{5,4},{6,7},{7,6},{8,9},{9,8},{10,11... | collective-permute-start | bytes 3538952 | tf_op jit(solution)/shard_map/ppermute | solution.py:142
  79.9 2.8 %collective-permute-done.7 = f32[2,8,16,1152]{3,2,1,0:T(8,128)S(1)} collective-permute-done((f32[2,8,16,1152]{3,2,1,0:T(8,128)S(1)}, f32[2,8,16,1152]{3,2,1,0:T(8,128)S(1)}, u32[]{:S(2)}, u32[]{:S(2)}) %collective-permute-start.7) | collective-permute-done | bytes 1179680 | tf_op jit(solution)/shard_map/ppermute | solution.py:142
  82.8 0.1 fusion
  82.8 4.3 %collective-permute-start.8 = (f32[8,16,1024]{2,1,0:T(8,128)S(1)}, f32[8,16,1024]{2,1,0:T(8,128)}, u32[]{:S(2)}, u32[]{:S(2)}) collective-permute-start(f32[8,16,1024]{2,1,0:T(8,128)S(1)} %fusion), channel_id=1, source_target_pairs={{0,4},{1,29},{4,8},{5,1},{8,12},{9,5},{12,16},{13,9},{16,20},{17,1... | collective-permute-start | bytes 1572872 | tf_op jit(solution)/shard_map/ppermute | solution.py:142
  87.2 16.0 %all_to_all.20 = f32[32,1,128]{2,1,0:T(1,128)S(1)} all-to-all(f32[32,1,128]{2,1,0:T(1,128)S(1)} %broadcast_in_dim.10), channel_id=1, replica_groups=mesh['x'=4,'yh'=4,'zh'=4,'zl'=2,'yl'=2,'c'=2] {'x','zh','zl'}, dimensions={0} | all-to-all | bytes 32768 | tf_op jit(solution)/shard_map/all_to_all | solution.py:146
  103.3 1.1 fusion.2
  104.4 24.7 %all_to_all.21 = f32[8,16,1152]{2,1,0:T(8,128)S(1)} all-to-all(f32[8,16,1152]{2,1,0:T(8,128)S(1)} %pad_maximum_fusion), channel_id=1, replica_groups=mesh['x'=4,'yh'=4,'zh'=4,'zl'=2,'yl'=2,'c'=2] {'yh','yl'}, dimensions={0} | all-to-all | bytes 1179648 | tf_op jit(solution)/shard_map/all_to_all | solution.py:146
  129.1 0.7 slice_reduce_fusion
  129.8 0.5 slice_reduce_fusion.1
  (9 shorter events, 0.1 us)
Async XLA Ops:
  2.4 25.7 %all-to-all-start = ((f32[4,32,1024]{2,1,0:T(8,128)}), f32[4,32,1024]{2,1,0:T(8,128)S(1)}, u32[]{:S(2)}, u32[]{:S(2)}) async-start(f32[4,32,1024]{2,1,0:T(8,128)} %get-tuple-element.11), calls=%async_computation | async-start | bytes 1048576 | tf_op jit(solution)/shard_map/all_to_all | solution.py:146
  10.0 20.4 %collective-permute-start.1 = (f32[32,1024]{1,0:T(8,128)}, f32[32,1024]{1,0:T(8,128)S(1)}, u32[]{:S(2)}, u32[]{:S(2)}) collective-permute-start(f32[32,1024]{1,0:T(8,128)} %get-tuple-element.12), channel_id=1, source_target_pairs={{0,8},{4,12},{8,16},{12,20},{16,24},{20,28},{24,0},{28,4},{1,9},{5... | collective-permute-start | bytes 393224 | tf_op jit(solution)/shard_map/ppermute | solution.py:142
  15.8 14.6 %collective-permute-start.2 = (f32[32,1024]{1,0:T(8,128)}, f32[32,1024]{1,0:T(8,128)S(1)}, u32[]{:S(2)}, u32[]{:S(2)}) collective-permute-start(f32[32,1024]{1,0:T(8,128)} %get-tuple-element.12), channel_id=1, source_target_pairs={{0,24},{4,28},{8,0},{12,4},{16,8},{20,12},{24,16},{28,20},{1,25},{... | collective-permute-start | bytes 393224 | tf_op jit(solution)/shard_map/ppermute | solution.py:142
  22.6 9.9 %collective-permute-start.3 = (f32[32,1024]{1,0:T(8,128)}, f32[32,1024]{1,0:T(8,128)S(1)}, u32[]{:S(2)}, u32[]{:S(2)}) collective-permute-start(f32[32,1024]{1,0:T(8,128)} %get-tuple-element.12), channel_id=1, source_target_pairs={{0,16},{4,20},{8,24},{12,28},{16,0},{20,4},{24,8},{28,12},{1,17},{... | collective-permute-start | bytes 393224 | tf_op jit(solution)/shard_map/ppermute | solution.py:142
  28.1 11.9 %collective-permute-start = (f32[4,32,1024]{2,1,0:T(8,128)S(1)}, f32[4,32,1024]{2,1,0:T(8,128)S(1)}, u32[]{:S(2)}, u32[]{:S(2)}) collective-permute-start(f32[4,32,1024]{2,1,0:T(8,128)S(1)} %all-to-all-done), channel_id=1, source_target_pairs={{0,98},{1,3},{2,0},{3,33},{32,2},{33,35},{34,32},{35,65},{64,34},{... | collective-permute-start | bytes 1572872 | tf_op jit(solution)/shard_map/ppermute | solution.py:142
  35.1 26.0 %all-to-all-start.1 = ((f32[4,4,32,1024]{3,2,1,0:T(8,128)}), f32[4,4,32,1024]{3,2,1,0:T(8,128)S(1)}, u32[]{:S(2)}, u32[]{:S(2)}) async-start(f32[4,4,32,1024]{3,2,1,0:T(8,128)} %broadcast_in_dim.8), calls=%async_computation.1 | async-start | bytes 4194304 | tf_op jit(solution)/shard_map/all_to_all | solution.py:146
  40.8 20.3 %collective-permute-start.4 = (f32[8,32,1024]{2,1,0:T(8,128)}, f32[8,32,1024]{2,1,0:T(8,128)}, u32[]{:S(2)}, u32[]{:S(2)}) collective-permute-start(f32[8,32,1024]{2,1,0:T(8,128)} %constant_dynamic-update-slice_fusion.first_ref), channel_id=1, source_target_pairs={{0,28},{1,5},{4,0},{5,9},{8,4},{9,13},{12,8},{13,17},{16,12},{17,2... | collective-permute-start | bytes 3145736 | tf_op jit(solution)/shard_map/ppermute | solution.py:142
  49.0 24.2 %collective-permute-start.5 = (f32[8,32,1024]{2,1,0:T(8,128)}, f32[8,32,1024]{2,1,0:T(8,128)}, u32[]{:S(2)}, u32[]{:S(2)}) collective-permute-start(f32[8,32,1024]{2,1,0:T(8,128)} %constant_dynamic-update-slice_fusion.first_ref), channel_id=1, source_target_pairs={{0,1},{1,0},{2,3},{3,2},{4,5},{5,4},{6,7},{7,6},{8,9},{9,8},{10,11... | collective-permute-start | bytes 3145736 | tf_op jit(solution)/shard_map/ppermute | solution.py:142
  61.1 12.1 %collective-permute-start.6 = (f32[8,32,1024]{2,1,0:T(8,128)}, f32[8,32,1024]{2,1,0:T(8,128)}, u32[]{:S(2)}, u32[]{:S(2)}) collective-permute-start(f32[8,32,1024]{2,1,0:T(8,128)} %collective-permute-done.4.second_ref), channel_id=1, source_target_pairs={{0,1},{1,0},{2,3},{3,2},{4,5},{5,4},{6,7},{7,6},{8,9},{9,8},{10,11... | collective-permute-start | bytes 3145736 | tf_op jit(solution)/shard_map/ppermute | solution.py:142
  78.0 4.7 %collective-permute-start.7 = (f32[2,8,16,1152]{3,2,1,0:T(8,128)S(1)}, f32[2,8,16,1152]{3,2,1,0:T(8,128)S(1)}, u32[]{:S(2)}, u32[]{:S(2)}) collective-permute-start(f32[2,8,16,1152]{3,2,1,0:T(8,128)S(1)} %get-tuple-element.18), channel_id=1, source_target_pairs={{0,1},{1,0},{2,3},{3,2},{4,5},{5,4},{6,7},{7,6},{8,9},{9,8},{10,11... | collective-permute-start | bytes 3538952 | tf_op jit(solution)/shard_map/ppermute | solution.py:142
  82.8 20.4 %collective-permute-start.8 = (f32[8,16,1024]{2,1,0:T(8,128)S(1)}, f32[8,16,1024]{2,1,0:T(8,128)}, u32[]{:S(2)}, u32[]{:S(2)}) collective-permute-start(f32[8,16,1024]{2,1,0:T(8,128)S(1)} %fusion), channel_id=1, source_target_pairs={{0,4},{1,29},{4,8},{5,1},{8,12},{9,5},{12,16},{13,9},{16,20},{17,1... | collective-permute-start | bytes 1572872 | tf_op jit(solution)/shard_map/ppermute | solution.py:142

commit v10 on v9

--- a/solution.py
+++ b/solution.py
@@ -1,3 +1,5 @@
+import functools
+
 import jax
 import jax.numpy as jnp
 from jax import lax
@@ -53,9 +55,17 @@
     return -1.0 if kind == 0 else 1.0
 
 
-def pair_kernel(place_ref, first_ref, second_ref, cols_ref, *refs):
-    row_refs, (out_refs, energy_ref) = (first_ref, second_ref), refs[-2:]
-    before = refs[0][0:1, 0:1] if len(refs) == 3 else 0.0
+def pair_kernel(final, place_ref, first_ref, second_ref, *refs):
+    row_refs = (first_ref, second_ref)
+    if final:
+        high_ref, low_ref, squares_ref, before_ref, out_refs, energy_ref = refs
+    else:
+        cols_ref, out_refs, energy_ref, high_ref, low_ref, squares_ref = refs
+        for kind in range(2):
+            cols = flat(cols_ref[:, kind * OWN : (kind + 1) * OWN, :])
+            high_ref[kind], low_ref[kind] = halves(cols)
+            squares = jnp.broadcast_to(jnp.sum(cols * cols, axis=1, keepdims=True), (DEPTH, 128))
+            squares_ref[kind] = jnp.transpose(squares)[0:8, :]
 
     def rows_of(kind):
         return jnp.concatenate([flat(ref[:, kind * OWN : (kind + 1) * OWN, :]) for ref in row_refs], axis=0)
@@ -68,10 +78,8 @@
     energy = jnp.zeros((1, DEPTH), jnp.float32)
     force = jnp.zeros((COUNT, WIDTH), jnp.float32)
     for kind in range(2):
-        cols = flat(cols_ref[:, kind * OWN : (kind + 1) * OWN, :])
-        cols_sq = jnp.sum(cols * cols, axis=1, keepdims=True)
-        cols_sq = jnp.transpose(jnp.broadcast_to(cols_sq, (DEPTH, 128)))[0:1, :]
-        cols_hl = halves(cols)
+        cols_hl = (high_ref[kind], low_ref[kind])
+        cols_sq = squares_ref[kind, 0:1, :]
         used = COUNT if kind == 0 else 2 * COUNT
         inner = product((rows_hl[0][:used], rows_hl[1][:used]), cols_hl, NT)
         square = jnp.maximum(rows_sq[:used] + cols_sq - 2.0 * inner, 0.0) + 1.0
@@ -91,22 +99,28 @@
             at = (group * LINE + member) * OWN
             to = 2 * (member % 4) + place_ref[member // 4]
             out_refs[group, to, :, :WIDTH] = force[at : at + OWN]
-    energy = before + jnp.sum(energy, axis=1, keepdims=True) / (TOTAL * TOTAL * ROOT_WIDTH)
+    energy = jnp.sum(energy, axis=1, keepdims=True) / (TOTAL * TOTAL * ROOT_WIDTH)
+    if final:
+        energy = before_ref[0:1, 0:1] + energy
     energy_ref[...] = jnp.broadcast_to(energy, energy_ref.shape)
-    if out_refs.shape[-1] > WIDTH:
+    if final:
         out_refs[:, :, :, WIDTH:] = jnp.broadcast_to(energy, (*out_refs.shape[:3], 128))
 
 
-def pairs(place, first, second, cols, *before, flops):
-    extra = 128 * len(before)
+def pairs(place, first, second, *operands, flops):
+    final = len(operands) > 1
+    split = shape(2, DEPTH, WIDTH, dtype=jnp.bfloat16)
+    outs = (shape(2, LINE, OWN, WIDTH + 128 * final), shape(8, 128))
+    if not final:
+        outs += (split, split, shape(2, 8, DEPTH))
     return pl.pallas_call(
-        pair_kernel,
-        out_shape=(shape(2, LINE, OWN, WIDTH + extra), shape(8, 128)),
-        in_specs=[SMEM] + [VMEM] * (3 + len(before)),
-        out_specs=[VMEM] * 2,
+        functools.partial(pair_kernel, final),
+        out_shape=outs,
+        in_specs=[SMEM] + [VMEM] * (2 + len(operands)),
+        out_specs=[VMEM] * len(outs),
         compiler_params=PARAMS,
         cost_estimate=cost(flops),
-    )(place, first, second, cols, *before)
+    )(place, first, second, *operands)
 
 
 def spread_kernel(gen_ref, data_ref, own_ref, copies_ref):
@@ -122,6 +136,21 @@
         in_specs=[VMEM] * 2,
         out_specs=[VMEM] * 2,
     )(generated, data)
+
+
+def layout_kernel(*refs):
+    for peer in range(4):
+        for unit, ref in enumerate(refs[:4]):
+            refs[4][peer, unit] = ref[...]
+
+
+def layout(*units):
+    return pl.pallas_call(
+        layout_kernel,
+        out_shape=shape(4, 4, 2 * OWN, WIDTH),
+        in_specs=[VMEM] * 4,
+        out_specs=VMEM,
+    )(*units)
 
 
 def sent(value, axes, move):
@@ -168,9 +197,9 @@
 def body(generated, data):
     own, copies = spread(generated, data)
     line = exchanged(copies, ("yh",))
-    parity = jnp.stack([own] + [along(own, Z, steps) for steps in (2, -2, 4)])
-    parity, _ = lax.optimization_barrier((parity, line))
-    cols = exchanged(jnp.broadcast_to(parity[None], (4,) + parity.shape), ("x",))
+    up, down, far = (along(own, Z, steps) for steps in (2, -2, 4))
+    parity, _ = lax.optimization_barrier((layout(own, up, down, far), line))
+    cols = exchanged(parity, ("x",))
     line = joined(line, shifted(line, Y, -1))
     near = shifted(line, Z, -1)
     line_away = swapped(line)
@@ -178,8 +207,8 @@
     near_away = swapped(near)
     yl = lax.axis_index("yl")
     place = jnp.stack([yl, 1 - yl]).astype(jnp.int32)
-    mine, energy = pairs(place, line, near, cols, flops=6_000_000_000)
-    back, energy = pairs(place, line_away, near_away, cols, energy, flops=2_000_000_000)
+    mine, energy, *split = pairs(place, line, near, cols, flops=6_000_000_000)
+    back, energy = pairs(place, line_away, near_away, *split, energy, flops=2_000_000_000)
     back = swapped(back)
     energy = energy[:1] + back[0, 0, :1, WIDTH:]
     back = back[:, :, :, :WIDTH]

time: 131 us -> 131 us (level)
  Pallas kernels: 11.3 us -> 14.1 us
  other arithmetic: 3.46 us -> 1.48 us
    pallas_call x2 -> x3, Pallas kernels: 9.58 us -> 12.3 us  [the longest x2 9.72 us: pairs(): pl.pallas_call(functools.partial(pair_kernel, final), out_shape=outs, in_...]
    broadcast_in_dim x1 -> x0, local copies, waits for them, and re-layouts: 1.63 us -> none  [body(): jnp.broadcast_to(parity[None], (4,) + parity.shape)]
  transfers between devices with their start and end apart: 11 -> 11, of which waited for: 3 -> 3; matrix products, arithmetic and copies ran while one was open for 3% -> 1% of each run, Pallas kernels for 4% -> 6%
where the time goes in v10:
time: 131 us; the launch traced here: 130 us
  starting transfers between devices  57.7 us (44%)
  blocking collectives  40 us (31%)
  Pallas kernels  14.1 us (11%)
  waiting for transfers between devices  13.7 us (10%)
  local copies, waits for them, and re-layouts  2.35 us (2%)
  other arithmetic  1.48 us (1%)
    ppermute x9, starting transfers between devices, sent(): return lax.ppermute(value, axes, perm)  46 us
    all_to_all x2, blocking collectives, exchanged(): return lax.all_to_all(value, axes, split_axis=0, concat_axis=0, tiled=True)  40 us
    ppermute x9, waiting for transfers between devices, sent(): return lax.ppermute(value, axes, perm)  13.7 us
    all_to_all x2, starting transfers between devices, exchanged(): return lax.all_to_all(value, axes, split_axis=0, concat_axis=0, tiled=True)  11.7 us
    pallas_call x2, Pallas kernels, pairs(): pl.pallas_call(functools.partial(pair_kernel, final), out_shape=outs, in_...  9.72 us
  transfers between devices with their start and end apart: 11, of which 3 were waited for; matrix products, arithmetic and copies ran while one was open for 1% of the time, Pallas kernels for 6%

profile of v10, /device:TPU:1, one launch (start us, length us, event | category | flops | bytes accessed | tf_op | source)
XLA Modules:
  0.0 130.1 jit_solution(4021980439809623633)
XLA Ops:
  0.6 1.8 %shard_map.41 = (f32[32,1024]{1,0:T(8,128)}, f32[4,32,1024]{2,1,0:T(8,128)}) custom-call(f32[16,1024]{1,0:T(8,128)} %gen_ref.1, f32[16,1024]{1,0:T(8,128)} %data_ref.1), custom_call_target="tpu_custom_call" | custom-call | tf_op jit(solution)/shard_map/pallas_call | solution.py:133
  2.4 7.6 %all-to-all-start = ((f32[4,32,1024]{2,1,0:T(8,128)}), f32[4,32,1024]{2,1,0:T(8,128)S(1)}, u32[]{:S(2)}, u32[]{:S(2)}) async-start(f32[4,32,1024]{2,1,0:T(8,128)} %get-tuple-element.14), calls=%async_computation | async-start | bytes 1048576 | tf_op jit(solution)/shard_map/all_to_all | solution.py:175
  10.0 5.8 %collective-permute-start.1 = (f32[32,1024]{1,0:T(8,128)}, f32[32,1024]{1,0:T(8,128)S(1)}, u32[]{:S(2)}, u32[]{:S(2)}) collective-permute-start(f32[32,1024]{1,0:T(8,128)} %get-tuple-element.15.refs_0_), channel_id=1, source_target_pairs={{0,8},{4,12},{8,16},{12,20},{16,24},{20,28},{24,0},{28,4},{1,9},{5... | collective-permute-start | bytes 393224 | tf_op jit(solution)/shard_map/ppermute | solution.py:171
  15.8 6.8 %collective-permute-start.2 = (f32[32,1024]{1,0:T(8,128)}, f32[32,1024]{1,0:T(8,128)S(1)}, u32[]{:S(2)}, u32[]{:S(2)}) collective-permute-start(f32[32,1024]{1,0:T(8,128)} %get-tuple-element.15.refs_0_), channel_id=1, source_target_pairs={{0,24},{4,28},{8,0},{12,4},{16,8},{20,12},{24,16},{28,20},{1,25},{... | collective-permute-start | bytes 393224 | tf_op jit(solution)/shard_map/ppermute | solution.py:171
  22.6 5.5 %collective-permute-start.3 = (f32[32,1024]{1,0:T(8,128)}, f32[32,1024]{1,0:T(8,128)S(1)}, u32[]{:S(2)}, u32[]{:S(2)}) collective-permute-start(f32[32,1024]{1,0:T(8,128)} %get-tuple-element.15.refs_0_), channel_id=1, source_target_pairs={{0,16},{4,20},{8,24},{12,28},{16,0},{20,4},{24,8},{28,12},{1,17},{... | collective-permute-start | bytes 393224 | tf_op jit(solution)/shard_map/ppermute | solution.py:171
  28.1 0.0 all-to-all-done
  28.1 2.3 %collective-permute-start = (f32[4,32,1024]{2,1,0:T(8,128)S(1)}, f32[4,32,1024]{2,1,0:T(8,128)S(1)}, u32[]{:S(2)}, u32[]{:S(2)}) collective-permute-start(f32[4,32,1024]{2,1,0:T(8,128)S(1)} %all-to-all-done), channel_id=1, source_target_pairs={{0,98},{1,3},{2,0},{3,33},{32,2},{33,35},{34,32},{35,65},{64,34},{... | collective-permute-start | bytes 1572872 | tf_op jit(solution)/shard_map/ppermute | solution.py:171
  30.4 0.0 collective-permute-done.2.refs_2_
  30.4 2.1 %collective-permute-done.3.refs_3_ = f32[32,1024]{1,0:T(8,128)S(1)} collective-permute-done((f32[32,1024]{1,0:T(8,128)}, f32[32,1024]{1,0:T(8,128)S(1)}, u32[]{:S(2)}, u32[]{:S(2)}) %collective-permute-start.3) | collective-permute-done | bytes 131104 | tf_op jit(solution)/shard_map/ppermute | solution.py:171
  32.6 0.7 copy-done.2
  33.2 2.6 %shard_map.42 = f32[4,4,32,1024]{3,2,1,0:T(8,128)} custom-call(f32[32,1024]{1,0:T(8,128)} %get-tuple-element.15.refs_0_, f32[32,1024]{1,0:T(8,128)} %copy-done, f32[32,1024]{1,0:T(8,128)} %copy-done.1, f32[32,1024]{1,0:T(8,128)} %copy-done.2), custom_call_target="tpu_custom_call" | custom-call | tf_op jit(solution)/shard_map/pallas_call | solution.py:148
  35.8 4.0 %all-to-all-start.1 = ((f32[4,4,32,1024]{3,2,1,0:T(8,128)}), f32[4,4,32,1024]{3,2,1,0:T(8,128)S(1)}, u32[]{:S(2)}, u32[]{:S(2)}) async-start(f32[4,4,32,1024]{3,2,1,0:T(8,128)} %shard_map.42), calls=%async_computation.1 | async-start | bytes 4194304 | tf_op jit(solution)/shard_map/all_to_all | solution.py:175
  39.8 0.8 constant_dynamic-update-slice_fusion.1
  40.6 0.0 collective-permute-done
  40.6 0.8 constant_dynamic-update-slice_fusion.first_ref
  41.5 8.2 %collective-permute-start.4 = (f32[8,32,1024]{2,1,0:T(8,128)}, f32[8,32,1024]{2,1,0:T(8,128)}, u32[]{:S(2)}, u32[]{:S(2)}) collective-permute-start(f32[8,32,1024]{2,1,0:T(8,128)} %constant_dynamic-update-slice_fusion.first_ref), channel_id=1, source_target_pairs={{0,28},{1,5},{4,0},{5,9},{8,4},{9,13},{12,8},{13,17},{16,12},{17,2... | collective-permute-start | bytes 3145736 | tf_op jit(solution)/shard_map/ppermute | solution.py:171
  49.7 3.3 %collective-permute-start.5 = (f32[8,32,1024]{2,1,0:T(8,128)}, f32[8,32,1024]{2,1,0:T(8,128)}, u32[]{:S(2)}, u32[]{:S(2)}) collective-permute-start(f32[8,32,1024]{2,1,0:T(8,128)} %constant_dynamic-update-slice_fusion.first_ref), channel_id=1, source_target_pairs={{0,1},{1,0},{2,3},{3,2},{4,5},{5,4},{6,7},{7,6},{8,9},{9,8},{10,11... | collective-permute-start | bytes 3145736 | tf_op jit(solution)/shard_map/ppermute | solution.py:171
  53.0 8.8 %collective-permute-done.4.second_ref = f32[8,32,1024]{2,1,0:T(8,128)} collective-permute-done((f32[8,32,1024]{2,1,0:T(8,128)}, f32[8,32,1024]{2,1,0:T(8,128)}, u32[]{:S(2)}, u32[]{:S(2)}) %collective-permute-start.4) | collective-permute-done | bytes 1048608 | tf_op jit(solution)/shard_map/ppermute | solution.py:171
  61.7 7.2 %collective-permute-start.6 = (f32[8,32,1024]{2,1,0:T(8,128)}, f32[8,32,1024]{2,1,0:T(8,128)}, u32[]{:S(2)}, u32[]{:S(2)}) collective-permute-start(f32[8,32,1024]{2,1,0:T(8,128)} %collective-permute-done.4.second_ref), channel_id=1, source_target_pairs={{0,1},{1,0},{2,3},{3,2},{4,5},{5,4},{6,7},{7,6},{8,9},{9,8},{10,11... | collective-permute-start | bytes 3145736 | tf_op jit(solution)/shard_map/ppermute | solution.py:171
  69.0 0.1 pad_add_fusion.place_ref
  69.1 4.9 %shard_map.43 = (f32[2,8,16,1024]{3,2,1,0:T(8,128)S(1)}, f32[8,128]{1,0:T(8,128)S(1)}, bf16[2,256,1024]{2,1,0:T(8,128)(2,1)S(1)}, bf16[2,256,1024]{2,1,0:T(8,128)(2,1)S(1)}, f32[2,8,256]{2,1,0:T(8,128)S(1)}) custom-call(s32[2]{0:T(128)S(1)} %pad_add_fusion.place_ref, f32[8,32,1024]{2,1,0:T(8,128)} %constant_dynamic-update-slice_fusion.first_ref, ...), custom_call_target="tpu_custom_call" | custom-call | flops 6000000000 | bytes 4000000 | tf_op jit(solution)/shard_map/pallas_call | solution.py:116
  74.0 0.0 collective-permute-done.6.second_ref
  74.0 4.8 %shard_map.44 = (f32[2,8,16,1152]{3,2,1,0:T(8,128)S(1)}, f32[8,128]{1,0:T(8,128)S(1)}) custom-call(s32[2]{0:T(128)S(1)} %pad_add_fusion.place_ref, f32[8,32,1024]{2,1,0:T(8,128)} %collective-permute-done.5.first_ref, f32[8,32,1024]{2,1,0:T(8,128)} %collective-permute-done.6.second_ref, bf16[2,256,1024]{2,1,0:T(8,128)(2,1)S(1)} %get-tuple-element.20.refs_0_, ...), custom_call_target="tpu_custom_call" | custom-call | flops 2000000000 | bytes 4000000 | tf_op jit(solution)/shard_map/pallas_call | solution.py:116
  78.8 1.9 %collective-permute-start.7 = (f32[2,8,16,1152]{3,2,1,0:T(8,128)S(1)}, f32[2,8,16,1152]{3,2,1,0:T(8,128)S(1)}, u32[]{:S(2)}, u32[]{:S(2)}) collective-permute-start(f32[2,8,16,1152]{3,2,1,0:T(8,128)S(1)} %get-tuple-element.24), channel_id=1, source_target_pairs={{0,1},{1,0},{2,3},{3,2},{4,5},{5,4},{6,7},{7,6},{8,9},{9,8},{10,11... | collective-permute-start | bytes 3538952 | tf_op jit(solution)/shard_map/ppermute | solution.py:171
  80.8 2.8 %collective-permute-done.7 = f32[2,8,16,1152]{3,2,1,0:T(8,128)S(1)} collective-permute-done((f32[2,8,16,1152]{3,2,1,0:T(8,128)S(1)}, f32[2,8,16,1152]{3,2,1,0:T(8,128)S(1)}, u32[]{:S(2)}, u32[]{:S(2)}) %collective-permute-start.7) | collective-permute-done | bytes 1179680 | tf_op jit(solution)/shard_map/ppermute | solution.py:171
  83.6 0.1 fusion
  83.6 5.0 %collective-permute-start.8 = (f32[8,16,1024]{2,1,0:T(8,128)S(1)}, f32[8,16,1024]{2,1,0:T(8,128)S(1)}, u32[]{:S(2)}, u32[]{:S(2)}) collective-permute-start(f32[8,16,1024]{2,1,0:T(8,128)S(1)} %fusion), channel_id=1, source_target_pairs={{0,4},{1,29},{4,8},{5,1},{8,12},{9,5},{12,16},{13,9},{16,20},{17,1... | collective-permute-start | bytes 1572872 | tf_op jit(solution)/shard_map/ppermute | solution.py:171
  88.7 15.3 %all_to_all.20 = f32[32,1,128]{2,1,0:T(1,128)S(1)} all-to-all(f32[32,1,128]{2,1,0:T(1,128)S(1)} %broadcast_in_dim.7), channel_id=1, replica_groups=mesh['x'=4,'yh'=4,'zh'=4,'zl'=2,'yl'=2,'c'=2] {'x','zh','zl'}, dimensions={0} | all-to-all | bytes 32768 | tf_op jit(solution)/shard_map/all_to_all | solution.py:175
  104.1 0.1 fusion.2
  104.2 24.7 %all_to_all.21 = f32[8,16,1152]{2,1,0:T(8,128)S(1)} all-to-all(f32[8,16,1152]{2,1,0:T(8,128)S(1)} %pad_maximum_fusion), channel_id=1, replica_groups=mesh['x'=4,'yh'=4,'zh'=4,'zl'=2,'yl'=2,'c'=2] {'yh','yl'}, dimensions={0} | all-to-all | bytes 1179648 | tf_op jit(solution)/shard_map/all_to_all | solution.py:175
  128.9 0.7 slice_reduce_fusion
  129.5 0.5 slice_reduce_fusion.1
  (14 shorter events, 0.1 us)
Async XLA Ops:
  2.4 25.7 %all-to-all-start = ((f32[4,32,1024]{2,1,0:T(8,128)}), f32[4,32,1024]{2,1,0:T(8,128)S(1)}, u32[]{:S(2)}, u32[]{:S(2)}) async-start(f32[4,32,1024]{2,1,0:T(8,128)} %get-tuple-element.14), calls=%async_computation | async-start | bytes 1048576 | tf_op jit(solution)/shard_map/all_to_all | solution.py:175
  10.0 20.4 %collective-permute-start.1 = (f32[32,1024]{1,0:T(8,128)}, f32[32,1024]{1,0:T(8,128)S(1)}, u32[]{:S(2)}, u32[]{:S(2)}) collective-permute-start(f32[32,1024]{1,0:T(8,128)} %get-tuple-element.15.refs_0_), channel_id=1, source_target_pairs={{0,8},{4,12},{8,16},{12,20},{16,24},{20,28},{24,0},{28,4},{1,9},{5... | collective-permute-start | bytes 393224 | tf_op jit(solution)/shard_map/ppermute | solution.py:171
  15.8 14.6 %collective-permute-start.2 = (f32[32,1024]{1,0:T(8,128)}, f32[32,1024]{1,0:T(8,128)S(1)}, u32[]{:S(2)}, u32[]{:S(2)}) collective-permute-start(f32[32,1024]{1,0:T(8,128)} %get-tuple-element.15.refs_0_), channel_id=1, source_target_pairs={{0,24},{4,28},{8,0},{12,4},{16,8},{20,12},{24,16},{28,20},{1,25},{... | collective-permute-start | bytes 393224 | tf_op jit(solution)/shard_map/ppermute | solution.py:171
  22.6 9.9 %collective-permute-start.3 = (f32[32,1024]{1,0:T(8,128)}, f32[32,1024]{1,0:T(8,128)S(1)}, u32[]{:S(2)}, u32[]{:S(2)}) collective-permute-start(f32[32,1024]{1,0:T(8,128)} %get-tuple-element.15.refs_0_), channel_id=1, source_target_pairs={{0,16},{4,20},{8,24},{12,28},{16,0},{20,4},{24,8},{28,12},{1,17},{... | collective-permute-start | bytes 393224 | tf_op jit(solution)/shard_map/ppermute | solution.py:171
  28.1 12.5 %collective-permute-start = (f32[4,32,1024]{2,1,0:T(8,128)S(1)}, f32[4,32,1024]{2,1,0:T(8,128)S(1)}, u32[]{:S(2)}, u32[]{:S(2)}) collective-permute-start(f32[4,32,1024]{2,1,0:T(8,128)S(1)} %all-to-all-done), channel_id=1, source_target_pairs={{0,98},{1,3},{2,0},{3,33},{32,2},{33,35},{34,32},{35,65},{64,34},{... | collective-permute-start | bytes 1572872 | tf_op jit(solution)/shard_map/ppermute | solution.py:171
  30.4 2.1 %copy-start = (f32[32,1024]{1,0:T(8,128)}, f32[32,1024]{1,0:T(8,128)S(1)}, u32[]{:S(2)}) copy-start(f32[32,1024]{1,0:T(8,128)S(1)} %collective-permute-done.1.refs_1_) | copy-start | bytes 393220
  30.4 2.1 %copy-start.1 = (f32[32,1024]{1,0:T(8,128)}, f32[32,1024]{1,0:T(8,128)S(1)}, u32[]{:S(2)}) copy-start(f32[32,1024]{1,0:T(8,128)S(1)} %collective-permute-done.2.refs_2_) | copy-start | bytes 393220
  32.6 0.7 copy-start.2
  35.8 26.0 %all-to-all-start.1 = ((f32[4,4,32,1024]{3,2,1,0:T(8,128)}), f32[4,4,32,1024]{3,2,1,0:T(8,128)S(1)}, u32[]{:S(2)}, u32[]{:S(2)}) async-start(f32[4,4,32,1024]{3,2,1,0:T(8,128)} %shard_map.42), calls=%async_computation.1 | async-start | bytes 4194304 | tf_op jit(solution)/shard_map/all_to_all | solution.py:175
  41.5 20.3 %collective-permute-start.4 = (f32[8,32,1024]{2,1,0:T(8,128)}, f32[8,32,1024]{2,1,0:T(8,128)}, u32[]{:S(2)}, u32[]{:S(2)}) collective-permute-start(f32[8,32,1024]{2,1,0:T(8,128)} %constant_dynamic-update-slice_fusion.first_ref), channel_id=1, source_target_pairs={{0,28},{1,5},{4,0},{5,9},{8,4},{9,13},{12,8},{13,17},{16,12},{17,2... | collective-permute-start | bytes 3145736 | tf_op jit(solution)/shard_map/ppermute | solution.py:171
  49.7 24.3 %collective-permute-start.5 = (f32[8,32,1024]{2,1,0:T(8,128)}, f32[8,32,1024]{2,1,0:T(8,128)}, u32[]{:S(2)}, u32[]{:S(2)}) collective-permute-start(f32[8,32,1024]{2,1,0:T(8,128)} %constant_dynamic-update-slice_fusion.first_ref), channel_id=1, source_target_pairs={{0,1},{1,0},{2,3},{3,2},{4,5},{5,4},{6,7},{7,6},{8,9},{9,8},{10,11... | collective-permute-start | bytes 3145736 | tf_op jit(solution)/shard_map/ppermute | solution.py:171
  61.7 12.2 %collective-permute-start.6 = (f32[8,32,1024]{2,1,0:T(8,128)}, f32[8,32,1024]{2,1,0:T(8,128)}, u32[]{:S(2)}, u32[]{:S(2)}) collective-permute-start(f32[8,32,1024]{2,1,0:T(8,128)} %collective-permute-done.4.second_ref), channel_id=1, source_target_pairs={{0,1},{1,0},{2,3},{3,2},{4,5},{5,4},{6,7},{7,6},{8,9},{9,8},{10,11... | collective-permute-start | bytes 3145736 | tf_op jit(solution)/shard_map/ppermute | solution.py:171
  78.8 4.7 %collective-permute-start.7 = (f32[2,8,16,1152]{3,2,1,0:T(8,128)S(1)}, f32[2,8,16,1152]{3,2,1,0:T(8,128)S(1)}, u32[]{:S(2)}, u32[]{:S(2)}) collective-permute-start(f32[2,8,16,1152]{3,2,1,0:T(8,128)S(1)} %get-tuple-element.24), channel_id=1, source_target_pairs={{0,1},{1,0},{2,3},{3,2},{4,5},{5,4},{6,7},{7,6},{8,9},{9,8},{10,11... | collective-permute-start | bytes 3538952 | tf_op jit(solution)/shard_map/ppermute | solution.py:171
  83.6 20.4 %collective-permute-start.8 = (f32[8,16,1024]{2,1,0:T(8,128)S(1)}, f32[8,16,1024]{2,1,0:T(8,128)S(1)}, u32[]{:S(2)}, u32[]{:S(2)}) collective-permute-start(f32[8,16,1024]{2,1,0:T(8,128)S(1)} %fusion), channel_id=1, source_target_pairs={{0,4},{1,29},{4,8},{5,1},{8,12},{9,5},{12,16},{13,9},{16,20},{17,1... | collective-permute-start | bytes 1572872 | tf_op jit(solution)/shard_map/ppermute | solution.py:171

commit v11 on v9

--- a/solution.py
+++ b/solution.py
@@ -39,10 +39,10 @@
 
 
 def product(left, right, dims):
-    def dot(a, b):
-        return lax.dot_general(a, b, dims, preferred_element_type=jnp.float32)
-
-    return dot(left[0], right[0]) + (dot(left[0], right[1]) + dot(left[1], right[0]))
+    (left_at,), (right_at,) = dims[0]
+    left = jnp.concatenate([left[0], left[0], left[1]], axis=left_at)
+    right = jnp.concatenate([right[0], right[1], right[0]], axis=right_at)
+    return lax.dot_general(left, right, dims, preferred_element_type=jnp.float32)
 
 
 def flat(block):

time: 131 us -> 133 us (1.015)
  Pallas kernels: 11.3 us -> 12.9 us
    pallas_call x2, Pallas kernels: 9.58 us -> 11.1 us  [pairs(): pl.pallas_call(pair_kernel, out_shape=(shape(2, LINE, OWN, WIDTH + extra)...]
where the time goes in v11:
time: 133 us; the launch traced here: 132 us
  starting transfers between devices  56.6 us (43%)
  blocking collectives  40.6 us (31%)
  waiting for transfers between devices  14.1 us (11%)
  Pallas kernels  12.9 us (10%)
  other arithmetic  3.46 us (3%)
  local copies, waits for them, and re-layouts  3.31 us (2%)
    ppermute x9, starting transfers between devices, sent(): return lax.ppermute(value, axes, perm)  45 us
    all_to_all x2, blocking collectives, exchanged(): return lax.all_to_all(value, axes, split_axis=0, concat_axis=0, tiled=True)  40.6 us
    ppermute x9, waiting for transfers between devices, sent(): return lax.ppermute(value, axes, perm)  14 us
    all_to_all x2, starting transfers between devices, exchanged(): return lax.all_to_all(value, axes, split_axis=0, concat_axis=0, tiled=True)  11.7 us
    pallas_call x2, Pallas kernels, pairs(): pl.pallas_call(pair_kernel, out_shape=(shape(2, LINE, OWN, WIDTH + extra)...  11.1 us
  transfers between devices with their start and end apart: 11, of which 3 were waited for; matrix products, arithmetic and copies ran while one was open for 3% of the time, Pallas kernels for 4%

profile of v11, /device:TPU:1, one launch (start us, length us, event | category | flops | bytes accessed | tf_op | source)
XLA Modules:
  0.0 131.8 jit_solution(6241548584420507345)
XLA Ops:
  0.6 1.8 %shard_map.41 = (f32[32,1024]{1,0:T(8,128)}, f32[4,32,1024]{2,1,0:T(8,128)}) custom-call(f32[16,1024]{1,0:T(8,128)} %gen_ref.1, f32[16,1024]{1,0:T(8,128)} %data_ref.1), custom_call_target="tpu_custom_call" | custom-call | tf_op jit(solution)/shard_map/pallas_call | solution.py:119
  2.4 7.6 %all-to-all-start = ((f32[4,32,1024]{2,1,0:T(8,128)}), f32[4,32,1024]{2,1,0:T(8,128)S(1)}, u32[]{:S(2)}, u32[]{:S(2)}) async-start(f32[4,32,1024]{2,1,0:T(8,128)} %get-tuple-element.11), calls=%async_computation | async-start | bytes 1048576 | tf_op jit(solution)/shard_map/all_to_all | solution.py:146
  10.0 5.8 %collective-permute-start.1 = (f32[32,1024]{1,0:T(8,128)}, f32[32,1024]{1,0:T(8,128)S(1)}, u32[]{:S(2)}, u32[]{:S(2)}) collective-permute-start(f32[32,1024]{1,0:T(8,128)} %get-tuple-element.12), channel_id=1, source_target_pairs={{0,8},{4,12},{8,16},{12,20},{16,24},{20,28},{24,0},{28,4},{1,9},{5... | collective-permute-start | bytes 393224 | tf_op jit(solution)/shard_map/ppermute | solution.py:142
  15.8 6.8 %collective-permute-start.2 = (f32[32,1024]{1,0:T(8,128)}, f32[32,1024]{1,0:T(8,128)S(1)}, u32[]{:S(2)}, u32[]{:S(2)}) collective-permute-start(f32[32,1024]{1,0:T(8,128)} %get-tuple-element.12), channel_id=1, source_target_pairs={{0,24},{4,28},{8,0},{12,4},{16,8},{20,12},{24,16},{28,20},{1,25},{... | collective-permute-start | bytes 393224 | tf_op jit(solution)/shard_map/ppermute | solution.py:142
  22.6 5.5 %collective-permute-start.3 = (f32[32,1024]{1,0:T(8,128)}, f32[32,1024]{1,0:T(8,128)S(1)}, u32[]{:S(2)}, u32[]{:S(2)}) collective-permute-start(f32[32,1024]{1,0:T(8,128)} %get-tuple-element.12), channel_id=1, source_target_pairs={{0,16},{4,20},{8,24},{12,28},{16,0},{20,4},{24,8},{28,12},{1,17},{... | collective-permute-start | bytes 393224 | tf_op jit(solution)/shard_map/ppermute | solution.py:142
  28.1 0.0 all-to-all-done
  28.1 2.3 %collective-permute-start = (f32[4,32,1024]{2,1,0:T(8,128)S(1)}, f32[4,32,1024]{2,1,0:T(8,128)S(1)}, u32[]{:S(2)}, u32[]{:S(2)}) collective-permute-start(f32[4,32,1024]{2,1,0:T(8,128)S(1)} %all-to-all-done), channel_id=1, source_target_pairs={{0,98},{1,3},{2,0},{3,33},{32,2},{33,35},{34,32},{35,65},{64,34},{... | collective-permute-start | bytes 1572872 | tf_op jit(solution)/shard_map/ppermute | solution.py:142
  30.4 2.1 %collective-permute-done.3 = f32[32,1024]{1,0:T(8,128)S(1)} collective-permute-done((f32[32,1024]{1,0:T(8,128)}, f32[32,1024]{1,0:T(8,128)S(1)}, u32[]{:S(2)}, u32[]{:S(2)}) %collective-permute-start.3) | collective-permute-done | bytes 131104 | tf_op jit(solution)/shard_map/ppermute | solution.py:142
  32.5 0.9 pad_maximum_fusion.1
  33.5 1.6 %broadcast_in_dim.8 = f32[4,4,32,1024]{3,2,1,0:T(8,128)} broadcast(f32[4,32,1024]{2,1,0:T(8,128)S(1)} %pad_maximum_fusion.1), dimensions={1,2,3} | broadcast | bytes 2621440 | tf_op jit(solution)/shard_map/broadcast_in_dim | solution.py:173
  35.1 4.0 %all-to-all-start.1 = ((f32[4,4,32,1024]{3,2,1,0:T(8,128)}), f32[4,4,32,1024]{3,2,1,0:T(8,128)S(1)}, u32[]{:S(2)}, u32[]{:S(2)}) async-start(f32[4,4,32,1024]{3,2,1,0:T(8,128)} %broadcast_in_dim.8), calls=%async_computation.1 | async-start | bytes 4194304 | tf_op jit(solution)/shard_map/all_to_all | solution.py:146
  39.1 0.8 constant_dynamic-update-slice_fusion.1
  40.0 0.0 collective-permute-done
  40.0 0.8 constant_dynamic-update-slice_fusion.first_ref
  40.8 8.2 %collective-permute-start.4 = (f32[8,32,1024]{2,1,0:T(8,128)}, f32[8,32,1024]{2,1,0:T(8,128)}, u32[]{:S(2)}, u32[]{:S(2)}) collective-permute-start(f32[8,32,1024]{2,1,0:T(8,128)} %constant_dynamic-update-slice_fusion.first_ref), channel_id=1, source_target_pairs={{0,28},{1,5},{4,0},{5,9},{8,4},{9,13},{12,8},{13,17},{16,12},{17,2... | collective-permute-start | bytes 3145736 | tf_op jit(solution)/shard_map/ppermute | solution.py:142
  49.0 2.9 %collective-permute-start.5 = (f32[8,32,1024]{2,1,0:T(8,128)}, f32[8,32,1024]{2,1,0:T(8,128)}, u32[]{:S(2)}, u32[]{:S(2)}) collective-permute-start(f32[8,32,1024]{2,1,0:T(8,128)} %constant_dynamic-update-slice_fusion.first_ref), channel_id=1, source_target_pairs={{0,1},{1,0},{2,3},{3,2},{4,5},{5,4},{6,7},{7,6},{8,9},{9,8},{10,11... | collective-permute-start | bytes 3145736 | tf_op jit(solution)/shard_map/ppermute | solution.py:142
  52.0 9.1 %collective-permute-done.4.second_ref = f32[8,32,1024]{2,1,0:T(8,128)} collective-permute-done((f32[8,32,1024]{2,1,0:T(8,128)}, f32[8,32,1024]{2,1,0:T(8,128)}, u32[]{:S(2)}, u32[]{:S(2)}) %collective-permute-start.4) | collective-permute-done | bytes 1048608 | tf_op jit(solution)/shard_map/ppermute | solution.py:142
  61.1 0.0 all-to-all-done.1
  61.1 7.2 %collective-permute-start.6 = (f32[8,32,1024]{2,1,0:T(8,128)}, f32[8,32,1024]{2,1,0:T(8,128)}, u32[]{:S(2)}, u32[]{:S(2)}) collective-permute-start(f32[8,32,1024]{2,1,0:T(8,128)} %collective-permute-done.4.second_ref), channel_id=1, source_target_pairs={{0,1},{1,0},{2,3},{3,2},{4,5},{5,4},{6,7},{7,6},{8,9},{9,8},{10,11... | collective-permute-start | bytes 3145736 | tf_op jit(solution)/shard_map/ppermute | solution.py:142
  68.3 0.1 pad_add_fusion.place_ref
  68.4 5.5 %shard_map.42 = (f32[2,8,16,1024]{3,2,1,0:T(8,128)S(1)}, f32[8,128]{1,0:T(8,128)S(1)}) custom-call(s32[2]{0:T(128)S(1)} %pad_add_fusion.place_ref, f32[8,32,1024]{2,1,0:T(8,128)} %constant_dynamic-update-slice_fusion.first_ref, f32[8,32,1024]{2,1,0:T(8,128)} %collective-permute-done.4.second_ref, f32[16,32,1024]{2,1,0:T(8,128)S(1)} %bitcast.24), custom_call_target="tpu_custom_call" | custom-call | flops 6000000000 | bytes 4000000 | tf_op jit(solution)/shard_map/pallas_call | solution.py:102
  74.0 0.0 collective-permute-done.5.first_ref
  74.0 5.6 %shard_map.43 = (f32[2,8,16,1152]{3,2,1,0:T(8,128)S(1)}, f32[8,128]{1,0:T(8,128)S(1)}) custom-call(s32[2]{0:T(128)S(1)} %pad_add_fusion.place_ref, f32[8,32,1024]{2,1,0:T(8,128)} %collective-permute-done.5.first_ref, f32[8,32,1024]{2,1,0:T(8,128)} %collective-permute-done.6.second_ref, f32[16,32,1024]{2,1,0:T(8,128)S(1)} %bitcast.25, ...), custom_call_target="tpu_custom_call" | custom-call | flops 2000000000 | bytes 4000000 | tf_op jit(solution)/shard_map/pallas_call | solution.py:102
  79.5 1.9 %collective-permute-start.7 = (f32[2,8,16,1152]{3,2,1,0:T(8,128)S(1)}, f32[2,8,16,1152]{3,2,1,0:T(8,128)S(1)}, u32[]{:S(2)}, u32[]{:S(2)}) collective-permute-start(f32[2,8,16,1152]{3,2,1,0:T(8,128)S(1)} %get-tuple-element.18), channel_id=1, source_target_pairs={{0,1},{1,0},{2,3},{3,2},{4,5},{5,4},{6,7},{7,6},{8,9},{9,8},{10,11... | collective-permute-start | bytes 3538952 | tf_op jit(solution)/shard_map/ppermute | solution.py:142
  81.5 2.8 %collective-permute-done.7 = f32[2,8,16,1152]{3,2,1,0:T(8,128)S(1)} collective-permute-done((f32[2,8,16,1152]{3,2,1,0:T(8,128)S(1)}, f32[2,8,16,1152]{3,2,1,0:T(8,128)S(1)}, u32[]{:S(2)}, u32[]{:S(2)}) %collective-permute-start.7) | collective-permute-done | bytes 1179680 | tf_op jit(solution)/shard_map/ppermute | solution.py:142
  84.3 0.1 fusion
  84.4 4.3 %collective-permute-start.8 = (f32[8,16,1024]{2,1,0:T(8,128)S(1)}, f32[8,16,1024]{2,1,0:T(8,128)}, u32[]{:S(2)}, u32[]{:S(2)}) collective-permute-start(f32[8,16,1024]{2,1,0:T(8,128)S(1)} %fusion), channel_id=1, source_target_pairs={{0,4},{1,29},{4,8},{5,1},{8,12},{9,5},{12,16},{13,9},{16,20},{17,1... | collective-permute-start | bytes 1572872 | tf_op jit(solution)/shard_map/ppermute | solution.py:142
  88.7 16.0 %all_to_all.20 = f32[32,1,128]{2,1,0:T(1,128)S(1)} all-to-all(f32[32,1,128]{2,1,0:T(1,128)S(1)} %broadcast_in_dim.10), channel_id=1, replica_groups=mesh['x'=4,'yh'=4,'zh'=4,'zl'=2,'yl'=2,'c'=2] {'x','zh','zl'}, dimensions={0} | all-to-all | bytes 32768 | tf_op jit(solution)/shard_map/all_to_all | solution.py:146
  104.8 1.1 fusion.2
  106.0 24.6 %all_to_all.21 = f32[8,16,1152]{2,1,0:T(8,128)S(1)} all-to-all(f32[8,16,1152]{2,1,0:T(8,128)S(1)} %pad_maximum_fusion), channel_id=1, replica_groups=mesh['x'=4,'yh'=4,'zh'=4,'zl'=2,'yl'=2,'c'=2] {'yh','yl'}, dimensions={0} | all-to-all | bytes 1179648 | tf_op jit(solution)/shard_map/all_to_all | solution.py:146
  130.6 0.7 slice_reduce_fusion
  131.3 0.5 slice_reduce_fusion.1
  (9 shorter events, 0.1 us)
Async XLA Ops:
  2.4 25.7 %all-to-all-start = ((f32[4,32,1024]{2,1,0:T(8,128)}), f32[4,32,1024]{2,1,0:T(8,128)S(1)}, u32[]{:S(2)}, u32[]{:S(2)}) async-start(f32[4,32,1024]{2,1,0:T(8,128)} %get-tuple-element.11), calls=%async_computation | async-start | bytes 1048576 | tf_op jit(solution)/shard_map/all_to_all | solution.py:146
  10.0 20.4 %collective-permute-start.1 = (f32[32,1024]{1,0:T(8,128)}, f32[32,1024]{1,0:T(8,128)S(1)}, u32[]{:S(2)}, u32[]{:S(2)}) collective-permute-start(f32[32,1024]{1,0:T(8,128)} %get-tuple-element.12), channel_id=1, source_target_pairs={{0,8},{4,12},{8,16},{12,20},{16,24},{20,28},{24,0},{28,4},{1,9},{5... | collective-permute-start | bytes 393224 | tf_op jit(solution)/shard_map/ppermute | solution.py:142
  15.8 14.6 %collective-permute-start.2 = (f32[32,1024]{1,0:T(8,128)}, f32[32,1024]{1,0:T(8,128)S(1)}, u32[]{:S(2)}, u32[]{:S(2)}) collective-permute-start(f32[32,1024]{1,0:T(8,128)} %get-tuple-element.12), channel_id=1, source_target_pairs={{0,24},{4,28},{8,0},{12,4},{16,8},{20,12},{24,16},{28,20},{1,25},{... | collective-permute-start | bytes 393224 | tf_op jit(solution)/shard_map/ppermute | solution.py:142
  22.6 9.9 %collective-permute-start.3 = (f32[32,1024]{1,0:T(8,128)}, f32[32,1024]{1,0:T(8,128)S(1)}, u32[]{:S(2)}, u32[]{:S(2)}) collective-permute-start(f32[32,1024]{1,0:T(8,128)} %get-tuple-element.12), channel_id=1, source_target_pairs={{0,16},{4,20},{8,24},{12,28},{16,0},{20,4},{24,8},{28,12},{1,17},{... | collective-permute-start | bytes 393224 | tf_op jit(solution)/shard_map/ppermute | solution.py:142
  28.1 11.9 %collective-permute-start = (f32[4,32,1024]{2,1,0:T(8,128)S(1)}, f32[4,32,1024]{2,1,0:T(8,128)S(1)}, u32[]{:S(2)}, u32[]{:S(2)}) collective-permute-start(f32[4,32,1024]{2,1,0:T(8,128)S(1)} %all-to-all-done), channel_id=1, source_target_pairs={{0,98},{1,3},{2,0},{3,33},{32,2},{33,35},{34,32},{35,65},{64,34},{... | collective-permute-start | bytes 1572872 | tf_op jit(solution)/shard_map/ppermute | solution.py:142
  35.1 26.0 %all-to-all-start.1 = ((f32[4,4,32,1024]{3,2,1,0:T(8,128)}), f32[4,4,32,1024]{3,2,1,0:T(8,128)S(1)}, u32[]{:S(2)}, u32[]{:S(2)}) async-start(f32[4,4,32,1024]{3,2,1,0:T(8,128)} %broadcast_in_dim.8), calls=%async_computation.1 | async-start | bytes 4194304 | tf_op jit(solution)/shard_map/all_to_all | solution.py:146
  40.8 20.3 %collective-permute-start.4 = (f32[8,32,1024]{2,1,0:T(8,128)}, f32[8,32,1024]{2,1,0:T(8,128)}, u32[]{:S(2)}, u32[]{:S(2)}) collective-permute-start(f32[8,32,1024]{2,1,0:T(8,128)} %constant_dynamic-update-slice_fusion.first_ref), channel_id=1, source_target_pairs={{0,28},{1,5},{4,0},{5,9},{8,4},{9,13},{12,8},{13,17},{16,12},{17,2... | collective-permute-start | bytes 3145736 | tf_op jit(solution)/shard_map/ppermute | solution.py:142
  49.0 24.9 %collective-permute-start.5 = (f32[8,32,1024]{2,1,0:T(8,128)}, f32[8,32,1024]{2,1,0:T(8,128)}, u32[]{:S(2)}, u32[]{:S(2)}) collective-permute-start(f32[8,32,1024]{2,1,0:T(8,128)} %constant_dynamic-update-slice_fusion.first_ref), channel_id=1, source_target_pairs={{0,1},{1,0},{2,3},{3,2},{4,5},{5,4},{6,7},{7,6},{8,9},{9,8},{10,11... | collective-permute-start | bytes 3145736 | tf_op jit(solution)/shard_map/ppermute | solution.py:142
  61.1 12.9 %collective-permute-start.6 = (f32[8,32,1024]{2,1,0:T(8,128)}, f32[8,32,1024]{2,1,0:T(8,128)}, u32[]{:S(2)}, u32[]{:S(2)}) collective-permute-start(f32[8,32,1024]{2,1,0:T(8,128)} %collective-permute-done.4.second_ref), channel_id=1, source_target_pairs={{0,1},{1,0},{2,3},{3,2},{4,5},{5,4},{6,7},{7,6},{8,9},{9,8},{10,11... | collective-permute-start | bytes 3145736 | tf_op jit(solution)/shard_map/ppermute | solution.py:142
  79.5 4.7 %collective-permute-start.7 = (f32[2,8,16,1152]{3,2,1,0:T(8,128)S(1)}, f32[2,8,16,1152]{3,2,1,0:T(8,128)S(1)}, u32[]{:S(2)}, u32[]{:S(2)}) collective-permute-start(f32[2,8,16,1152]{3,2,1,0:T(8,128)S(1)} %get-tuple-element.18), channel_id=1, source_target_pairs={{0,1},{1,0},{2,3},{3,2},{4,5},{5,4},{6,7},{7,6},{8,9},{9,8},{10,11... | collective-permute-start | bytes 3538952 | tf_op jit(solution)/shard_map/ppermute | solution.py:142
  84.4 20.4 %collective-permute-start.8 = (f32[8,16,1024]{2,1,0:T(8,128)S(1)}, f32[8,16,1024]{2,1,0:T(8,128)}, u32[]{:S(2)}, u32[]{:S(2)}) collective-permute-start(f32[8,16,1024]{2,1,0:T(8,128)S(1)} %fusion), channel_id=1, source_target_pairs={{0,4},{1,29},{4,8},{5,1},{8,12},{9,5},{12,16},{13,9},{16,20},{17,1... | collective-permute-start | bytes 1572872 | tf_op jit(solution)/shard_map/ppermute | solution.py:142

commit v12 on v9

--- a/solution.py
+++ b/solution.py
@@ -168,9 +168,10 @@
 def body(generated, data):
     own, copies = spread(generated, data)
     line = exchanged(copies, ("yh",))
-    parity = jnp.stack([own] + [along(own, Z, steps) for steps in (2, -2, 4)])
+    parity = [own] + [along(own, Z, steps) for steps in (2, -2, 4)]
+    parity = joined(*parity * 4).reshape((4, 4) + own.shape)
     parity, _ = lax.optimization_barrier((parity, line))
-    cols = exchanged(jnp.broadcast_to(parity[None], (4,) + parity.shape), ("x",))
+    cols = exchanged(parity, ("x",))
     line = joined(line, shifted(line, Y, -1))
     near = shifted(line, Z, -1)
     line_away = swapped(line)

time: 131 us -> 136 us (1.038)
  waiting for transfers between devices: 14.1 us -> 32 us
  starting transfers between devices: 56.6 us -> 47.5 us
  blocking collectives: 40.7 us -> 36.6 us
    all_to_all x2, waiting for transfers between devices: 0.01 us -> 14.4 us  [exchanged(): return lax.all_to_all(value, axes, split_axis=0, concat_axis=0, tiled=True)]
    ppermute x9, starting transfers between devices: 45 us -> 36.6 us  [sent(): return lax.ppermute(value, axes, perm)]
    all_to_all x2, blocking collectives: 40.7 us -> 36.6 us  [exchanged(): return lax.all_to_all(value, axes, split_axis=0, concat_axis=0, tiled=True)]
    ppermute x9, waiting for transfers between devices: 14 us -> 17.6 us  [sent(): return lax.ppermute(value, axes, perm)]
    unnamed x1 -> x20, local copies, waits for them, and re-layouts: 0.84 us -> 3.26 us
    broadcast_in_dim x1 -> x0, local copies, waits for them, and re-layouts: 1.63 us -> none  [body(): jnp.broadcast_to(parity[None], (4,) + parity.shape)]
  transfers between devices with their start and end apart: 11 -> 11, of which waited for: 3 -> 5; matrix products, arithmetic and copies ran while one was open for 3% -> 2% of each run, Pallas kernels for 4% -> 4%
where the time goes in v12:
time: 136 us; the launch traced here: 135 us
  starting transfers between devices  47.5 us (35%)
  blocking collectives  36.6 us (27%)
  waiting for transfers between devices  32 us (24%)
  Pallas kernels  11.3 us (8%)
  local copies, waits for them, and re-layouts  4.12 us (3%)
  other arithmetic  2.52 us (2%)
    ppermute x9, starting transfers between devices, sent(): return lax.ppermute(value, axes, perm)  36.6 us
    all_to_all x2, blocking collectives, exchanged(): return lax.all_to_all(value, axes, split_axis=0, concat_axis=0, tiled=True)  36.6 us
    ppermute x9, waiting for transfers between devices, sent(): return lax.ppermute(value, axes, perm)  17.6 us
    all_to_all x2, waiting for transfers between devices, exchanged(): return lax.all_to_all(value, axes, split_axis=0, concat_axis=0, tiled=True)  14.4 us
    all_to_all x2, starting transfers between devices, exchanged(): return lax.all_to_all(value, axes, split_axis=0, concat_axis=0, tiled=True)  10.8 us
    pallas_call x2, Pallas kernels, pairs(): pl.pallas_call(pair_kernel, out_shape=(shape(2, LINE, OWN, WIDTH + extra)...  9.57 us
    unnamed x20, local copies, waits for them, and re-layouts  3.26 us
  transfers between devices with their start and end apart: 11, of which 5 were waited for; matrix products, arithmetic and copies ran while one was open for 2% of the time, Pallas kernels for 4%

profile of v12, /device:TPU:1, one launch (start us, length us, event | category | flops | bytes accessed | tf_op | source)
XLA Modules:
  0.0 135.0 jit_solution(1308343422523802791)
XLA Ops:
  0.6 1.8 %shard_map.41 = (f32[32,1024]{1,0:T(8,128)}, f32[4,32,1024]{2,1,0:T(8,128)}) custom-call(f32[16,1024]{1,0:T(8,128)} %gen_ref.1, f32[16,1024]{1,0:T(8,128)} %data_ref.1), custom_call_target="tpu_custom_call" | custom-call | tf_op jit(solution)/shard_map/pallas_call | solution.py:119
  2.4 6.8 %collective-permute-start.1 = (f32[32,1024]{1,0:T(8,128)}, f32[32,1024]{1,0:T(8,128)S(1)}, u32[]{:S(2)}, u32[]{:S(2)}) collective-permute-start(f32[32,1024]{1,0:T(8,128)} %get-tuple-element.12), channel_id=1, source_target_pairs={{0,8},{4,12},{8,16},{12,20},{16,24},{20,28},{24,0},{28,4},{1,9},{5... | collective-permute-start | bytes 393224 | tf_op jit(solution)/shard_map/ppermute | solution.py:142
  9.1 6.8 %collective-permute-start.2 = (f32[32,1024]{1,0:T(8,128)}, f32[32,1024]{1,0:T(8,128)S(1)}, u32[]{:S(2)}, u32[]{:S(2)}) collective-permute-start(f32[32,1024]{1,0:T(8,128)} %get-tuple-element.12), channel_id=1, source_target_pairs={{0,24},{4,28},{8,0},{12,4},{16,8},{20,12},{24,16},{28,20},{1,25},{... | collective-permute-start | bytes 393224 | tf_op jit(solution)/shard_map/ppermute | solution.py:142
  15.9 5.5 %collective-permute-start.3 = (f32[32,1024]{1,0:T(8,128)}, f32[32,1024]{1,0:T(8,128)S(1)}, u32[]{:S(2)}, u32[]{:S(2)}) collective-permute-start(f32[32,1024]{1,0:T(8,128)} %get-tuple-element.12), channel_id=1, source_target_pairs={{0,16},{4,20},{8,24},{12,28},{16,0},{20,4},{24,8},{28,12},{1,17},{... | collective-permute-start | bytes 393224 | tf_op jit(solution)/shard_map/ppermute | solution.py:142
  21.4 6.8 %all-to-all-start = ((f32[4,32,1024]{2,1,0:T(8,128)}), f32[4,32,1024]{2,1,0:T(8,128)S(1)}, u32[]{:S(2)}, u32[]{:S(2)}) async-start(f32[4,32,1024]{2,1,0:T(8,128)} %get-tuple-element.11), calls=%async_computation | async-start | bytes 1048576 | tf_op jit(solution)/shard_map/all_to_all | solution.py:146
  28.2 0.9 constant_dynamic-update-slice_fusion.17
  29.4 13.6 %all-to-all-done = f32[4,32,1024]{2,1,0:T(8,128)S(1)} async-done(((f32[4,32,1024]{2,1,0:T(8,128)}), f32[4,32,1024]{2,1,0:T(8,128)S(1)}, u32[]{:S(2)}, u32[]{:S(2)}) %all-to-all-start) | async-done | bytes 524320 | tf_op jit(solution)/shard_map/all_to_all | solution.py:146
  43.0 1.9 %collective-permute-start = (f32[4,32,1024]{2,1,0:T(8,128)S(1)}, f32[4,32,1024]{2,1,0:T(8,128)S(1)}, u32[]{:S(2)}, u32[]{:S(2)}) collective-permute-start(f32[4,32,1024]{2,1,0:T(8,128)S(1)} %all-to-all-done), channel_id=1, source_target_pairs={{0,98},{1,3},{2,0},{3,33},{32,2},{33,35},{34,32},{35,65},{64,34},{... | collective-permute-start | bytes 1572872 | tf_op jit(solution)/shard_map/ppermute | solution.py:142
  45.0 1.3 copy-done
  46.3 4.0 %all-to-all-start.1 = ((f32[4,4,32,1024]{3,2,1,0:T(8,128)}), f32[4,4,32,1024]{3,2,1,0:T(8,128)S(1)}, u32[]{:S(2)}, u32[]{:S(2)}) async-start(f32[4,4,32,1024]{3,2,1,0:T(8,128)} %bitcast.23), calls=%async_computation.1 | async-start | bytes 4194304 | tf_op jit(solution)/shard_map/all_to_all | solution.py:146
  50.4 0.8 constant_dynamic-update-slice_fusion.1
  51.2 3.0 %collective-permute-done = f32[4,32,1024]{2,1,0:T(8,128)S(1)} collective-permute-done((f32[4,32,1024]{2,1,0:T(8,128)S(1)}, f32[4,32,1024]{2,1,0:T(8,128)S(1)}, u32[]{:S(2)}, u32[]{:S(2)}) %collective-permute-start) | collective-permute-done | bytes 524320 | tf_op jit(solution)/shard_map/ppermute | solution.py:142
  54.2 0.8 constant_dynamic-update-slice_fusion.first_ref
  55.0 3.1 %collective-permute-start.4 = (f32[8,32,1024]{2,1,0:T(8,128)}, f32[8,32,1024]{2,1,0:T(8,128)}, u32[]{:S(2)}, u32[]{:S(2)}) collective-permute-start(f32[8,32,1024]{2,1,0:T(8,128)} %constant_dynamic-update-slice_fusion.first_ref), channel_id=1, source_target_pairs={{0,28},{1,5},{4,0},{5,9},{8,4},{9,13},{12,8},{13,17},{16,12},{17,2... | collective-permute-start | bytes 3145736 | tf_op jit(solution)/shard_map/ppermute | solution.py:142
  58.1 2.3 %collective-permute-start.5 = (f32[8,32,1024]{2,1,0:T(8,128)}, f32[8,32,1024]{2,1,0:T(8,128)}, u32[]{:S(2)}, u32[]{:S(2)}) collective-permute-start(f32[8,32,1024]{2,1,0:T(8,128)} %constant_dynamic-update-slice_fusion.first_ref), channel_id=1, source_target_pairs={{0,1},{1,0},{2,3},{3,2},{4,5},{5,4},{6,7},{7,6},{8,9},{9,8},{10,11... | collective-permute-start | bytes 3145736 | tf_op jit(solution)/shard_map/ppermute | solution.py:142
  60.4 11.8 %collective-permute-done.4.second_ref = f32[8,32,1024]{2,1,0:T(8,128)} collective-permute-done((f32[8,32,1024]{2,1,0:T(8,128)}, f32[8,32,1024]{2,1,0:T(8,128)}, u32[]{:S(2)}, u32[]{:S(2)}) %collective-permute-start.4) | collective-permute-done | bytes 1048608 | tf_op jit(solution)/shard_map/ppermute | solution.py:142
  72.3 0.8 all-to-all-done.1
  73.1 6.5 %collective-permute-start.6 = (f32[8,32,1024]{2,1,0:T(8,128)}, f32[8,32,1024]{2,1,0:T(8,128)}, u32[]{:S(2)}, u32[]{:S(2)}) collective-permute-start(f32[8,32,1024]{2,1,0:T(8,128)} %collective-permute-done.4.second_ref), channel_id=1, source_target_pairs={{0,1},{1,0},{2,3},{3,2},{4,5},{5,4},{6,7},{7,6},{8,9},{9,8},{10,11... | collective-permute-start | bytes 3145736 | tf_op jit(solution)/shard_map/ppermute | solution.py:142
  79.5 0.1 pad_add_fusion.place_ref
  79.6 4.8 %shard_map.42 = (f32[2,8,16,1024]{3,2,1,0:T(8,128)S(1)}, f32[8,128]{1,0:T(8,128)S(1)}) custom-call(s32[2]{0:T(128)S(1)} %pad_add_fusion.place_ref, f32[8,32,1024]{2,1,0:T(8,128)} %constant_dynamic-update-slice_fusion.first_ref, f32[8,32,1024]{2,1,0:T(8,128)} %collective-permute-done.4.second_ref, f32[16,32,1024]{2,1,0:T(8,128)S(1)} %bitcast.21), custom_call_target="tpu_custom_call" | custom-call | flops 6000000000 | bytes 4000000 | tf_op jit(solution)/shard_map/pallas_call | solution.py:102
  84.4 0.0 collective-permute-done.6.second_ref
  84.4 4.8 %shard_map.43 = (f32[2,8,16,1152]{3,2,1,0:T(8,128)S(1)}, f32[8,128]{1,0:T(8,128)S(1)}) custom-call(s32[2]{0:T(128)S(1)} %pad_add_fusion.place_ref, f32[8,32,1024]{2,1,0:T(8,128)} %collective-permute-done.5.first_ref, f32[8,32,1024]{2,1,0:T(8,128)} %collective-permute-done.6.second_ref, f32[16,32,1024]{2,1,0:T(8,128)S(1)} %bitcast.22, ...), custom_call_target="tpu_custom_call" | custom-call | flops 2000000000 | bytes 4000000 | tf_op jit(solution)/shard_map/pallas_call | solution.py:102
  89.2 1.9 %collective-permute-start.7 = (f32[2,8,16,1152]{3,2,1,0:T(8,128)S(1)}, f32[2,8,16,1152]{3,2,1,0:T(8,128)S(1)}, u32[]{:S(2)}, u32[]{:S(2)}) collective-permute-start(f32[2,8,16,1152]{3,2,1,0:T(8,128)S(1)} %get-tuple-element.18), channel_id=1, source_target_pairs={{0,1},{1,0},{2,3},{3,2},{4,5},{5,4},{6,7},{7,6},{8,9},{9,8},{10,11... | collective-permute-start | bytes 3538952 | tf_op jit(solution)/shard_map/ppermute | solution.py:142
  91.2 2.8 %collective-permute-done.7 = f32[2,8,16,1152]{3,2,1,0:T(8,128)S(1)} collective-permute-done((f32[2,8,16,1152]{3,2,1,0:T(8,128)S(1)}, f32[2,8,16,1152]{3,2,1,0:T(8,128)S(1)}, u32[]{:S(2)}, u32[]{:S(2)}) %collective-permute-start.7) | collective-permute-done | bytes 1179680 | tf_op jit(solution)/shard_map/ppermute | solution.py:142
  94.0 0.1 fusion
  94.0 1.9 %collective-permute-start.8 = (f32[8,16,1024]{2,1,0:T(8,128)S(1)}, f32[8,16,1024]{2,1,0:T(8,128)}, u32[]{:S(2)}, u32[]{:S(2)}) collective-permute-start(f32[8,16,1024]{2,1,0:T(8,128)S(1)} %fusion), channel_id=1, source_target_pairs={{0,4},{1,29},{4,8},{5,1},{8,12},{9,5},{12,16},{13,9},{16,20},{17,1... | collective-permute-start | bytes 1572872 | tf_op jit(solution)/shard_map/ppermute | solution.py:142
  96.0 14.9 %all_to_all.20 = f32[32,1,128]{2,1,0:T(1,128)S(1)} all-to-all(f32[32,1,128]{2,1,0:T(1,128)S(1)} %broadcast_in_dim.7), channel_id=1, replica_groups=mesh['x'=4,'yh'=4,'zh'=4,'zl'=2,'yl'=2,'c'=2] {'x','zh','zl'}, dimensions={0} | all-to-all | bytes 32768 | tf_op jit(solution)/shard_map/all_to_all | solution.py:146
  111.0 0.0 collective-permute-done.8
  111.0 1.1 fusion.2
  112.1 21.6 %all_to_all.21 = f32[8,16,1152]{2,1,0:T(8,128)S(1)} all-to-all(f32[8,16,1152]{2,1,0:T(8,128)S(1)} %pad_maximum_fusion), channel_id=1, replica_groups=mesh['x'=4,'yh'=4,'zh'=4,'zl'=2,'yl'=2,'c'=2] {'yh','yl'}, dimensions={0} | all-to-all | bytes 1179648 | tf_op jit(solution)/shard_map/all_to_all | solution.py:146
  133.8 0.7 slice_reduce_fusion
  134.4 0.5 slice_reduce_fusion.1
  (27 shorter events, 0.3 us)
Async XLA Ops:
  2.4 26.8 %copy-start.1 = (f32[32,1024]{1,0:T(8,128)S(1)}, f32[32,1024]{1,0:T(8,128)}, u32[]{:S(2)}) copy-start(f32[32,1024]{1,0:T(8,128)} %get-tuple-element.12) | copy-start | bytes 393220
  2.4 26.7 %collective-permute-start.1 = (f32[32,1024]{1,0:T(8,128)}, f32[32,1024]{1,0:T(8,128)S(1)}, u32[]{:S(2)}, u32[]{:S(2)}) collective-permute-start(f32[32,1024]{1,0:T(8,128)} %get-tuple-element.12), channel_id=1, source_target_pairs={{0,8},{4,12},{8,16},{12,20},{16,24},{20,28},{24,0},{28,4},{1,9},{5... | collective-permute-start | bytes 393224 | tf_op jit(solution)/shard_map/ppermute | solution.py:142
  9.1 20.0 %collective-permute-start.2 = (f32[32,1024]{1,0:T(8,128)}, f32[32,1024]{1,0:T(8,128)S(1)}, u32[]{:S(2)}, u32[]{:S(2)}) collective-permute-start(f32[32,1024]{1,0:T(8,128)} %get-tuple-element.12), channel_id=1, source_target_pairs={{0,24},{4,28},{8,0},{12,4},{16,8},{20,12},{24,16},{28,20},{1,25},{... | collective-permute-start | bytes 393224 | tf_op jit(solution)/shard_map/ppermute | solution.py:142
  15.9 13.3 %collective-permute-start.3 = (f32[32,1024]{1,0:T(8,128)}, f32[32,1024]{1,0:T(8,128)S(1)}, u32[]{:S(2)}, u32[]{:S(2)}) collective-permute-start(f32[32,1024]{1,0:T(8,128)} %get-tuple-element.12), channel_id=1, source_target_pairs={{0,16},{4,20},{8,24},{12,28},{16,0},{20,4},{24,8},{28,12},{1,17},{... | collective-permute-start | bytes 393224 | tf_op jit(solution)/shard_map/ppermute | solution.py:142
  21.4 21.7 %all-to-all-start = ((f32[4,32,1024]{2,1,0:T(8,128)}), f32[4,32,1024]{2,1,0:T(8,128)S(1)}, u32[]{:S(2)}, u32[]{:S(2)}) async-start(f32[4,32,1024]{2,1,0:T(8,128)} %get-tuple-element.11), calls=%async_computation | async-start | bytes 1048576 | tf_op jit(solution)/shard_map/all_to_all | solution.py:146
  43.0 11.1 %collective-permute-start = (f32[4,32,1024]{2,1,0:T(8,128)S(1)}, f32[4,32,1024]{2,1,0:T(8,128)S(1)}, u32[]{:S(2)}, u32[]{:S(2)}) collective-permute-start(f32[4,32,1024]{2,1,0:T(8,128)S(1)} %all-to-all-done), channel_id=1, source_target_pairs={{0,98},{1,3},{2,0},{3,33},{32,2},{33,35},{34,32},{35,65},{64,34},{... | collective-permute-start | bytes 1572872 | tf_op jit(solution)/shard_map/ppermute | solution.py:142
  45.0 1.3 copy-start
  46.3 26.7 %all-to-all-start.1 = ((f32[4,4,32,1024]{3,2,1,0:T(8,128)}), f32[4,4,32,1024]{3,2,1,0:T(8,128)S(1)}, u32[]{:S(2)}, u32[]{:S(2)}) async-start(f32[4,4,32,1024]{3,2,1,0:T(8,128)} %bitcast.23), calls=%async_computation.1 | async-start | bytes 4194304 | tf_op jit(solution)/shard_map/all_to_all | solution.py:146
  55.0 17.2 %collective-permute-start.4 = (f32[8,32,1024]{2,1,0:T(8,128)}, f32[8,32,1024]{2,1,0:T(8,128)}, u32[]{:S(2)}, u32[]{:S(2)}) collective-permute-start(f32[8,32,1024]{2,1,0:T(8,128)} %constant_dynamic-update-slice_fusion.first_ref), channel_id=1, source_target_pairs={{0,28},{1,5},{4,0},{5,9},{8,4},{9,13},{12,8},{13,17},{16,12},{17,2... | collective-permute-start | bytes 3145736 | tf_op jit(solution)/shard_map/ppermute | solution.py:142
  58.1 26.3 %collective-permute-start.5 = (f32[8,32,1024]{2,1,0:T(8,128)}, f32[8,32,1024]{2,1,0:T(8,128)}, u32[]{:S(2)}, u32[]{:S(2)}) collective-permute-start(f32[8,32,1024]{2,1,0:T(8,128)} %constant_dynamic-update-slice_fusion.first_ref), channel_id=1, source_target_pairs={{0,1},{1,0},{2,3},{3,2},{4,5},{5,4},{6,7},{7,6},{8,9},{9,8},{10,11... | collective-permute-start | bytes 3145736 | tf_op jit(solution)/shard_map/ppermute | solution.py:142
  73.1 11.4 %collective-permute-start.6 = (f32[8,32,1024]{2,1,0:T(8,128)}, f32[8,32,1024]{2,1,0:T(8,128)}, u32[]{:S(2)}, u32[]{:S(2)}) collective-permute-start(f32[8,32,1024]{2,1,0:T(8,128)} %collective-permute-done.4.second_ref), channel_id=1, source_target_pairs={{0,1},{1,0},{2,3},{3,2},{4,5},{5,4},{6,7},{7,6},{8,9},{9,8},{10,11... | collective-permute-start | bytes 3145736 | tf_op jit(solution)/shard_map/ppermute | solution.py:142
  89.2 4.7 %collective-permute-start.7 = (f32[2,8,16,1152]{3,2,1,0:T(8,128)S(1)}, f32[2,8,16,1152]{3,2,1,0:T(8,128)S(1)}, u32[]{:S(2)}, u32[]{:S(2)}) collective-permute-start(f32[2,8,16,1152]{3,2,1,0:T(8,128)S(1)} %get-tuple-element.18), channel_id=1, source_target_pairs={{0,1},{1,0},{2,3},{3,2},{4,5},{5,4},{6,7},{7,6},{8,9},{9,8},{10,11... | collective-permute-start | bytes 3538952 | tf_op jit(solution)/shard_map/ppermute | solution.py:142
  94.0 16.9 %collective-permute-start.8 = (f32[8,16,1024]{2,1,0:T(8,128)S(1)}, f32[8,16,1024]{2,1,0:T(8,128)}, u32[]{:S(2)}, u32[]{:S(2)}) collective-permute-start(f32[8,16,1024]{2,1,0:T(8,128)S(1)} %fusion), channel_id=1, source_target_pairs={{0,4},{1,29},{4,8},{5,1},{8,12},{9,5},{12,16},{13,9},{16,20},{17,1... | collective-permute-start | bytes 1572872 | tf_op jit(solution)/shard_map/ppermute | solution.py:142
